TPU v7x, 32 devices: a whole 2x2x4 slice. The times are simulated.
32 devices in a mesh: dp: 8 (over z, x), tensor: 4 (over y, core).
Axes of the slice: x: 2, y: 2, z: 4, core: 2. Of those that a mesh axis runs over, the one named last changes fastest.
Arguments:
- features: bfloat16 [1792, 12288], P('dp', 'tensor'), may hold values from -6 to 6
- weights: bfloat16 [1536, 96, 128], P(None, 'tensor'), may hold values from -0.109375 to 0.109375
- block_cols: int32 [96, 12], P('tensor'), may hold values from 0 to 47, as said below
- cotangent: bfloat16 [1792, 6144], P('dp', 'tensor'), may hold values from -6 to 6
Outputs:
- input_grad: bfloat16 [1792, 12288], P('dp', 'tensor')
- weight_grad: float32 [1536, 96, 128], P('dp', 'tensor')
Inputs may be any that keep to these rules, and one draw needn't show every extreme that they name: Each row of block_cols names 12 distinct block columns; in each aligned group of four block rows the four rows name disjoint sets, so every block column is named by exactly one row of each group.
All inputs are finite; a program needn't handle non-finite values.
Results may differ from a plain program's by a relative error of at most 0.0049.
Values may be sent and summed in bfloat16 or wider, within the bound.
No kernel may reach another device: no remote copies, remote signals or barrier semaphores. Data moves between devices by JAX's collectives and lax.ppermute only.
A program may use at most 192 MiB of HBM per device.

v0:
```python
import jax
import jax.numpy as jnp
from jax import lax
from jax.sharding import PartitionSpec as P

gelu_coef = 0.7978845608


def gelu_slope(pre_act):
    inner_arg = gelu_coef * (pre_act + 0.044715 * pre_act * pre_act * pre_act)
    tanh_val = jnp.tanh(inner_arg)
    return 0.5 * (1.0 + tanh_val) + 0.5 * pre_act * (1.0 - tanh_val * tanh_val) * gelu_coef * (
        1.0 + 0.134145 * pre_act * pre_act
    )


def on_device(features, weights, block_cols, cotangent):
    tok_rows = features.shape[0]
    block_size = weights.shape[2]
    local_rows = weights.shape[1]
    slot_count = block_cols.shape[1]
    col_count = 4 * slot_count
    group_count = local_rows // 4
    blocks = weights.reshape(slot_count, block_size, local_rows, block_size)
    inputs = features.reshape(tok_rows, local_rows, block_size)
    products = jnp.einsum("tri,kirj->trkj", inputs, blocks, preferred_element_type=jnp.float32)
    grouped = products.reshape(tok_rows, group_count, col_count, block_size)
    group_cols = block_cols.reshape(group_count, col_count)
    col_order = jnp.argsort(group_cols, axis=1, stable=True)
    arranged = jnp.take_along_axis(grouped, col_order[None, :, :, None], axis=2)
    partial_sum = jnp.sum(arranged, axis=1).reshape(tok_rows, col_count * block_size)
    full_sum = lax.psum(partial_sum, "tensor")
    upstream = lax.all_gather(cotangent, "tensor", axis=1, tiled=True)
    slope = (upstream.astype(jnp.float32) * gelu_slope(full_sum)).astype(jnp.bfloat16)
    picked = jnp.take(slope.reshape(tok_rows, col_count, block_size), block_cols, axis=1)
    grad_rows = jnp.einsum("trkj,kirj->tri", picked, blocks, preferred_element_type=jnp.float32)
    input_grad = grad_rows.astype(jnp.bfloat16).reshape(tok_rows, local_rows * block_size)
    grad_scale = float(tok_rows * lax.axis_size("dp")) ** (-0.5)
    grad_term = (
        jnp.einsum("tri,trkj->kirj", inputs, picked, preferred_element_type=jnp.float32)
        * grad_scale
    )
    grad_term = grad_term.reshape(slot_count * block_size, local_rows, block_size)
    weight_grad = lax.psum_scatter(grad_term, "dp", scatter_dimension=0, tiled=True)
    return (input_grad, weight_grad)


def solution(mesh):
    return jax.shard_map(
        on_device,
        mesh=mesh,
        in_specs=(P("dp", "tensor"), P(None, "tensor", None), P("tensor", None), P("dp", "tensor")),
        out_specs=(P("dp", "tensor"), P("dp", "tensor", None)),
        check_vma=False,
    )
```

profile of v0, /device:TPU:0, one launch (start us, length us, event | category | flops | bytes accessed | tf_op | source)
XLA Modules:
  0.0 597.7 jit_solution(5528821752326964985)
XLA Ops:
  7.2 0.0 all-reduce.2.cloned.1.call-start
  7.2 0.8 copy.52
  8.0 0.1 reshape.53
  8.1 0.1 copy.53
  8.2 1.0 sort.17
  9.2 1.6 copy.75
  10.8 0.0 copy-start
  10.8 0.1 copy.57
  10.9 0.1 reshape.70
  11.0 0.1 copy.54
  11.0 17.8 %fusion.5 = f32[24,12,128,224]{2,3,1,0:T(8,128)} fusion(bf16[12,128,24,128]{3,2,1,0:T(8,128)(2,1)} %bitcast.55, bf16[224,24,128,1]{2,1,0,3:T(8,128)(2,1)S(1)} %bitcast.58), kind=kOutput, calls=%fused_computation.10 | convolution fusion | flops 2113929216 | bytes 43843584 | tf_op jit(solution)/shard_map/tri,kirj->trkj/dot_general | solution.py:26
  28.8 0.0 copy-done
  28.8 39.0 %gather_fusion.1 = f32[288,224,128]{2,1,0:T(8,128)} fusion(f32[224,6,48,128]{3,0,2,1:T(8,128)} %bitcast.51, s32[288]{0:T(512)S(1)} %reshape.70), kind=kCustom, calls=%fused_computation.1 | custom fusion | bytes 66062592 | tf_op jit(solution)/shard_map/jit(take_along_axis)/gather | solution.py:30
  67.9 13.3 %select_reduce_fusion = f32[48,224,128]{2,1,0:T(8,128)S(1)} fusion(f32[6,48,224,128]{3,2,1,0:T(8,128)} %bitcast.52, pred[6,48]{1,0:T(8,128)(4,1)S(1)} %copy.54), kind=kLoop, calls=%fused_computation.2 | loop fusion | flops 15138816 | bytes 38535456 | tf_op jit(solution)/shard_map/reduce_sum | solution.py:31
  81.1 3.1 copy_bitcast_fusion
  84.2 0.0 copy-start.1
  84.2 0.0 all-reduce.2.cloned.1.call-update
  84.3 0.0 all-gather.2.cloned.1.call-start
  84.3 0.7 all-gather.2.cloned.1.call-update
  85.0 0.2 reduce-scatter.2.cloned.1.call-start
  85.2 0.0 copy-done.1
  85.3 0.1 copy.59
  85.3 0.1 reshape.64
  85.5 0.1 copy.51
  85.6 108.4 %all-reduce.2.cloned.1.call-done = f32[224,6144]{1,0:T(8,128)} async-done(((f32[224,6144]{1,0:T(8,128)}), f32[224,6144]{1,0:T(8,128)}) %all-reduce.2.cloned.1.call-update) | async-done | bytes 5505040 | tf_op jit(solution)/shard_map/psum | solution.py:32
  194.0 28.1 %all-gather.2.cloned.1.call-done = bf16[224,6144]{1,0:T(8,128)(2,1)} async-done(((bf16[224,1536]{1,0:T(8,128)(2,1)}), bf16[224,6144]{1,0:T(8,128)(2,1)}) %all-gather.2.cloned.1.call-update) | async-done | bytes 2752528 | tf_op jit(solution)/shard_map/all_gather | solution.py:33
  222.0 5.9 copy_bitcast_fusion.1
  228.0 12.9 %gather_fusion = bf16[288,224,128]{2,1,0:T(8,128)(2,1)} fusion(bf16[224,48,128]{2,0,1:T(8,128)(2,1)S(1)} %copy_bitcast_fusion.1, s32[1024]{0:T(1024)S(1)} %pad_clamp_fusion), kind=kCustom, calls=%fused_computation | custom fusion | bytes 33031296 | tf_op jit(solution)/shard_map/jit(_take)/gather | solution.py:35
  240.9 11.9 %broadcast_multiply_fusion = f32[24,12,128,128]{2,3,1,0:T(8,128)} fusion(bf16[24,12,224,128]{3,2,1,0:T(8,128)(2,1)} %bitcast.53, pred[24,12]{1,0:T(8,128)(4,1)S(1)} %copy.51, bf16[224,24,128,1]{2,1,0,3:T(8,128)(2,1)} %bitcast.59), kind=kOutput, calls=%fused_computation.8 | convolution fusion | flops 2126905344 | bytes 36765984 | tf_op jit(solution)/shard_map/tri,trkj->kirj/dot_general | solution.py:40
  252.8 24.8 %copy.64 = f32[1536,24,128]{2,1,0:T(8,128)} copy(f32[1536,24,128]{2,0,1:T(8,128)} %bitcast.57) | data formatting | bytes 37748736 | tf_op jit(solution)/shard_map/reshape | solution.py:43
  277.6 0.0 reduce-scatter.2.cloned.1.call-update
  277.6 12.0 %fusion.23 = bf16[24,28,8,128]{3,2,1,0:T(8,128)(2,1)S(1)} fusion(bf16[12,128,24,128]{3,2,1,0:T(8,128)(2,1)} %bitcast.56, bf16[24,12,224,128]{3,2,1,0:T(8,128)(2,1)} %bitcast.54, pred[24,12]{1,0:T(8,128)(4,1)S(1)} %copy.51), kind=kOutput, calls=%fused_computation.27 | convolution fusion | flops 2122874880 | bytes 27328800 | tf_op jit(solution)/shard_map/trkj,kirj->tri/dot_general | solution.py:36
  289.6 1.5 copy.91
  291.0 300.1 %reduce-scatter.2.cloned.1.call-done = f32[192,24,128]{2,1,0:T(8,128)} async-done(((f32[1536,24,128]{2,1,0:T(8,128)}), f32[192,24,128]{2,1,0:T(8,128)}) %reduce-scatter.2.cloned.1.call-update) | async-done | bytes 2359312 | tf_op jit(solution)/shard_map/reduce_scatter | solution.py:44
  (6 shorter events, 0.0 us)
Async XLA Ops:
  7.2 186.8 %all-reduce.2.cloned.1.call-start = ((), (), s32[]{:S(2)}) async-start(), calls=%async_computation.2 | async-start | bytes 11010048 | tf_op jit(solution)/shard_map/psum | solution.py:32
  10.8 18.0 %copy-start = (bf16[28,8,24,128]{3,2,1,0:T(8,128)(2,1)}, bf16[28,8,24,128]{3,2,1,0:T(8,128)(2,1)S(1)}, u32[]{:S(2)}) copy-start(bf16[28,8,24,128]{3,2,1,0:T(8,128)(2,1)S(1)} %copy.75) | copy-start | bytes 4128772
  84.2 1.0 copy-start.1
  84.3 137.8 %all-gather.2.cloned.1.call-start = ((), (), s32[]{:S(2)}) async-start(), calls=%async_computation.1 | async-start | bytes 3440640 | tf_op jit(solution)/shard_map/all_gather | solution.py:33
  85.0 506.1 %reduce-scatter.2.cloned.1.call-start = ((), (), s32[]{:S(2)}) async-start(), calls=%async_computation.3 | async-start | bytes 21233664 | tf_op jit(solution)/shard_map/reduce_scatter | solution.py:44
Sparse Core Ops, SparseCore 0:
  84.4 109.5 all-reduce.1
  195.5 26.4 all-gather.1
  277.7 313.3 reduce-scatter.1
where the time goes:
time: 598 us
  waiting for transfers between devices  437 us (73%)
  local copies, waits for them, and re-layouts  84.3 us (14%)
  matrix products  41.7 us (7%)
  other arithmetic  20.2 us (3%)
  between operations  13.8 us (2%)
    reduce_scatter x1, waiting for transfers between devices, on_device(): lax.psum_scatter(grad_term, 'dp', scatter_dimension=0, tiled=True)  300 us
    psum x1, waiting for transfers between devices, on_device(): full_sum = lax.psum(partial_sum, 'tensor')  108 us
    gather x3, local copies, waits for them, and re-layouts, on_device(): arranged = jnp.take_along_axis(grouped, col_order[None, :, :, None], axis=2)  39.2 us
    all_gather x1, waiting for transfers between devices, on_device(): upstream = lax.all_gather(cotangent, 'tensor', axis=1, tiled=True)  28.1 us
    reshape x1, local copies, waits for them, and re-layouts, on_device(): grad_term.reshape(slot_count * block_size, local_rows, block_size)  24.8 us
    dot_general x1, matrix products, on_device(): jnp.einsum('tri,kirj->trkj', inputs, blocks, preferred_element_type=jnp.f...  17.8 us
    reduce_sum x1, other arithmetic, on_device(): jnp.sum(arranged, axis=1).reshape(tok_rows, col_count * block_size)  13.3 us
    gather x1, local copies, waits for them, and re-layouts, on_device(): jnp.take(slope.reshape(tok_rows, col_count, block_size), block_cols, axis=1)  12.9 us
  transfers between devices with their start and end apart: 3, of which 3 were waited for; matrix products, arithmetic and copies ran while one was open for 2% of the time, Pallas kernels for 0%

commit v1 on v0

v1 whole, which is shorter than its diff:
```python
import functools

import jax
import jax.numpy as jnp
from jax import lax
from jax.experimental import pallas as pl
from jax.experimental.pallas import tpu as pltpu
from jax.sharding import PartitionSpec as P

gelu_coef = 0.7978845608
f32 = jnp.float32
bf16 = jnp.bfloat16
FAR_LIMIT = 40
SHORT = pl.CostEstimate(flops=1000, bytes_accessed=1000, transcendentals=0)


def gelu_slope(pre_act):
    square = pre_act * pre_act
    twice = pre_act * (2.0 * gelu_coef + (2.0 * gelu_coef * 0.044715) * square)
    s = 1.0 / (1.0 + jnp.exp(-twice))
    inner = pre_act * (2.0 * gelu_coef + (2.0 * gelu_coef * 0.134145) * square)
    return s + s * (1.0 - s) * inner


def swap(value, axis, bit):
    count = lax.axis_size(axis)
    return lax.ppermute(value, axis, [(i, i ^ bit) for i in range(count)])


def whole():
    return pl.BlockSpec(memory_space=pltpu.VMEM)


def anywhere():
    return pl.BlockSpec(memory_space=pl.ANY)


def column_sums(x_ref, w_ref, entry_ref, out_ref, owner, slots, groups, first=0):
    col_count, rows = 4 * slots, 4 * groups
    for cc in range(out_ref.shape[0]):
        col = owner * slots + first + cc
        left, right = [], []
        for g in range(groups):
            e = entry_ref[g * col_count + col]
            lane = pl.multiple_of(lax.rem(e, rows) * 128, 128)
            left.append(x_ref[:, pl.ds(lane, 128)])
            right.append(w_ref[e])
        total = jnp.dot(
            jnp.concatenate(left, axis=1), jnp.concatenate(right, axis=0), preferred_element_type=f32
        )
        out_ref[cc] = total.astype(out_ref.dtype)


def turn_weights(slots, rows, w_ref, wt_ref, raw, wide, sems):
    few = 8 * rows

    def fetch(j, h):
        return pltpu.make_async_copy(
            w_ref.at[pl.ds(j * 128 + h * 64, 64)], raw.at[j, pl.ds(h * 64, 64)], sems.at[j, h]
        )

    for j in range(slots):
        for h in range(2):
            fetch(j, h).start(priority=h)
    to = lax.broadcasted_iota(jnp.int32, (few, few), 0)
    source = lax.broadcasted_iota(jnp.int32, (few, few), 1)
    turn = jnp.where(source == (to % 8) * rows + to // 8, 1.0, 0.0).astype(bf16)

    @pl.loop(0, slots // 2)
    def _(n):
        k, j = 2 * n, 2 * n + 1
        for h in range(2):
            fetch(k, h).wait()
            fetch(j, h).wait()
        wide[...] = raw[k].astype(f32).reshape(128 * rows, 128)
        value = raw[j].astype(f32).reshape(128 * rows, 128).astype(bf16)
        for i in range(8):
            two = value[2 * i * few : 2 * (i + 1) * few]
            both = jnp.concatenate([two[:few], two[few:]], axis=1)
            done = jnp.dot(turn, both, preferred_element_type=f32)
            for r in range(rows):
                here = done[r * 8 : (r + 1) * 8]
                block = jnp.concatenate([here[:, :128], here[:, 128:]], axis=0).astype(bf16)
                wt_ref[j * rows + r, pl.ds(16 * i, 16), :] = block
            for r in range(i * rows // 8, (i + 1) * rows // 8):
                wt_ref[k * rows + r] = wide[pl.ds(r, 128, stride=rows), :].astype(bf16)


def run_turn_weights(weights, slots):
    rows = weights.shape[1]
    return pl.pallas_call(
        functools.partial(turn_weights, slots, rows),
        in_specs=[anywhere()],
        out_specs=whole(),
        scratch_shapes=[
            pltpu.VMEM((slots, 128, rows, 128), bf16),
            pltpu.VMEM((128 * rows, 128), f32),
            pltpu.SemaphoreType.DMA((slots, 2)),
        ],
        out_shape=jax.ShapeDtypeStruct((rows * slots, 128, 128), bf16),
        compiler_params=pltpu.CompilerParams(vmem_limit_bytes=FAR_LIMIT * 2**20),
        cost_estimate=SHORT,
        name="turn_weights",
    )(weights)


def forward_first(slots, groups, cols_ref, w_ref, x_ref, send_ref, entry_ref):
    rows = 4 * groups
    for k in range(slots):
        for r in range(rows):
            entry_ref[(r // 4) * 4 * slots + cols_ref[k, r]] = k * rows + r
    column_sums(x_ref, w_ref, entry_ref, send_ref, lax.axis_index("tensor") ^ 3, slots, groups)


def forward_more(slots, groups, wanted, entry_ref, w_ref, x_ref, *refs):
    outs = refs[-len(wanted) :]
    for (flip, first), out_ref in zip(wanted, outs):
        owner = lax.axis_index("tensor") ^ flip
        column_sums(x_ref, w_ref, entry_ref, out_ref, owner, slots, groups, first)


def run_forward_first(features, turned, cols):
    tokens, _ = features.shape
    slots, rows = cols.shape
    smem = pl.BlockSpec(memory_space=pltpu.SMEM)
    return pl.pallas_call(
        functools.partial(forward_first, slots, rows // 4),
        in_specs=[smem, whole(), whole()],
        out_specs=[whole(), smem],
        out_shape=[
            jax.ShapeDtypeStruct((slots, tokens, 128), bf16),
            jax.ShapeDtypeStruct((rows * slots,), jnp.int32),
        ],
        compiler_params=pltpu.CompilerParams(vmem_limit_bytes=24 * 2**20),
        cost_estimate=SHORT,
        name="forward_first",
    )(cols, turned, features)


def run_forward_more(features, turned, entry, slots, wanted, after=()):
    tokens, width = features.shape
    shapes = [jax.ShapeDtypeStruct((count, tokens, 128), kind) for _, _, count, kind in wanted]
    return pl.pallas_call(
        functools.partial(forward_more, slots, width // 512, [w[:2] for w in wanted]),
        in_specs=[pl.BlockSpec(memory_space=pltpu.SMEM), whole(), whole()] + [anywhere()] * len(after),
        out_specs=[whole()] * len(shapes),
        out_shape=shapes,
        compiler_params=pltpu.CompilerParams(vmem_limit_bytes=24 * 2**20),
        cost_estimate=SHORT,
        name="forward_more",
    )(entry, turned, features, *after)


def own_slope(keep_ref, near_lo_ref, near_hi_ref, across_ref, cot_ref, out_ref, lo_ref, hi_ref):
    n = keep_ref.shape[0]
    for j in range(n):
        near = near_lo_ref[j] if j < n // 2 else near_hi_ref[j - n // 2]
        pre = keep_ref[j] + near.astype(f32) + across_ref[j].astype(f32)
        upstream = cot_ref[:, j * 128 : (j + 1) * 128].astype(f32)
        value = (upstream * gelu_slope(pre)).astype(bf16)
        out_ref[j] = value
        if j < n // 2:
            lo_ref[j] = value
        else:
            hi_ref[j - n // 2] = value


def run_own_slope(keep, near, across, cotangent):
    slots, tokens, _ = keep.shape
    shapes = [(slots, tokens, 128), (slots // 2, tokens, 128), (slots - slots // 2, tokens, 128)]
    return pl.pallas_call(
        own_slope,
        in_specs=[whole()] * 5,
        out_specs=[whole()] * 3,
        out_shape=[jax.ShapeDtypeStruct(s, bf16) for s in shapes],
        compiler_params=pltpu.CompilerParams(vmem_limit_bytes=12 * 2**20),
        cost_estimate=SHORT,
        name="own_slope",
    )(keep, *near, across, cotangent)


def slot_of(col, s, slots):
    owner = col // slots
    return (owner ^ s) * slots + (col - owner * slots)


def load_pieces(pieces, held, sems):
    copies = []
    at = 0
    for i, ref in enumerate(pieces):
        n = ref.shape[0]
        copies.append(pltpu.make_async_copy(ref, held.at[pl.ds(at, n)], sems.at[i]))
        at += n
    for c in copies:
        c.start()
    for c in copies:
        c.wait()


def odd_z():
    return lax.rem(lax.axis_index("dp") // 2, 2)


def turn_features(n, mine, *refs):
    parts, out_ref = refs[:n], refs[-1]
    count = out_ref.shape[0]
    first = odd_z() * (count * 128) if mine else 0
    for r in range(count):
        lanes = pl.ds(pl.multiple_of(first + r * 128, 128), 128)
        row = jnp.concatenate([part[:, lanes].astype(f32) for part in parts], axis=0)
        out_ref[r] = jnp.transpose(row).astype(bf16)


def run_turn_features(parts, count, mine, after=()):
    tokens = sum(p.shape[0] for p in parts)
    return pl.pallas_call(
        functools.partial(turn_features, len(parts), mine),
        in_specs=[whole()] * len(parts) + [anywhere()] * len(after),
        out_specs=whole(),
        out_shape=jax.ShapeDtypeStruct((count, 128, tokens), bf16),
        compiler_params=pltpu.CompilerParams(vmem_limit_bytes=12 * 2**20),
        cost_estimate=SHORT,
        name="turn_features",
    )(*parts, *after)


def partner_features(x_ref, *refs):
    out_ref, sem = refs[-2:]
    width = out_ref.shape[1]
    lanes = pl.ds(pl.multiple_of((1 - odd_z()) * width, 128), width)
    copy = pltpu.make_async_copy(x_ref.at[:, lanes], out_ref, sem)
    copy.start()
    copy.wait()


def run_partner_features(features, after):
    tokens, width = features.shape
    return pl.pallas_call(
        partner_features,
        in_specs=[whole(), anywhere()],
        out_specs=whole(),
        out_shape=jax.ShapeDtypeStruct((tokens, width // 2), bf16),
        scratch_shapes=[pltpu.SemaphoreType.DMA],
        compiler_params=pltpu.CompilerParams(vmem_limit_bytes=8 * 2**20),
        cost_estimate=SHORT,
        name="partner_features",
    )(features, after)


def put_grads(low, r, xt_row, own, xt2_row, other, sends, keeps):
    total = jnp.dot(xt_row, own, preferred_element_type=f32)
    total += jnp.dot(xt2_row, other, preferred_element_type=f32)
    for i, (send, keep) in enumerate(zip(sends, keeps)):
        b0, b1, b2 = [total[:, (3 * i + kk) * 128 : (3 * i + kk + 1) * 128] for kk in range(3)]
        v0 = jnp.concatenate([b0, b1[:64]], axis=0)
        v1 = jnp.concatenate([b1[64:], b2], axis=0)
        send[r] = jnp.where(low, v1, v0).astype(bf16)
        keep[r] = jnp.where(low, v0, v1)


def block_grads(slots, flips, lo, hi, cols_ref, xt_ref, xt2_ref, held, sends, keeps):
    if len(sends) < len(flips):
        sends = [sends[0].at[i] for i in range(len(flips))]
    low = lax.rem(lax.axis_index("dp"), 2) == 0
    for r in range(lo, hi):
        at = columns_of(slots, flips, r, xt_ref.shape[0], cols_ref)
        own = jnp.concatenate([held[a] for a in at], axis=1)
        other = jnp.concatenate([held[4 * slots + a] for a in at], axis=1)
        put_grads(low, r - lo, xt_ref[r], own, xt2_ref[r], other, sends, keeps)


def columns_of(slots, flips, r, half_rows, cols_ref):
    s, z = lax.axis_index("tensor"), lax.axis_index("dp") // 2
    row = odd_z() * half_rows + r
    return [slot_of(cols_ref[(z ^ flip) * 3 + kk, row], s, slots) for flip in flips for kk in range(3)]


def few_grads(slots, flips, lo, hi, n_pieces, cols_ref, xt_ref, xt2_ref, *refs):
    pieces, (send, *keeps), (tiles, sems) = refs[:n_pieces], refs[n_pieces:-2], refs[-2:]
    per_row = 3 * len(flips)
    half = 4 * slots
    for r in range(lo, hi):
        for i, at in enumerate(columns_of(slots, flips, r, xt_ref.shape[0], cols_ref)):
            n = 2 * ((r - lo) * per_row + i)
            start = 0
            for ref in pieces:
                count = ref.shape[0]
                which = n if start < half else n + 1
                here = at - start % half

                @pl.when((here >= 0) & (here < count))
                def _(ref=ref, which=which, here=here):
                    pltpu.make_async_copy(ref.at[here], tiles.at[which], sems.at[which]).start()

                start += count
    for n in range(tiles.shape[0]):
        pltpu.make_async_copy(pieces[0].at[0], tiles.at[n], sems.at[n]).wait()
    low = lax.rem(lax.axis_index("dp"), 2) == 0
    for r in range(lo, hi):
        at = [2 * ((r - lo) * per_row + i) for i in range(per_row)]
        own = jnp.concatenate([tiles[n] for n in at], axis=1)
        other = jnp.concatenate([tiles[n + 1] for n in at], axis=1)
        put_grads(low, r - lo, xt_ref[r], own, xt2_ref[r], other, [send.at[i] for i in range(len(flips))], keeps)


def first_grads(slots, flips, lo, hi, n_pieces, cols_ref, xt_ref, xt2_ref, *refs):
    pieces, outs, (held, sems) = refs[:n_pieces], refs[n_pieces + 1 : -2], refs[-2:]
    load_pieces(pieces, held, sems)
    n = len(outs) - len(flips)
    block_grads(slots, flips, lo, hi, cols_ref, xt_ref, xt2_ref, held, outs[:n], outs[n:])


def more_grads(slots, flips, lo, hi, n_after, cols_ref, xt_ref, xt2_ref, held, *refs):
    outs = refs[n_after:]
    n = len(outs) - len(flips)
    block_grads(slots, flips, lo, hi, cols_ref, xt_ref, xt2_ref, held, outs[:n], outs[n:])


def grad_shapes(flips, lo, hi, joint):
    part = (hi - lo, 192, 128)
    sends = [(len(flips), *part)] if joint else [part] * len(flips)
    return [jax.ShapeDtypeStruct(s, bf16) for s in sends] + [jax.ShapeDtypeStruct(part, f32)] * len(flips)


def run_few_grads(cols, xt, xt2, pieces, flips, lo, hi):
    slots, n = cols.shape[0], len(pieces)
    tokens = pieces[0].shape[1]
    shapes = grad_shapes(flips, lo, hi, True)
    count = (hi - lo) * 6 * len(flips)
    return pl.pallas_call(
        functools.partial(few_grads, slots, flips, lo, hi, n),
        in_specs=[pl.BlockSpec(memory_space=pltpu.SMEM), whole(), whole()] + [anywhere()] * n,
        out_specs=[whole()] * len(shapes),
        out_shape=shapes,
        scratch_shapes=[pltpu.VMEM((count, tokens, 128), bf16), pltpu.SemaphoreType.DMA((count,))],
        compiler_params=pltpu.CompilerParams(vmem_limit_bytes=12 * 2**20),
        cost_estimate=SHORT,
        name="few_grads",
    )(cols, xt, xt2, *pieces)


def run_first_grads(cols, xt, xt2, pieces, flips, lo, hi, after):
    slots, n = cols.shape[0], len(pieces)
    tokens = pieces[0].shape[1]
    shapes = grad_shapes(flips, lo, hi, True) + [jax.ShapeDtypeStruct((8 * slots, tokens, 128), bf16)]
    return pl.pallas_call(
        functools.partial(first_grads, slots, flips, lo, hi, n),
        in_specs=[pl.BlockSpec(memory_space=pltpu.SMEM), whole(), whole()] + [anywhere()] * (n + 1),
        out_specs=[whole()] * len(shapes),
        out_shape=shapes,
        scratch_shapes=[pltpu.SemaphoreType.DMA((n,))],
        compiler_params=pltpu.CompilerParams(vmem_limit_bytes=20 * 2**20),
        cost_estimate=SHORT,
        name="first_grads",
    )(cols, xt, xt2, *pieces, after)


def run_more_grads(cols, xt, xt2, held, flips, lo, hi, joint, after=()):
    slots = cols.shape[0]
    shapes = grad_shapes(flips, lo, hi, joint)
    return pl.pallas_call(
        functools.partial(more_grads, slots, flips, lo, hi, len(after)),
        in_specs=[pl.BlockSpec(memory_space=pltpu.SMEM)] + [whole()] * 3 + [anywhere()] * len(after),
        out_specs=[whole()] * len(shapes),
        out_shape=shapes,
        compiler_params=pltpu.CompilerParams(vmem_limit_bytes=20 * 2**20),
        cost_estimate=SHORT,
        name="more_grads",
    )(cols, xt, xt2, held, *after)


def input_grads(slots, n_pieces, cols_ref, w_ref, *refs):
    pieces, out_ref, held, sems = refs[:n_pieces], refs[-3], refs[-2], refs[-1]
    r = pl.program_id(0)

    @pl.when(r == 0)
    def _():
        load_pieces(pieces, held, sems)

    s = lax.axis_index("tensor")
    left = jnp.concatenate([held[slot_of(cols_ref[k, r], s, slots)] for k in range(slots)], axis=1)
    right = jnp.concatenate([w_ref[k, 0] for k in range(slots)], axis=1)
    total = lax.dot_general(left, right, (((1,), (1,)), ((), ())), preferred_element_type=f32)
    out_ref[...] = total.astype(bf16)


def run_input_grads(cols, turned, pieces, after=()):
    slots, rows = cols.shape
    tokens = pieces[0].shape[1]
    return pl.pallas_call(
        functools.partial(input_grads, slots, len(pieces)),
        grid_spec=pltpu.PrefetchScalarGridSpec(
            num_scalar_prefetch=1,
            grid=(rows,),
            in_specs=[pl.BlockSpec((slots, 1, 128, 128), lambda r, c: (0, r, 0, 0))]
            + [anywhere()] * (len(pieces) + len(after)),
            out_specs=pl.BlockSpec((tokens, 128), lambda r, c: (0, r)),
            scratch_shapes=[
                pltpu.VMEM((4 * slots, tokens, 128), bf16),
                pltpu.SemaphoreType.DMA((len(pieces),)),
            ],
        ),
        out_shape=jax.ShapeDtypeStruct((tokens, rows * 128), bf16),
        compiler_params=pltpu.CompilerParams(vmem_limit_bytes=16 * 2**20),
        cost_estimate=SHORT,
        name="input_grads",
    )(cols, turned.reshape(slots, rows, 128, 128), *pieces, *after)


def by_rows(mine, other):
    even = odd_z() == 0
    return jnp.where(even, mine, other), jnp.where(even, other, mine)


def main_sum(scale, cuts, keep_ref, recv_ref, near_ref, *refs):
    n = len(cuts) - 2
    mine_refs, other_refs, out_ref = refs[:n], refs[n:-1], refs[-1]

    def half(base, fars):
        parts = [base[: cuts[1]]]
        for i, far in enumerate(fars):
            parts.append(base[cuts[i + 1] : cuts[i + 2]] + far[...].astype(f32))
        return jnp.concatenate(parts, axis=0) * scale

    mine = half(keep_ref[...] + recv_ref[...].astype(f32), mine_refs)
    other = half(near_ref[...].astype(f32), other_refs)
    out_ref[...] = jnp.swapaxes(jnp.concatenate(by_rows(mine, other), axis=0), 0, 1)


def run_main_sum(scale, cuts, keep, recv, near, fars_mine, fars_other):
    rows = 2 * keep.shape[0]
    args = [keep, recv, near, *fars_mine, *fars_other]
    return pl.pallas_call(
        functools.partial(main_sum, scale, cuts),
        grid=(6,),
        in_specs=[pl.BlockSpec((a.shape[0], 32, 128), lambda i: (0, i, 0)) for a in args],
        out_specs=pl.BlockSpec((32, rows, 128), lambda i: (i, 0, 0)),
        out_shape=jax.ShapeDtypeStruct((192, rows, 128), f32),
        compiler_params=pltpu.CompilerParams(vmem_limit_bytes=12 * 2**20),
        cost_estimate=SHORT,
        name="main_sum",
    )(*args)


def last_sum(scale, base_ref, mine_ref, other_ref, out_ref):
    n, half = mine_ref.shape[0], base_ref.shape[1] // 2
    fars = by_rows(mine_ref[...].astype(f32), other_ref[...].astype(f32))
    for i, far in enumerate(fars):
        lo = i * half
        out_ref[:, lo : lo + n] = base_ref[:, lo : lo + n] + jnp.swapaxes(far * scale, 0, 1)
        out_ref[:, lo + n : lo + half] = base_ref[:, lo + n : lo + half]


def run_last_sum(scale, base, mine, other):
    n, rows = mine.shape[0], base.shape[1]
    tile = pl.BlockSpec((48, rows, 128), lambda i: (i, 0, 0))
    far = pl.BlockSpec((n, 48, 128), lambda i: (0, i, 0))
    return pl.pallas_call(
        functools.partial(last_sum, scale),
        grid=(4,),
        in_specs=[tile, far, far],
        out_specs=tile,
        out_shape=jax.ShapeDtypeStruct(base.shape, f32),
        compiler_params=pltpu.CompilerParams(vmem_limit_bytes=8 * 2**20),
        cost_estimate=SHORT,
        name="last_sum",
    )(base, mine, other)


def on_device(features, weights, block_cols, cotangent):
    tokens = features.shape[0]
    rows, slots = block_cols.shape
    cols = block_cols.T
    n_dp = lax.axis_size("dp")
    scale = float(tokens * n_dp) ** (-0.5)
    paired = n_dp == 8
    after = lax.optimization_barrier

    turned = run_turn_weights(weights, slots)
    far_send, entry = run_forward_first(features, turned, cols)
    far_recv = swap(far_send, "tensor", 1)
    (far_keep,) = run_forward_more(features, turned, entry, slots, [(2, 0, slots, f32)])
    far_sum = (far_keep + far_recv.astype(f32)).astype(bf16)
    across = swap(far_sum, "tensor", 2)
    features, far_sum = after((features, far_sum))
    cut = slots // 2
    wanted = [(1, 0, cut, bf16), (1, cut, slots - cut, bf16), (0, 0, slots, f32)]
    near_lo, near_hi, near_keep = run_forward_more(features, turned, entry, slots, wanted, [far_sum])
    near_recv = [swap(near_lo, "tensor", 1), swap(near_hi, "tensor", 1)]
    if paired:
        features2 = swap(run_partner_features(features, far_sum), "dp", 2)
    s0, s0a, s0b = run_own_slope(near_keep, near_recv, across, cotangent)

    s2b = swap(s0b, "tensor", 2)
    s2a = swap(s0a, "tensor", 2)
    s1 = swap(s0, "tensor", 1)
    s3b = swap(s2b, "tensor", 1)

    if not paired:
        s3a = swap(s2a, "tensor", 1)
        own = [s0, s1, s2a, s2b, s3a, s3b]
        held = jnp.concatenate(own, axis=0)
        at = slot_of(block_cols, lax.axis_index("tensor"), slots)
        picked = jnp.take(held, at, axis=0)
        x = features.reshape(tokens, rows, 128)
        grad = jnp.einsum("tri,rktj->kirj", x, picked, preferred_element_type=f32) * scale
        grad = grad.reshape(slots * 128, rows, 128)
        weight_grad = lax.psum_scatter(grad, "dp", scatter_dimension=0, tiled=True)
        return run_input_grads(cols, turned, own), weight_grad

    xt = run_turn_features([features], rows // 2, True, [near_lo])

    z0a = swap(s0a, "dp", 2)
    s0b, features2 = after((s0b, features2))
    z0b = swap(s0b, "dp", 2)
    xt2 = run_turn_features([features2], rows // 2, False, [s0])
    z0a, xt, xt2 = after((z0a, xt, xt2))
    z2a = swap(z0a, "tensor", 2)
    z2b = swap(s2b, "dp", 2)
    z1a = swap(z0a, "tensor", 1)
    s2a, z0b, z2a, z2b = after((s2a, z0b, z2a, z2b))
    s3a = swap(s2a, "tensor", 1)
    z1b = swap(z0b, "tensor", 1)
    z3a = swap(z2a, "tensor", 1)
    z3b = swap(z2b, "tensor", 1)
    own = [s0, s1, s2a, s2b, s3a, s3b]
    pieces = own + [z0a, z0b, z1a, z1b, z2a, z2b, z3a, z3b]

    half = rows // 2
    cuts = [0, half * 5 // 12, half * 10 // 12, half]
    far = (2, 3)

    def add(keep, recv):
        return (keep + recv.astype(f32)).astype(bf16)

    send_a, *keeps_a = run_few_grads(cols, xt, xt2, pieces, far, cuts[2], cuts[3])
    recv_a = swap(send_a, "dp", 1)
    send_b, keep_b2, keep_b3, held = run_first_grads(cols, xt, xt2, pieces, far, cuts[1], cuts[2], send_a)
    recv_b = swap(send_b, "dp", 1)
    totals_a = [add(*parts) for parts in zip(keeps_a, recv_a)]
    far_a2, far_a3 = swap(totals_a[0], "dp", 4), swap(totals_a[1], "dp", 6)
    send_c, keep_c2, keep_c3 = run_more_grads(cols, xt, xt2, held, far, cuts[0], cuts[1], True, totals_a)
    recv_c = swap(send_c, "dp", 1)
    send1, send0, keep1, keep0 = run_more_grads(cols, xt, xt2, held, (1, 0), 0, half, False, totals_a)
    recv1 = swap(send1, "dp", 1)
    keep_b2, far_a2 = after((keep_b2, far_a2))
    total_b2 = add(keep_b2, recv_b[0])
    far_b2 = swap(total_b2, "dp", 4)
    total_b2, send0 = after((total_b2, send0))
    recv0 = swap(send0, "dp", 1)
    keep_b3, far_a3, total_b2 = after((keep_b3, far_a3, total_b2))
    total_b3 = add(keep_b3, recv_b[1])
    far_b3 = swap(total_b3, "dp", 6)
    keep_c2, far_b2, total_b3 = after((keep_c2, far_b2, total_b3))
    total_c2 = add(keep_c2, recv_c[0])
    far_c2 = swap(total_c2, "dp", 4)
    keep_c3, far_b3, total_c2 = after((keep_c3, far_b3, total_c2))
    total_c3 = add(keep_c3, recv_c[1])
    far_c3 = swap(total_c3, "dp", 6)
    far_c2 = far_c2.astype(f32)
    total1 = add(keep1, recv1)
    near = swap(total1, "dp", 2)

    input_grad = run_input_grads(cols, turned, own, [total_b2, total_b3, total_c2, total_c3, total1])
    base = run_main_sum(scale, cuts, keep0, recv0, near, [far_b2, far_a2], [far_b3, far_a3])
    return input_grad, run_last_sum(scale, base, far_c2, far_c3)


def solution(mesh):
    return jax.shard_map(
        on_device,
        mesh=mesh,
        in_specs=(P("dp", "tensor"), P(None, "tensor", None), P("tensor", None), P("dp", "tensor")),
        out_specs=(P("dp", "tensor"), P("dp", "tensor", None)),
        check_vma=False,
    )
```

time: 598 us -> 132 us (0.22)
  waiting for transfers between devices: 437 us -> 56.5 us
  local copies, waits for them, and re-layouts: 84.3 us -> 0.01 us
  Pallas kernels: 0 us -> 45.7 us
  matrix products: 41.7 us -> 0 us
  starting transfers between devices: 0.3 us -> 28.3 us
  other arithmetic: 20.2 us -> 0.68 us
  between operations: 13.8 us -> 0.87 us
    reduce_scatter x1 -> x0, waiting for transfers between devices: 300 us -> none  [on_device(): lax.psum_scatter(grad_term, 'dp', scatter_dimension=0, tiled=True)]
    psum x1 -> x0, waiting for transfers between devices: 108 us -> none  [on_device(): full_sum = lax.psum(partial_sum, 'tensor')]
    ppermute x0 -> x30, waiting for transfers between devices: none -> 56.5 us  [swap(): return lax.ppermute(value, axis, [(i, i ^ bit) for i in range(count)])]
    gather x4 -> x0, local copies, waits for them, and re-layouts: 52.1 us -> none  [the longest x3 39.2 us: on_device(): arranged = jnp.take_along_axis(grouped, col_order[None, :, :, None], axis=2)]
    pallas_call x0 -> x15, Pallas kernels: none -> 45.7 us  [the longest x1 14.3 us: run_input_grads(): pl.pallas_call(functools.partial(input_grads, slots, len(pieces)), grid_s...]
    dot_general x3 -> x0, matrix products: 41.7 us -> none  [the longest x1 17.8 us: on_device(): jnp.einsum('tri,kirj->trkj', inputs, blocks, preferred_element_type=jnp.f...]
    reshape x5 -> x0, local copies, waits for them, and re-layouts: 29.5 us -> none  [the longest x1 24.8 us: on_device(): grad_term.reshape(slot_count * block_size, local_rows, block_size)]
    ppermute x0 -> x30, starting transfers between devices: none -> 28.3 us  [swap(): return lax.ppermute(value, axis, [(i, i ^ bit) for i in range(count)])]
  transfers between devices with their start and end apart: 3 -> 30, of which waited for: 3 -> 17; matrix products, arithmetic and copies ran while one was open for 2% -> 0% of each run, Pallas kernels for 0% -> 22%
where the time goes in v1:
time: 132 us
  waiting for transfers between devices  56.5 us (43%)
  Pallas kernels  45.7 us (35%)
  starting transfers between devices  28.3 us (21%)
    ppermute x30, waiting for transfers between devices, swap(): return lax.ppermute(value, axis, [(i, i ^ bit) for i in range(count)])  56.5 us
    ppermute x30, starting transfers between devices, swap(): return lax.ppermute(value, axis, [(i, i ^ bit) for i in range(count)])  28.3 us
    pallas_call x1, Pallas kernels, run_input_grads(): pl.pallas_call(functools.partial(input_grads, slots, len(pieces)), grid_s...  14.3 us
    pallas_call x1, Pallas kernels, run_turn_weights(): pl.pallas_call(functools.partial(turn_weights, slots, rows), in_specs=[an...  7.11 us
    pallas_call x2, Pallas kernels, run_forward_more(): pl.pallas_call(functools.partial(forward_more, slots, width // 512, [w[:2...  4.97 us
    pallas_call x1, Pallas kernels, run_few_grads(): pl.pallas_call(functools.partial(few_grads, slots, flips, lo, hi, n), in_...  4.42 us
    pallas_call x1, Pallas kernels, run_first_grads(): pl.pallas_call(functools.partial(first_grads, slots, flips, lo, hi, n), i...  3.64 us
    pallas_call x2, Pallas kernels, run_more_grads(): pl.pallas_call(functools.partial(more_grads, slots, flips, lo, hi, len(af...  3.63 us
  transfers between devices with their start and end apart: 30, of which 17 were waited for; matrix products, arithmetic and copies ran while one was open for 0% of the time, Pallas kernels for 22%

profile of v1, /device:TPU:0, one launch (start us, length us, event | category | flops | bytes accessed | tf_op | source)
XLA Modules:
  0.0 132.1 jit_solution(6737521601014473084)
XLA Ops:
  0.6 7.1 %turn_weights.1.w_ref = bf16[288,128,128]{2,1,0:T(8,128)(2,1)S(1)} custom-call(bf16[1536,24,128]{2,1,0:T(8,128)(2,1)} %w_ref.1), custom_call_target="tpu_custom_call" | custom-call | flops 1000 | bytes 1000 | tf_op jit(solution)/shard_map/turn_weights/pallas_call | solution.py:91
  7.8 2.8 %forward_first.1 = (bf16[12,224,128]{2,1,0:T(8,128)(2,1)S(1)}, s32[288]{0:T(512)S(1)}) custom-call(s32[12,24]{1,0:T(8,128)S(1)} %bitcast.33, bf16[288,128,128]{2,1,0:T(8,128)(2,1)S(1)} %turn_weights.1.w_ref, bf16[224,3072]{1,0:T(8,128)(2,1)S(1)} %copy-done), custom_call_target="tpu_custom_call" | custom-call | flops 1000 | bytes 1000 | tf_op jit(solution)/shard_map/forward_first/pallas_call | solution.py:126
  10.6 0.5 collective-permute-start
  11.1 1.9 %forward_more.2 = f32[12,224,128]{2,1,0:T(8,128)S(1)} custom-call(s32[288]{0:T(512)S(1)} %get-tuple-element.48.entry_ref, bf16[288,128,128]{2,1,0:T(8,128)(2,1)S(1)} %turn_weights.1.w_ref, bf16[224,3072]{1,0:T(8,128)(2,1)S(1)} %copy-done), custom_call_target="tpu_custom_call" | custom-call | flops 1000 | bytes 1000 | tf_op jit(solution)/shard_map/forward_more/pallas_call | solution.py:143
  13.0 0.2 add_convert_fusion.refs_0_
  13.2 2.8 %collective-permute-start.3 = (bf16[12,224,128]{2,1,0:T(8,128)(2,1)S(1)}, bf16[12,224,128]{2,1,0:T(8,128)(2,1)S(1)}, u32[]{:S(2)}, u32[]{:S(2)}) collective-permute-start(bf16[12,224,128]{2,1,0:T(8,128)(2,1)S(1)} %add_convert_fusion.refs_0_), channel_id=1, source_target_pairs={{0,2},{1,3},{2,0},{3,1},{4,6},{5,7},{6,4},{7,5},{8,10},{9,11},{10,... | collective-permute-start | bytes 2064392 | tf_op jit(solution)/shard_map/ppermute | solution.py:27
  16.0 0.1 partner_features.1
  16.0 0.0 copy-start.1
  16.0 1.7 %collective-permute-start.6 = (bf16[224,1536]{1,0:T(8,128)(2,1)S(1)}, bf16[224,1536]{1,0:T(8,128)(2,1)S(1)}, u32[]{:S(2)}, u32[]{:S(2)}) collective-permute-start(bf16[224,1536]{1,0:T(8,128)(2,1)S(1)} %partner_features.1), channel_id=1, source_target_pairs={{0,8},{4,12},{8,0},{12,4},{16,24},{20,28},{24,16},{28,20},{1,9},{5... | collective-permute-start | bytes 2064392 | tf_op jit(solution)/shard_map/ppermute | solution.py:27
  17.7 3.1 %forward_more.3 = (bf16[6,224,128]{2,1,0:T(8,128)(2,1)S(1)}, bf16[6,224,128]{2,1,0:T(8,128)(2,1)S(1)}, f32[12,224,128]{2,1,0:T(8,128)S(1)}) custom-call(s32[288]{0:T(512)S(1)} %get-tuple-element.48.entry_ref, bf16[288,128,128]{2,1,0:T(8,128)(2,1)S(1)} %turn_weights.1.w_ref, bf16[224,3072]{1,0:T(8,128)(2,1)S(1)} %copy-done, ...), custom_call_target="tpu_custom_call" | custom-call | flops 1000 | bytes 1000 | tf_op jit(solution)/shard_map/forward_more/pallas_call | solution.py:143
  20.8 0.1 collective-permute-start.1
  20.9 0.5 collective-permute-start.2
  21.4 1.1 collective-permute-done.1.near_lo_ref
  22.5 0.5 collective-permute-done.2.near_hi_ref
  23.0 8.8 %collective-permute-done.3.across_ref = bf16[12,224,128]{2,1,0:T(8,128)(2,1)S(1)} collective-permute-done((bf16[12,224,128]{2,1,0:T(8,128)(2,1)S(1)}, bf16[12,224,128]{2,1,0:T(8,128)(2,1)S(1)}, u32[]{:S(2)}, u32[]{:S(2)}) %collective-permute-start.3) | collective-permute-done | bytes 688160 | tf_op jit(solution)/shard_map/ppermute | solution.py:27
  31.9 1.0 own_slope.1
  32.9 1.9 %collective-permute-start.8 = (bf16[6,224,128]{2,1,0:T(8,128)(2,1)S(1)}, bf16[6,224,128]{2,1,0:T(8,128)(2,1)S(1)}, u32[]{:S(2)}, u32[]{:S(2)}) collective-permute-start(bf16[6,224,128]{2,1,0:T(8,128)(2,1)S(1)} %get-tuple-element.56), channel_id=1, source_target_pairs={{0,8},{4,12},{8,0},{12,4},{16,24},{20,28},{24,16},{28,20},{1,9},{5... | collective-permute-start | bytes 1032200 | tf_op jit(solution)/shard_map/ppermute | solution.py:27
  34.8 1.5 %collective-permute-start.10 = (bf16[6,224,128]{2,1,0:T(8,128)(2,1)S(1)}, bf16[6,224,128]{2,1,0:T(8,128)(2,1)S(1)}, u32[]{:S(2)}, u32[]{:S(2)}) collective-permute-start(bf16[6,224,128]{2,1,0:T(8,128)(2,1)S(1)} %get-tuple-element.58), channel_id=1, source_target_pairs={{0,2},{1,3},{2,0},{3,1},{4,6},{5,7},{6,4},{7,5},{8,10},{9,11},{10,... | collective-permute-start | bytes 1032200 | tf_op jit(solution)/shard_map/ppermute | solution.py:27
  36.3 0.4 collective-permute-start.7
  36.7 0.3 collective-permute-start.5
  37.0 0.3 turn_features.2.xt_ref
  37.3 0.3 turn_features.3.xt2_ref
  37.6 6.3 %collective-permute-done.8.refs_6_ = bf16[6,224,128]{2,1,0:T(8,128)(2,1)S(1)} collective-permute-done((bf16[6,224,128]{2,1,0:T(8,128)(2,1)S(1)}, bf16[6,224,128]{2,1,0:T(8,128)(2,1)S(1)}, u32[]{:S(2)}, u32[]{:S(2)}) %collective-permute-start.8) | collective-permute-done | bytes 344096 | tf_op jit(solution)/shard_map/ppermute | solution.py:27
  43.9 1.8 %collective-permute-start.9 = (bf16[6,224,128]{2,1,0:T(8,128)(2,1)S(1)}, bf16[6,224,128]{2,1,0:T(8,128)(2,1)S(1)}, u32[]{:S(2)}, u32[]{:S(2)}) collective-permute-start(bf16[6,224,128]{2,1,0:T(8,128)(2,1)S(1)} %collective-permute-done.8.refs_6_), channel_id=1, source_target_pairs={{0,2},{1,3},{2,0},{3,1},{4,6},{5,7},{6,4},{7,5},{8,10},{9,11},{10,... | collective-permute-start | bytes 1032200 | tf_op jit(solution)/shard_map/ppermute | solution.py:27
  45.7 0.1 collective-permute-done.10.refs_3_
  45.8 1.5 %collective-permute-start.11 = (bf16[6,224,128]{2,1,0:T(8,128)(2,1)S(1)}, bf16[6,224,128]{2,1,0:T(8,128)(2,1)S(1)}, u32[]{:S(2)}, u32[]{:S(2)}) collective-permute-start(bf16[6,224,128]{2,1,0:T(8,128)(2,1)S(1)} %collective-permute-done.10.refs_3_), channel_id=1, source_target_pairs={{0,8},{4,12},{8,0},{12,4},{16,24},{20,28},{24,16},{28,20},{1,9},{5... | collective-permute-start | bytes 1032200 | tf_op jit(solution)/shard_map/ppermute | solution.py:27
  47.3 4.0 %collective-permute-done.7.refs_7_ = bf16[6,224,128]{2,1,0:T(8,128)(2,1)S(1)} collective-permute-done((bf16[6,224,128]{2,1,0:T(8,128)(2,1)S(1)}, bf16[6,224,128]{2,1,0:T(8,128)(2,1)S(1)}, u32[]{:S(2)}, u32[]{:S(2)}) %collective-permute-start.7) | collective-permute-done | bytes 344096 | tf_op jit(solution)/shard_map/ppermute | solution.py:27
  51.3 1.9 %collective-permute-done.5.refs_2_ = bf16[6,224,128]{2,1,0:T(8,128)(2,1)S(1)} collective-permute-done((bf16[6,224,128]{2,1,0:T(8,128)(2,1)S(1)}, bf16[6,224,128]{2,1,0:T(8,128)(2,1)S(1)}, u32[]{:S(2)}, u32[]{:S(2)}) %collective-permute-start.5) | collective-permute-done | bytes 344096 | tf_op jit(solution)/shard_map/ppermute | solution.py:27
  53.1 5.5 %collective-permute-done.9.refs_10_ = bf16[6,224,128]{2,1,0:T(8,128)(2,1)S(1)} collective-permute-done((bf16[6,224,128]{2,1,0:T(8,128)(2,1)S(1)}, bf16[6,224,128]{2,1,0:T(8,128)(2,1)S(1)}, u32[]{:S(2)}, u32[]{:S(2)}) %collective-permute-start.9) | collective-permute-done | bytes 344096 | tf_op jit(solution)/shard_map/ppermute | solution.py:27
  58.7 0.5 collective-permute-start.15
  59.2 0.5 collective-permute-start.17
  59.7 0.6 collective-permute-done.12.refs_4_
  60.3 0.5 collective-permute-done.15.refs_9_
  60.8 0.5 collective-permute-done.16.refs_12_
  61.3 0.5 collective-permute-done.17.refs_13_
  61.8 4.4 %few_grads.1 = (bf16[2,2,192,128]{3,2,1,0:T(8,128)(2,1)S(1)}, f32[2,192,128]{2,1,0:T(8,128)S(1)}, f32[2,192,128]{2,1,0:T(8,128)S(1)}) custom-call(s32[12,24]{1,0:T(8,128)S(1)} %bitcast.34, bf16[12,128,224]{2,1,0:T(8,128)(2,1)S(1)} %turn_features.2.xt_ref, bf16[12,128,224]{2,1,0:T(8,128)(2,1)S(1)} %turn_features.3.xt2_ref, ...), custom_call_target="tpu_custom_call" | custom-call | flops 1000 | bytes 1000 | tf_op jit(solution)/shard_map/few_grads/pallas_call | solution.py:330
  66.2 1.5 %collective-permute-start.18 = (bf16[2,2,192,128]{3,2,1,0:T(8,128)(2,1)S(1)}, bf16[2,2,192,128]{3,2,1,0:T(8,128)(2,1)S(1)}, u32[]{:S(2)}, u32[]{:S(2)}) collective-permute-start(bf16[2,2,192,128]{3,2,1,0:T(8,128)(2,1)S(1)} %get-tuple-element.67.refs_14_), channel_id=1, source_target_pairs={{0,4},{4,0},{8,12},{12,8},{16,20},{20,16},{24,28},{28,24},{1,5},{5... | collective-permute-start | bytes 589832 | tf_op jit(solution)/shard_map/ppermute | solution.py:27
  67.8 3.6 %first_grads.1 = (bf16[2,5,192,128]{3,2,1,0:T(8,128)(2,1)S(1)}, f32[5,192,128]{2,1,0:T(8,128)S(1)}, f32[5,192,128]{2,1,0:T(8,128)S(1)}, bf16[96,224,128]{2,1,0:T(8,128)(2,1)S(1)}) custom-call(s32[12,24]{1,0:T(8,128)S(1)} %bitcast.35, bf16[12,128,224]{2,1,0:T(8,128)(2,1)S(1)} %turn_features.2.xt_ref, bf16[12,128,224]{2,1,0:T(8,128)(2,1)S(1)} %turn_features.3.xt2_ref, ...), custom_call_target="tpu_custom_call" | custom-call | flops 1000 | bytes 1000 | tf_op jit(solution)/shard_map/first_grads/pallas_call | solution.py:346
  71.4 0.6 collective-permute-start.21
  72.0 1.2 collective-permute-done.18
  73.3 2.7 %collective-permute-start.20 = (bf16[2,192,128]{2,1,0:T(8,128)(2,1)S(1)}, bf16[2,192,128]{2,1,0:T(8,128)(2,1)S(1)}, u32[]{:S(2)}, u32[]{:S(2)}) collective-permute-start(bf16[2,192,128]{2,1,0:T(8,128)(2,1)S(1)} %get-tuple-element.94.refs_0_), channel_id=1, source_target_pairs={{0,16},{4,20},{8,24},{12,28},{16,0},{20,4},{24,8},{28,12},{1,17},{... | collective-permute-start | bytes 294920 | tf_op jit(solution)/shard_map/ppermute | solution.py:27
  75.9 2.2 %more_grads.2 = (bf16[12,192,128]{2,1,0:T(8,128)(2,1)S(1)}, bf16[12,192,128]{2,1,0:T(8,128)(2,1)S(1)}, f32[12,192,128]{2,1,0:T(8,128)S(1)}, f32[12,192,128]{2,1,0:T(8,128)S(1)}) custom-call(s32[12,24]{1,0:T(8,128)S(1)} %bitcast.36, bf16[12,128,224]{2,1,0:T(8,128)(2,1)S(1)} %turn_features.2.xt_ref, bf16[12,128,224]{2,1,0:T(8,128)(2,1)S(1)} %turn_features.3.xt2_ref, ...), custom_call_target="tpu_custom_call" | custom-call | flops 1000 | bytes 1000 | tf_op jit(solution)/shard_map/more_grads/pallas_call | solution.py:361
  78.1 1.7 %collective-permute-start.25 = (bf16[12,192,128]{2,1,0:T(8,128)(2,1)S(1)}, bf16[12,192,128]{2,1,0:T(8,128)(2,1)S(1)}, u32[]{:S(2)}, u32[]{:S(2)}) collective-permute-start(bf16[12,192,128]{2,1,0:T(8,128)(2,1)S(1)} %get-tuple-element.87), channel_id=1, source_target_pairs={{0,4},{4,0},{8,12},{12,8},{16,20},{20,16},{24,28},{28,24},{1,5},{5... | collective-permute-start | bytes 1769480 | tf_op jit(solution)/shard_map/ppermute | solution.py:27
  79.9 0.1 collective-permute-start.19
  80.0 1.4 %more_grads.3 = (bf16[2,5,192,128]{3,2,1,0:T(8,128)(2,1)S(1)}, f32[5,192,128]{2,1,0:T(8,128)S(1)}, f32[5,192,128]{2,1,0:T(8,128)S(1)}) custom-call(s32[12,24]{1,0:T(8,128)S(1)} %bitcast.37, bf16[12,128,224]{2,1,0:T(8,128)(2,1)S(1)} %turn_features.2.xt_ref, bf16[12,128,224]{2,1,0:T(8,128)(2,1)S(1)} %turn_features.3.xt2_ref, ...), custom_call_target="tpu_custom_call" | custom-call | flops 1000 | bytes 1000 | tf_op jit(solution)/shard_map/more_grads/pallas_call | solution.py:361
  81.4 0.6 collective-permute-start.24
  82.0 3.5 %collective-permute-done.21 = bf16[2,5,192,128]{3,2,1,0:T(8,128)(2,1)S(1)} collective-permute-done((bf16[2,5,192,128]{3,2,1,0:T(8,128)(2,1)S(1)}, bf16[2,5,192,128]{3,2,1,0:T(8,128)(2,1)S(1)}, u32[]{:S(2)}, u32[]{:S(2)}) %collective-permute-start.21) | collective-permute-done | bytes 491552 | tf_op jit(solution)/shard_map/ppermute | solution.py:27
  85.6 0.1 fusion.3.refs_6_
  85.6 2.7 %collective-permute-start.22 = (bf16[5,192,128]{2,1,0:T(8,128)(2,1)S(1)}, bf16[5,192,128]{2,1,0:T(8,128)(2,1)S(1)}, u32[]{:S(2)}, u32[]{:S(2)}) collective-permute-start(bf16[5,192,128]{2,1,0:T(8,128)(2,1)S(1)} %fusion.3.refs_6_), channel_id=1, source_target_pairs={{0,16},{4,20},{8,24},{12,28},{16,0},{20,4},{24,8},{28,12},{1,17},{... | collective-permute-start | bytes 737288 | tf_op jit(solution)/shard_map/ppermute | solution.py:27
  88.3 0.1 fusion.2.refs_7_
  88.4 0.3 collective-permute-start.23
  88.7 0.6 collective-permute-start.26
  89.3 14.0 %collective-permute-done.22.refs_0_ = bf16[5,192,128]{2,1,0:T(8,128)(2,1)S(1)} collective-permute-done((bf16[5,192,128]{2,1,0:T(8,128)(2,1)S(1)}, bf16[5,192,128]{2,1,0:T(8,128)(2,1)S(1)}, u32[]{:S(2)}, u32[]{:S(2)}) %collective-permute-start.22) | collective-permute-done | bytes 245792 | tf_op jit(solution)/shard_map/ppermute | solution.py:27
  103.3 0.2 add_convert_fusion.1.refs_10_
  103.5 0.5 collective-permute-start.27
  104.0 4.8 %collective-permute-done.24 = bf16[2,5,192,128]{3,2,1,0:T(8,128)(2,1)S(1)} collective-permute-done((bf16[2,5,192,128]{3,2,1,0:T(8,128)(2,1)S(1)}, bf16[2,5,192,128]{3,2,1,0:T(8,128)(2,1)S(1)}, u32[]{:S(2)}, u32[]{:S(2)}) %collective-permute-start.24) | collective-permute-done | bytes 491552 | tf_op jit(solution)/shard_map/ppermute | solution.py:27
  108.7 0.1 fusion.1.refs_8_
  108.8 2.7 %collective-permute-start.28 = (bf16[5,192,128]{2,1,0:T(8,128)(2,1)S(1)}, bf16[5,192,128]{2,1,0:T(8,128)(2,1)S(1)}, u32[]{:S(2)}, u32[]{:S(2)}) collective-permute-start(bf16[5,192,128]{2,1,0:T(8,128)(2,1)S(1)} %fusion.1.refs_8_), channel_id=1, source_target_pairs={{0,16},{4,20},{8,24},{12,28},{16,0},{20,4},{24,8},{28,12},{1,17},{... | collective-permute-start | bytes 737288 | tf_op jit(solution)/shard_map/ppermute | solution.py:27
  111.5 0.1 fusion.refs_9_
  111.6 0.3 collective-permute-start.29
  111.9 14.3 %input_grads.1 = bf16[224,3072]{1,0:T(8,128)(2,1)} custom-call(s32[12,24]{1,0:T(8,128)S(1)} %bitcast.38, bf16[12,24,128,128]{3,2,1,0:T(8,128)(2,1)S(1)} %bitcast.32, bf16[12,224,128]{2,1,0:T(8,128)(2,1)S(1)} %get-tuple-element.55.refs_1_.refs_0_, bf16[12,224,128]{2,1,0:T(8,128)(2,1)S(1)} %collective-permute-done.4.refs_1_, ...), custom_call_target="tpu_custom_call" | custom-call | flops 1000 | bytes 1000 | tf_op jit(solution)/shard_map/input_grads/pallas_call | solution.py:390
  126.2 2.6 %collective-permute-done.28 = bf16[5,192,128]{2,1,0:T(8,128)(2,1)S(1)} collective-permute-done((bf16[5,192,128]{2,1,0:T(8,128)(2,1)S(1)}, bf16[5,192,128]{2,1,0:T(8,128)(2,1)S(1)}, u32[]{:S(2)}, u32[]{:S(2)}) %collective-permute-start.28) | collective-permute-done | bytes 245792 | tf_op jit(solution)/shard_map/ppermute | solution.py:27
  128.8 1.1 main_sum.1.base_ref
  129.9 2.1 %last_sum.1 = f32[192,24,128]{2,1,0:T(8,128)} custom-call(f32[192,24,128]{2,1,0:T(8,128)S(1)} %main_sum.1.base_ref, f32[5,192,128]{2,1,0:T(8,128)S(1)} %convert_element_type.91.mine_ref, bf16[5,192,128]{2,1,0:T(8,128)(2,1)S(1)} %collective-permute-done.29.other_ref), custom_call_target="tpu_custom_call" | custom-call | flops 1000 | bytes 1000 | tf_op jit(solution)/shard_map/last_sum/pallas_call | solution.py:458
  (25 shorter events, 0.1 us)
Async XLA Ops:
  0.6 7.1 %copy-start.2 = (s32[24,12]{0,1:T(8,128)S(1)}, s32[24,12]{0,1:T(8,128)}, u32[]{:S(2)}) copy-start(s32[24,12]{0,1:T(8,128)} %param.6) | copy-start | bytes 3460
  0.6 7.1 %copy-start = (bf16[224,3072]{1,0:T(8,128)(2,1)S(1)}, bf16[224,3072]{1,0:T(8,128)(2,1)}, u32[]{:S(2)}) copy-start(bf16[224,3072]{1,0:T(8,128)(2,1)} %refs_0_) | copy-start | bytes 4128772
  10.6 2.4 %collective-permute-start = (bf16[12,224,128]{2,1,0:T(8,128)(2,1)S(1)}, bf16[12,224,128]{2,1,0:T(8,128)(2,1)S(1)}, u32[]{:S(2)}, u32[]{:S(2)}) collective-permute-start(bf16[12,224,128]{2,1,0:T(8,128)(2,1)S(1)} %get-tuple-element.49), channel_id=1, source_target_pairs={{0,1},{1,0},{2,3},{3,2},{4,5},{5,4},{6,7},{7,6},{8,9},{9,8},{10,11... | collective-permute-start | bytes 2064392 | tf_op jit(solution)/shard_map/ppermute | solution.py:27
  13.2 18.7 %collective-permute-start.3 = (bf16[12,224,128]{2,1,0:T(8,128)(2,1)S(1)}, bf16[12,224,128]{2,1,0:T(8,128)(2,1)S(1)}, u32[]{:S(2)}, u32[]{:S(2)}) collective-permute-start(bf16[12,224,128]{2,1,0:T(8,128)(2,1)S(1)} %add_convert_fusion.refs_0_), channel_id=1, source_target_pairs={{0,2},{1,3},{2,0},{3,1},{4,6},{5,7},{6,4},{7,5},{8,10},{9,11},{10,... | collective-permute-start | bytes 2064392 | tf_op jit(solution)/shard_map/ppermute | solution.py:27
  16.0 15.8 %copy-start.1 = (bf16[224,1536]{1,0:T(8,128)(2,1)S(1)}, bf16[224,1536]{1,0:T(8,128)(2,1)}, u32[]{:S(2)}) copy-start(bf16[224,1536]{1,0:T(8,128)(2,1)} %cot_ref.1) | copy-start | bytes 2064388
  16.0 20.2 %collective-permute-start.6 = (bf16[224,1536]{1,0:T(8,128)(2,1)S(1)}, bf16[224,1536]{1,0:T(8,128)(2,1)S(1)}, u32[]{:S(2)}, u32[]{:S(2)}) collective-permute-start(bf16[224,1536]{1,0:T(8,128)(2,1)S(1)} %partner_features.1), channel_id=1, source_target_pairs={{0,8},{4,12},{8,0},{12,4},{16,24},{20,28},{24,16},{28,20},{1,9},{5... | collective-permute-start | bytes 2064392 | tf_op jit(solution)/shard_map/ppermute | solution.py:27
  20.8 1.7 %collective-permute-start.1 = (bf16[6,224,128]{2,1,0:T(8,128)(2,1)S(1)}, bf16[6,224,128]{2,1,0:T(8,128)(2,1)S(1)}, u32[]{:S(2)}, u32[]{:S(2)}) collective-permute-start(bf16[6,224,128]{2,1,0:T(8,128)(2,1)S(1)} %get-tuple-element.53.refs_1_), channel_id=1, source_target_pairs={{0,1},{1,0},{2,3},{3,2},{4,5},{5,4},{6,7},{7,6},{8,9},{9,8},{10,11... | collective-permute-start | bytes 1032200 | tf_op jit(solution)/shard_map/ppermute | solution.py:27
  20.9 2.1 %collective-permute-start.2 = (bf16[6,224,128]{2,1,0:T(8,128)(2,1)S(1)}, bf16[6,224,128]{2,1,0:T(8,128)(2,1)S(1)}, u32[]{:S(2)}, u32[]{:S(2)}) collective-permute-start(bf16[6,224,128]{2,1,0:T(8,128)(2,1)S(1)} %get-tuple-element.54), channel_id=1, source_target_pairs={{0,1},{1,0},{2,3},{3,2},{4,5},{5,4},{6,7},{7,6},{8,9},{9,8},{10,11... | collective-permute-start | bytes 1032200 | tf_op jit(solution)/shard_map/ppermute | solution.py:27
  32.9 11.0 %collective-permute-start.8 = (bf16[6,224,128]{2,1,0:T(8,128)(2,1)S(1)}, bf16[6,224,128]{2,1,0:T(8,128)(2,1)S(1)}, u32[]{:S(2)}, u32[]{:S(2)}) collective-permute-start(bf16[6,224,128]{2,1,0:T(8,128)(2,1)S(1)} %get-tuple-element.56), channel_id=1, source_target_pairs={{0,8},{4,12},{8,0},{12,4},{16,24},{20,28},{24,16},{28,20},{1,9},{5... | collective-permute-start | bytes 1032200 | tf_op jit(solution)/shard_map/ppermute | solution.py:27
  34.8 11.0 %collective-permute-start.10 = (bf16[6,224,128]{2,1,0:T(8,128)(2,1)S(1)}, bf16[6,224,128]{2,1,0:T(8,128)(2,1)S(1)}, u32[]{:S(2)}, u32[]{:S(2)}) collective-permute-start(bf16[6,224,128]{2,1,0:T(8,128)(2,1)S(1)} %get-tuple-element.58), channel_id=1, source_target_pairs={{0,2},{1,3},{2,0},{3,1},{4,6},{5,7},{6,4},{7,5},{8,10},{9,11},{10,... | collective-permute-start | bytes 1032200 | tf_op jit(solution)/shard_map/ppermute | solution.py:27
  36.3 15.0 %collective-permute-start.7 = (bf16[6,224,128]{2,1,0:T(8,128)(2,1)S(1)}, bf16[6,224,128]{2,1,0:T(8,128)(2,1)S(1)}, u32[]{:S(2)}, u32[]{:S(2)}) collective-permute-start(bf16[6,224,128]{2,1,0:T(8,128)(2,1)S(1)} %get-tuple-element.58), channel_id=1, source_target_pairs={{0,8},{4,12},{8,0},{12,4},{16,24},{20,28},{24,16},{28,20},{1,9},{5... | collective-permute-start | bytes 1032200 | tf_op jit(solution)/shard_map/ppermute | solution.py:27
  36.7 16.4 %collective-permute-start.5 = (bf16[6,224,128]{2,1,0:T(8,128)(2,1)S(1)}, bf16[6,224,128]{2,1,0:T(8,128)(2,1)S(1)}, u32[]{:S(2)}, u32[]{:S(2)}) collective-permute-start(bf16[6,224,128]{2,1,0:T(8,128)(2,1)S(1)} %get-tuple-element.56), channel_id=1, source_target_pairs={{0,2},{1,3},{2,0},{3,1},{4,6},{5,7},{6,4},{7,5},{8,10},{9,11},{10,... | collective-permute-start | bytes 1032200 | tf_op jit(solution)/shard_map/ppermute | solution.py:27
  43.9 14.8 %collective-permute-start.9 = (bf16[6,224,128]{2,1,0:T(8,128)(2,1)S(1)}, bf16[6,224,128]{2,1,0:T(8,128)(2,1)S(1)}, u32[]{:S(2)}, u32[]{:S(2)}) collective-permute-start(bf16[6,224,128]{2,1,0:T(8,128)(2,1)S(1)} %collective-permute-done.8.refs_6_), channel_id=1, source_target_pairs={{0,2},{1,3},{2,0},{3,1},{4,6},{5,7},{6,4},{7,5},{8,10},{9,11},{10,... | collective-permute-start | bytes 1032200 | tf_op jit(solution)/shard_map/ppermute | solution.py:27
  45.8 12.9 %collective-permute-start.11 = (bf16[6,224,128]{2,1,0:T(8,128)(2,1)S(1)}, bf16[6,224,128]{2,1,0:T(8,128)(2,1)S(1)}, u32[]{:S(2)}, u32[]{:S(2)}) collective-permute-start(bf16[6,224,128]{2,1,0:T(8,128)(2,1)S(1)} %collective-permute-done.10.refs_3_), channel_id=1, source_target_pairs={{0,8},{4,12},{8,0},{12,4},{16,24},{20,28},{24,16},{28,20},{1,9},{5... | collective-permute-start | bytes 1032200 | tf_op jit(solution)/shard_map/ppermute | solution.py:27
  47.3 11.9 %collective-permute-start.14 = (bf16[6,224,128]{2,1,0:T(8,128)(2,1)S(1)}, bf16[6,224,128]{2,1,0:T(8,128)(2,1)S(1)}, u32[]{:S(2)}, u32[]{:S(2)}) collective-permute-start(bf16[6,224,128]{2,1,0:T(8,128)(2,1)S(1)} %collective-permute-done.8.refs_6_), channel_id=1, source_target_pairs={{0,1},{1,0},{2,3},{3,2},{4,5},{5,4},{6,7},{7,6},{8,9},{9,8},{10,11... | collective-permute-start | bytes 1032200 | tf_op jit(solution)/shard_map/ppermute | solution.py:27
  51.3 8.4 %collective-permute-start.4 = (bf16[12,224,128]{2,1,0:T(8,128)(2,1)S(1)}, bf16[12,224,128]{2,1,0:T(8,128)(2,1)S(1)}, u32[]{:S(2)}, u32[]{:S(2)}) collective-permute-start(bf16[12,224,128]{2,1,0:T(8,128)(2,1)S(1)} %get-tuple-element.55.refs_1_.refs_0_), channel_id=1, source_target_pairs={{0,1},{1,0},{2,3},{3,2},{4,5},{5,4},{6,7},{7,6},{8,9},{9,8},{10,11... | collective-permute-start | bytes 2064392 | tf_op jit(solution)/shard_map/ppermute | solution.py:27
  53.1 6.1 %collective-permute-start.13 = (bf16[6,224,128]{2,1,0:T(8,128)(2,1)S(1)}, bf16[6,224,128]{2,1,0:T(8,128)(2,1)S(1)}, u32[]{:S(2)}, u32[]{:S(2)}) collective-permute-start(bf16[6,224,128]{2,1,0:T(8,128)(2,1)S(1)} %collective-permute-done.10.refs_3_), channel_id=1, source_target_pairs={{0,1},{1,0},{2,3},{3,2},{4,5},{5,4},{6,7},{7,6},{8,9},{9,8},{10,11... | collective-permute-start | bytes 1032200 | tf_op jit(solution)/shard_map/ppermute | solution.py:27
  58.7 1.7 %collective-permute-start.12 = (bf16[6,224,128]{2,1,0:T(8,128)(2,1)S(1)}, bf16[6,224,128]{2,1,0:T(8,128)(2,1)S(1)}, u32[]{:S(2)}, u32[]{:S(2)}) collective-permute-start(bf16[6,224,128]{2,1,0:T(8,128)(2,1)S(1)} %collective-permute-done.5.refs_2_), channel_id=1, source_target_pairs={{0,1},{1,0},{2,3},{3,2},{4,5},{5,4},{6,7},{7,6},{8,9},{9,8},{10,11... | collective-permute-start | bytes 1032200 | tf_op jit(solution)/shard_map/ppermute | solution.py:27
  58.7 2.1 %collective-permute-start.15 = (bf16[6,224,128]{2,1,0:T(8,128)(2,1)S(1)}, bf16[6,224,128]{2,1,0:T(8,128)(2,1)S(1)}, u32[]{:S(2)}, u32[]{:S(2)}) collective-permute-start(bf16[6,224,128]{2,1,0:T(8,128)(2,1)S(1)} %collective-permute-done.7.refs_7_), channel_id=1, source_target_pairs={{0,1},{1,0},{2,3},{3,2},{4,5},{5,4},{6,7},{7,6},{8,9},{9,8},{10,11... | collective-permute-start | bytes 1032200 | tf_op jit(solution)/shard_map/ppermute | solution.py:27
  59.2 2.1 %collective-permute-start.16 = (bf16[6,224,128]{2,1,0:T(8,128)(2,1)S(1)}, bf16[6,224,128]{2,1,0:T(8,128)(2,1)S(1)}, u32[]{:S(2)}, u32[]{:S(2)}) collective-permute-start(bf16[6,224,128]{2,1,0:T(8,128)(2,1)S(1)} %collective-permute-done.9.refs_10_), channel_id=1, source_target_pairs={{0,1},{1,0},{2,3},{3,2},{4,5},{5,4},{6,7},{7,6},{8,9},{9,8},{10,11... | collective-permute-start | bytes 1032200 | tf_op jit(solution)/shard_map/ppermute | solution.py:27
  59.2 2.6 %collective-permute-start.17 = (bf16[6,224,128]{2,1,0:T(8,128)(2,1)S(1)}, bf16[6,224,128]{2,1,0:T(8,128)(2,1)S(1)}, u32[]{:S(2)}, u32[]{:S(2)}) collective-permute-start(bf16[6,224,128]{2,1,0:T(8,128)(2,1)S(1)} %collective-permute-done.11.refs_11_), channel_id=1, source_target_pairs={{0,1},{1,0},{2,3},{3,2},{4,5},{5,4},{6,7},{7,6},{8,9},{9,8},{10,11... | collective-permute-start | bytes 1032200 | tf_op jit(solution)/shard_map/ppermute | solution.py:27
  66.2 7.0 %collective-permute-start.18 = (bf16[2,2,192,128]{3,2,1,0:T(8,128)(2,1)S(1)}, bf16[2,2,192,128]{3,2,1,0:T(8,128)(2,1)S(1)}, u32[]{:S(2)}, u32[]{:S(2)}) collective-permute-start(bf16[2,2,192,128]{3,2,1,0:T(8,128)(2,1)S(1)} %get-tuple-element.67.refs_14_), channel_id=1, source_target_pairs={{0,4},{4,0},{8,12},{12,8},{16,20},{20,16},{24,28},{28,24},{1,5},{5... | collective-permute-start | bytes 589832 | tf_op jit(solution)/shard_map/ppermute | solution.py:27
  71.4 14.2 %collective-permute-start.21 = (bf16[2,5,192,128]{3,2,1,0:T(8,128)(2,1)S(1)}, bf16[2,5,192,128]{3,2,1,0:T(8,128)(2,1)S(1)}, u32[]{:S(2)}, u32[]{:S(2)}) collective-permute-start(bf16[2,5,192,128]{3,2,1,0:T(8,128)(2,1)S(1)} %get-tuple-element.73), channel_id=1, source_target_pairs={{0,4},{4,0},{8,12},{12,8},{16,20},{20,16},{24,28},{28,24},{1,5},{5... | collective-permute-start | bytes 1474568 | tf_op jit(solution)/shard_map/ppermute | solution.py:27
  73.3 8.8 %collective-permute-start.20 = (bf16[2,192,128]{2,1,0:T(8,128)(2,1)S(1)}, bf16[2,192,128]{2,1,0:T(8,128)(2,1)S(1)}, u32[]{:S(2)}, u32[]{:S(2)}) collective-permute-start(bf16[2,192,128]{2,1,0:T(8,128)(2,1)S(1)} %get-tuple-element.94.refs_0_), channel_id=1, source_target_pairs={{0,16},{4,20},{8,24},{12,28},{16,0},{20,4},{24,8},{28,12},{1,17},{... | collective-permute-start | bytes 294920 | tf_op jit(solution)/shard_map/ppermute | solution.py:27
  78.1 25.2 %collective-permute-start.25 = (bf16[12,192,128]{2,1,0:T(8,128)(2,1)S(1)}, bf16[12,192,128]{2,1,0:T(8,128)(2,1)S(1)}, u32[]{:S(2)}, u32[]{:S(2)}) collective-permute-start(bf16[12,192,128]{2,1,0:T(8,128)(2,1)S(1)} %get-tuple-element.87), channel_id=1, source_target_pairs={{0,4},{4,0},{8,12},{12,8},{16,20},{20,16},{24,28},{28,24},{1,5},{5... | collective-permute-start | bytes 1769480 | tf_op jit(solution)/shard_map/ppermute | solution.py:27
  79.9 8.4 %collective-permute-start.19 = (bf16[2,192,128]{2,1,0:T(8,128)(2,1)S(1)}, bf16[2,192,128]{2,1,0:T(8,128)(2,1)S(1)}, u32[]{:S(2)}, u32[]{:S(2)}) collective-permute-start(bf16[2,192,128]{2,1,0:T(8,128)(2,1)S(1)} %get-tuple-element.95.refs_1_), channel_id=1, source_target_pairs={{0,24},{4,28},{8,16},{12,20},{16,8},{20,12},{24,0},{28,4},{1,25},{... | collective-permute-start | bytes 294920 | tf_op jit(solution)/shard_map/ppermute | solution.py:27
  81.4 27.3 %collective-permute-start.24 = (bf16[2,5,192,128]{3,2,1,0:T(8,128)(2,1)S(1)}, bf16[2,5,192,128]{3,2,1,0:T(8,128)(2,1)S(1)}, u32[]{:S(2)}, u32[]{:S(2)}) collective-permute-start(bf16[2,5,192,128]{3,2,1,0:T(8,128)(2,1)S(1)} %get-tuple-element.83), channel_id=1, source_target_pairs={{0,4},{4,0},{8,12},{12,8},{16,20},{20,16},{24,28},{28,24},{1,5},{5... | collective-permute-start | bytes 1474568 | tf_op jit(solution)/shard_map/ppermute | solution.py:27
  85.6 17.7 %collective-permute-start.22 = (bf16[5,192,128]{2,1,0:T(8,128)(2,1)S(1)}, bf16[5,192,128]{2,1,0:T(8,128)(2,1)S(1)}, u32[]{:S(2)}, u32[]{:S(2)}) collective-permute-start(bf16[5,192,128]{2,1,0:T(8,128)(2,1)S(1)} %fusion.3.refs_6_), channel_id=1, source_target_pairs={{0,16},{4,20},{8,24},{12,28},{16,0},{20,4},{24,8},{28,12},{1,17},{... | collective-permute-start | bytes 737288 | tf_op jit(solution)/shard_map/ppermute | solution.py:27
  88.4 23.1 %collective-permute-start.23 = (bf16[5,192,128]{2,1,0:T(8,128)(2,1)S(1)}, bf16[5,192,128]{2,1,0:T(8,128)(2,1)S(1)}, u32[]{:S(2)}, u32[]{:S(2)}) collective-permute-start(bf16[5,192,128]{2,1,0:T(8,128)(2,1)S(1)} %fusion.2.refs_7_), channel_id=1, source_target_pairs={{0,24},{4,28},{8,16},{12,20},{16,8},{20,12},{24,0},{28,4},{1,25},{... | collective-permute-start | bytes 737288 | tf_op jit(solution)/shard_map/ppermute | solution.py:27
  88.7 40.1 %collective-permute-start.26 = (bf16[12,192,128]{2,1,0:T(8,128)(2,1)S(1)}, bf16[12,192,128]{2,1,0:T(8,128)(2,1)S(1)}, u32[]{:S(2)}, u32[]{:S(2)}) collective-permute-start(bf16[12,192,128]{2,1,0:T(8,128)(2,1)S(1)} %get-tuple-element.89), channel_id=1, source_target_pairs={{0,4},{4,0},{8,12},{12,8},{16,20},{20,16},{24,28},{28,24},{1,5},{5... | collective-permute-start | bytes 1769480 | tf_op jit(solution)/shard_map/ppermute | solution.py:27
  103.5 25.3 %collective-permute-start.27 = (bf16[12,192,128]{2,1,0:T(8,128)(2,1)S(1)}, bf16[12,192,128]{2,1,0:T(8,128)(2,1)S(1)}, u32[]{:S(2)}, u32[]{:S(2)}) collective-permute-start(bf16[12,192,128]{2,1,0:T(8,128)(2,1)S(1)} %add_convert_fusion.1.refs_10_), channel_id=1, source_target_pairs={{0,8},{4,12},{8,0},{12,4},{16,24},{20,28},{24,16},{28,20},{1,9},{5... | collective-permute-start | bytes 1769480 | tf_op jit(solution)/shard_map/ppermute | solution.py:27
  108.8 19.9 %collective-permute-start.28 = (bf16[5,192,128]{2,1,0:T(8,128)(2,1)S(1)}, bf16[5,192,128]{2,1,0:T(8,128)(2,1)S(1)}, u32[]{:S(2)}, u32[]{:S(2)}) collective-permute-start(bf16[5,192,128]{2,1,0:T(8,128)(2,1)S(1)} %fusion.1.refs_8_), channel_id=1, source_target_pairs={{0,16},{4,20},{8,24},{12,28},{16,0},{20,4},{24,8},{28,12},{1,17},{... | collective-permute-start | bytes 737288 | tf_op jit(solution)/shard_map/ppermute | solution.py:27
  111.6 18.3 %collective-permute-start.29 = (bf16[5,192,128]{2,1,0:T(8,128)(2,1)S(1)}, bf16[5,192,128]{2,1,0:T(8,128)(2,1)S(1)}, u32[]{:S(2)}, u32[]{:S(2)}) collective-permute-start(bf16[5,192,128]{2,1,0:T(8,128)(2,1)S(1)} %fusion.refs_9_), channel_id=1, source_target_pairs={{0,24},{4,28},{8,16},{12,20},{16,8},{20,12},{24,0},{28,4},{1,25},{... | collective-permute-start | bytes 737288 | tf_op jit(solution)/shard_map/ppermute | solution.py:27

commit v2 on v1

--- a/solution.py
+++ b/solution.py
@@ -54,14 +54,11 @@
 def turn_weights(slots, rows, w_ref, wt_ref, raw, wide, sems):
     few = 8 * rows
 
-    def fetch(j, h):
-        return pltpu.make_async_copy(
-            w_ref.at[pl.ds(j * 128 + h * 64, 64)], raw.at[j, pl.ds(h * 64, 64)], sems.at[j, h]
-        )
-
-    for j in range(slots):
-        for h in range(2):
-            fetch(j, h).start(priority=h)
+    def fetch(n):
+        return pltpu.make_async_copy(w_ref.at[pl.ds(2 * n, 2)], raw.at[pl.ds(2 * n, 2)], sems.at[n])
+
+    for n in range(slots // 2):
+        fetch(n).start(priority=n % 2)
     to = lax.broadcasted_iota(jnp.int32, (few, few), 0)
     source = lax.broadcasted_iota(jnp.int32, (few, few), 1)
     turn = jnp.where(source == (to % 8) * rows + to // 8, 1.0, 0.0).astype(bf16)
@@ -69,9 +66,7 @@
     @pl.loop(0, slots // 2)
     def _(n):
         k, j = 2 * n, 2 * n + 1
-        for h in range(2):
-            fetch(k, h).wait()
-            fetch(j, h).wait()
+        fetch(n).wait()
         wide[...] = raw[k].astype(f32).reshape(128 * rows, 128)
         value = raw[j].astype(f32).reshape(128 * rows, 128).astype(bf16)
         for i in range(8):
@@ -95,13 +90,13 @@
         scratch_shapes=[
             pltpu.VMEM((slots, 128, rows, 128), bf16),
             pltpu.VMEM((128 * rows, 128), f32),
-            pltpu.SemaphoreType.DMA((slots, 2)),
+            pltpu.SemaphoreType.DMA((slots // 2,)),
         ],
         out_shape=jax.ShapeDtypeStruct((rows * slots, 128, 128), bf16),
         compiler_params=pltpu.CompilerParams(vmem_limit_bytes=FAR_LIMIT * 2**20),
         cost_estimate=SHORT,
         name="turn_weights",
-    )(weights)
+    )(weights.reshape(slots, 128, rows, 128))
 
 
 def forward_first(slots, groups, cols_ref, w_ref, x_ref, send_ref, entry_ref):
@@ -191,8 +186,8 @@
         n = ref.shape[0]
         copies.append(pltpu.make_async_copy(ref, held.at[pl.ds(at, n)], sems.at[i]))
         at += n
-    for c in copies:
-        c.start()
+    for i, c in enumerate(copies):
+        c.start(priority=i % 2)
     for c in copies:
         c.wait()
 
@@ -247,64 +242,32 @@
     )(features, after)
 
 
-def put_grads(low, r, xt_row, own, xt2_row, other, sends, keeps):
-    total = jnp.dot(xt_row, own, preferred_element_type=f32)
-    total += jnp.dot(xt2_row, other, preferred_element_type=f32)
-    for i, (send, keep) in enumerate(zip(sends, keeps)):
-        b0, b1, b2 = [total[:, (3 * i + kk) * 128 : (3 * i + kk + 1) * 128] for kk in range(3)]
-        v0 = jnp.concatenate([b0, b1[:64]], axis=0)
-        v1 = jnp.concatenate([b1[64:], b2], axis=0)
-        send[r] = jnp.where(low, v1, v0).astype(bf16)
-        keep[r] = jnp.where(low, v0, v1)
-
-
 def block_grads(slots, flips, lo, hi, cols_ref, xt_ref, xt2_ref, held, sends, keeps):
-    if len(sends) < len(flips):
-        sends = [sends[0].at[i] for i in range(len(flips))]
-    low = lax.rem(lax.axis_index("dp"), 2) == 0
+    s = lax.axis_index("tensor")
+    d = lax.axis_index("dp")
+    tokens_slots = 4 * slots
+    first_row = odd_z() * xt_ref.shape[0]
+    low = lax.rem(d, 2) == 0
     for r in range(lo, hi):
-        at = columns_of(slots, flips, r, xt_ref.shape[0], cols_ref)
+        at = []
+        for flip in flips:
+            first = (d // 2 ^ flip) * 3
+            at += [slot_of(cols_ref[first + kk, first_row + r], s, slots) for kk in range(3)]
         own = jnp.concatenate([held[a] for a in at], axis=1)
-        other = jnp.concatenate([held[4 * slots + a] for a in at], axis=1)
-        put_grads(low, r - lo, xt_ref[r], own, xt2_ref[r], other, sends, keeps)
-
-
-def columns_of(slots, flips, r, half_rows, cols_ref):
-    s, z = lax.axis_index("tensor"), lax.axis_index("dp") // 2
-    row = odd_z() * half_rows + r
-    return [slot_of(cols_ref[(z ^ flip) * 3 + kk, row], s, slots) for flip in flips for kk in range(3)]
-
-
-def few_grads(slots, flips, lo, hi, n_pieces, cols_ref, xt_ref, xt2_ref, *refs):
-    pieces, (send, *keeps), (tiles, sems) = refs[:n_pieces], refs[n_pieces:-2], refs[-2:]
-    per_row = 3 * len(flips)
-    half = 4 * slots
-    for r in range(lo, hi):
-        for i, at in enumerate(columns_of(slots, flips, r, xt_ref.shape[0], cols_ref)):
-            n = 2 * ((r - lo) * per_row + i)
-            start = 0
-            for ref in pieces:
-                count = ref.shape[0]
-                which = n if start < half else n + 1
-                here = at - start % half
-
-                @pl.when((here >= 0) & (here < count))
-                def _(ref=ref, which=which, here=here):
-                    pltpu.make_async_copy(ref.at[here], tiles.at[which], sems.at[which]).start()
-
-                start += count
-    for n in range(tiles.shape[0]):
-        pltpu.make_async_copy(pieces[0].at[0], tiles.at[n], sems.at[n]).wait()
-    low = lax.rem(lax.axis_index("dp"), 2) == 0
-    for r in range(lo, hi):
-        at = [2 * ((r - lo) * per_row + i) for i in range(per_row)]
-        own = jnp.concatenate([tiles[n] for n in at], axis=1)
-        other = jnp.concatenate([tiles[n + 1] for n in at], axis=1)
-        put_grads(low, r - lo, xt_ref[r], own, xt2_ref[r], other, [send.at[i] for i in range(len(flips))], keeps)
+        other = jnp.concatenate([held[tokens_slots + a] for a in at], axis=1)
+        total = jnp.dot(xt_ref[r], own, preferred_element_type=f32)
+        total += jnp.dot(xt2_ref[r], other, preferred_element_type=f32)
+        for i in range(len(flips)):
+            b0, b1, b2 = [total[:, (3 * i + kk) * 128 : (3 * i + kk + 1) * 128] for kk in range(3)]
+            v0 = jnp.concatenate([b0, b1[:64]], axis=0)
+            v1 = jnp.concatenate([b1[64:], b2], axis=0)
+            send = sends[i] if len(sends) > 1 else sends[0].at[i]
+            send[r - lo] = jnp.where(low, v1, v0).astype(bf16)
+            keeps[i][r - lo] = jnp.where(low, v0, v1)
 
 
 def first_grads(slots, flips, lo, hi, n_pieces, cols_ref, xt_ref, xt2_ref, *refs):
-    pieces, outs, (held, sems) = refs[:n_pieces], refs[n_pieces + 1 : -2], refs[-2:]
+    pieces, outs, (held, sems) = refs[:n_pieces], refs[n_pieces:-2], refs[-2:]
     load_pieces(pieces, held, sems)
     n = len(outs) - len(flips)
     block_grads(slots, flips, lo, hi, cols_ref, xt_ref, xt2_ref, held, outs[:n], outs[n:])
@@ -322,37 +285,20 @@
     return [jax.ShapeDtypeStruct(s, bf16) for s in sends] + [jax.ShapeDtypeStruct(part, f32)] * len(flips)
 
 
-def run_few_grads(cols, xt, xt2, pieces, flips, lo, hi):
-    slots, n = cols.shape[0], len(pieces)
-    tokens = pieces[0].shape[1]
-    shapes = grad_shapes(flips, lo, hi, True)
-    count = (hi - lo) * 6 * len(flips)
-    return pl.pallas_call(
-        functools.partial(few_grads, slots, flips, lo, hi, n),
-        in_specs=[pl.BlockSpec(memory_space=pltpu.SMEM), whole(), whole()] + [anywhere()] * n,
-        out_specs=[whole()] * len(shapes),
-        out_shape=shapes,
-        scratch_shapes=[pltpu.VMEM((count, tokens, 128), bf16), pltpu.SemaphoreType.DMA((count,))],
-        compiler_params=pltpu.CompilerParams(vmem_limit_bytes=12 * 2**20),
-        cost_estimate=SHORT,
-        name="few_grads",
-    )(cols, xt, xt2, *pieces)
-
-
-def run_first_grads(cols, xt, xt2, pieces, flips, lo, hi, after):
+def run_first_grads(cols, xt, xt2, pieces, flips, lo, hi):
     slots, n = cols.shape[0], len(pieces)
     tokens = pieces[0].shape[1]
     shapes = grad_shapes(flips, lo, hi, True) + [jax.ShapeDtypeStruct((8 * slots, tokens, 128), bf16)]
     return pl.pallas_call(
         functools.partial(first_grads, slots, flips, lo, hi, n),
-        in_specs=[pl.BlockSpec(memory_space=pltpu.SMEM), whole(), whole()] + [anywhere()] * (n + 1),
+        in_specs=[pl.BlockSpec(memory_space=pltpu.SMEM), whole(), whole()] + [anywhere()] * n,
         out_specs=[whole()] * len(shapes),
         out_shape=shapes,
         scratch_shapes=[pltpu.SemaphoreType.DMA((n,))],
         compiler_params=pltpu.CompilerParams(vmem_limit_bytes=20 * 2**20),
         cost_estimate=SHORT,
         name="first_grads",
-    )(cols, xt, xt2, *pieces, after)
+    )(cols, xt, xt2, *pieces)
 
 
 def run_more_grads(cols, xt, xt2, held, flips, lo, hi, joint, after=()):
@@ -412,24 +358,27 @@
     return jnp.where(even, mine, other), jnp.where(even, other, mine)
 
 
-def main_sum(scale, cuts, keep_ref, recv_ref, near_ref, *refs):
+def main_sum(scale, cuts, keep_ref, recv_ref, *refs):
     n = len(cuts) - 2
     mine_refs, other_refs, out_ref = refs[:n], refs[n:-1], refs[-1]
 
-    def half(base, fars):
-        parts = [base[: cuts[1]]]
+    def half(first, base, fars):
+        parts = [first]
         for i, far in enumerate(fars):
-            parts.append(base[cuts[i + 1] : cuts[i + 2]] + far[...].astype(f32))
+            here = slice(cuts[i + 1], cuts[i + 2])
+            parts.append(far[...].astype(f32) if base is None else base[here] + far[...].astype(f32))
         return jnp.concatenate(parts, axis=0) * scale
 
-    mine = half(keep_ref[...] + recv_ref[...].astype(f32), mine_refs)
-    other = half(near_ref[...].astype(f32), other_refs)
+    base = keep_ref[...] + recv_ref[...].astype(f32)
+    first = base[: cuts[1]]
+    mine = half(first, base, mine_refs)
+    other = half(jnp.zeros_like(first), None, other_refs)
     out_ref[...] = jnp.swapaxes(jnp.concatenate(by_rows(mine, other), axis=0), 0, 1)
 
 
-def run_main_sum(scale, cuts, keep, recv, near, fars_mine, fars_other):
+def run_main_sum(scale, cuts, keep, recv, fars_mine, fars_other):
     rows = 2 * keep.shape[0]
-    args = [keep, recv, near, *fars_mine, *fars_other]
+    args = [keep, recv, *fars_mine, *fars_other]
     return pl.pallas_call(
         functools.partial(main_sum, scale, cuts),
         grid=(6,),
@@ -442,29 +391,29 @@
     )(*args)
 
 
-def last_sum(scale, base_ref, mine_ref, other_ref, out_ref):
-    n, half = mine_ref.shape[0], base_ref.shape[1] // 2
-    fars = by_rows(mine_ref[...].astype(f32), other_ref[...].astype(f32))
-    for i, far in enumerate(fars):
-        lo = i * half
-        out_ref[:, lo : lo + n] = base_ref[:, lo : lo + n] + jnp.swapaxes(far * scale, 0, 1)
-        out_ref[:, lo + n : lo + half] = base_ref[:, lo + n : lo + half]
-
-
-def run_last_sum(scale, base, mine, other):
-    n, rows = mine.shape[0], base.shape[1]
+def last_sum(scale, base_ref, near_ref, mine_ref, other_ref, out_ref):
+    n, half = mine_ref.shape[0], near_ref.shape[0]
+    near = near_ref[...].astype(f32)
+    mine = jnp.concatenate([mine_ref[...].astype(f32), jnp.zeros_like(near[n:])], axis=0)
+    other = jnp.concatenate([near[:n] + other_ref[...].astype(f32), near[n:]], axis=0)
+    late = jnp.concatenate(by_rows(mine, other), axis=0) * scale
+    out_ref[...] = base_ref[...] + jnp.swapaxes(late, 0, 1)
+
+
+def run_last_sum(scale, base, near, mine, other):
+    rows = base.shape[1]
     tile = pl.BlockSpec((48, rows, 128), lambda i: (i, 0, 0))
-    far = pl.BlockSpec((n, 48, 128), lambda i: (0, i, 0))
+    late = [pl.BlockSpec((a.shape[0], 48, 128), lambda i: (0, i, 0)) for a in (near, mine, other)]
     return pl.pallas_call(
         functools.partial(last_sum, scale),
         grid=(4,),
-        in_specs=[tile, far, far],
+        in_specs=[tile, *late],
         out_specs=tile,
         out_shape=jax.ShapeDtypeStruct(base.shape, f32),
         compiler_params=pltpu.CompilerParams(vmem_limit_bytes=8 * 2**20),
         cost_estimate=SHORT,
         name="last_sum",
-    )(base, mine, other)
+    )(base, near, mine, other)
 
 
 def on_device(features, weights, block_cols, cotangent):
@@ -533,9 +482,9 @@
     def add(keep, recv):
         return (keep + recv.astype(f32)).astype(bf16)
 
-    send_a, *keeps_a = run_few_grads(cols, xt, xt2, pieces, far, cuts[2], cuts[3])
+    send_a, *keeps_a, held = run_first_grads(cols, xt, xt2, pieces, far, cuts[2], cuts[3])
     recv_a = swap(send_a, "dp", 1)
-    send_b, keep_b2, keep_b3, held = run_first_grads(cols, xt, xt2, pieces, far, cuts[1], cuts[2], send_a)
+    send_b, keep_b2, keep_b3 = run_more_grads(cols, xt, xt2, held, far, cuts[1], cuts[2], True)
     recv_b = swap(send_b, "dp", 1)
     totals_a = [add(*parts) for parts in zip(keeps_a, recv_a)]
     far_a2, far_a3 = swap(totals_a[0], "dp", 4), swap(totals_a[1], "dp", 6)
@@ -562,8 +511,8 @@
     near = swap(total1, "dp", 2)
 
     input_grad = run_input_grads(cols, turned, own, [total_b2, total_b3, total_c2, total_c3, total1])
-    base = run_main_sum(scale, cuts, keep0, recv0, near, [far_b2, far_a2], [far_b3, far_a3])
-    return input_grad, run_last_sum(scale, base, far_c2, far_c3)
+    base = run_main_sum(scale, cuts, keep0, recv0, [far_b2, far_a2], [far_b3, far_a3])
+    return input_grad, run_last_sum(scale, base, near, far_c2, far_c3)
 
 
 def solution(mesh):

time: 132 us -> 130 us (0.985)
  Pallas kernels: 45.7 us -> 42 us
    pallas_call x1 -> x0, Pallas kernels: 4.42 us -> none  [run_few_grads(): pl.pallas_call(functools.partial(few_grads, slots, flips, lo, hi, n), in_...]
    pallas_call x2 -> x3, Pallas kernels: 3.63 us -> 5.08 us  [run_more_grads(): pl.pallas_call(functools.partial(more_grads, slots, flips, lo, hi, len(af...]
  transfers between devices with their start and end apart: 30 -> 30, of which waited for: 17 -> 19; matrix products, arithmetic and copies ran while one was open for 0% -> 0% of each run, Pallas kernels for 22% -> 21%
where the time goes in v2:
time: 130 us
  waiting for transfers between devices  56.8 us (44%)
  Pallas kernels  42 us (32%)
  starting transfers between devices  29.2 us (22%)
    ppermute x30, waiting for transfers between devices, swap(): return lax.ppermute(value, axis, [(i, i ^ bit) for i in range(count)])  56.8 us
    ppermute x30, starting transfers between devices, swap(): return lax.ppermute(value, axis, [(i, i ^ bit) for i in range(count)])  29.2 us
    pallas_call x1, Pallas kernels, run_input_grads(): pl.pallas_call(functools.partial(input_grads, slots, len(pieces)), grid_s...  14.3 us
    pallas_call x1, Pallas kernels, run_turn_weights(): pl.pallas_call(functools.partial(turn_weights, slots, rows), in_specs=[an...  6.52 us
    pallas_call x3, Pallas kernels, run_more_grads(): pl.pallas_call(functools.partial(more_grads, slots, flips, lo, hi, len(af...  5.08 us
    pallas_call x2, Pallas kernels, run_forward_more(): pl.pallas_call(functools.partial(forward_more, slots, width // 512, [w[:2...  4.98 us
    pallas_call x1, Pallas kernels, run_first_grads(): pl.pallas_call(functools.partial(first_grads, slots, flips, lo, hi, n), i...  3.47 us
    pallas_call x1, Pallas kernels, run_forward_first(): pl.pallas_call(functools.partial(forward_first, slots, rows // 4), in_spe...  2.76 us
  transfers between devices with their start and end apart: 30, of which 19 were waited for; matrix products, arithmetic and copies ran while one was open for 0% of the time, Pallas kernels for 21%

profile of v2, /device:TPU:0, one launch (start us, length us, event | category | flops | bytes accessed | tf_op | source)
XLA Modules:
  0.0 129.5 jit_solution(262120938629315197)
XLA Ops:
  0.6 6.5 %turn_weights.1.w_ref = bf16[288,128,128]{2,1,0:T(8,128)(2,1)S(1)} custom-call(bf16[12,128,24,128]{3,2,1,0:T(8,128)(2,1)} %bitcast.40), custom_call_target="tpu_custom_call" | custom-call | flops 1000 | bytes 1000 | tf_op jit(solution)/shard_map/turn_weights/pallas_call | solution.py:86
  7.2 2.8 %forward_first.1 = (bf16[12,224,128]{2,1,0:T(8,128)(2,1)S(1)}, s32[288]{0:T(512)S(1)}) custom-call(s32[12,24]{1,0:T(8,128)S(1)} %bitcast.34, bf16[288,128,128]{2,1,0:T(8,128)(2,1)S(1)} %turn_weights.1.w_ref, bf16[224,3072]{1,0:T(8,128)(2,1)S(1)} %copy-done), custom_call_target="tpu_custom_call" | custom-call | flops 1000 | bytes 1000 | tf_op jit(solution)/shard_map/forward_first/pallas_call | solution.py:121
  10.0 0.5 collective-permute-start
  10.5 1.9 %forward_more.2 = f32[12,224,128]{2,1,0:T(8,128)S(1)} custom-call(s32[288]{0:T(512)S(1)} %get-tuple-element.48.entry_ref, bf16[288,128,128]{2,1,0:T(8,128)(2,1)S(1)} %turn_weights.1.w_ref, bf16[224,3072]{1,0:T(8,128)(2,1)S(1)} %copy-done), custom_call_target="tpu_custom_call" | custom-call | flops 1000 | bytes 1000 | tf_op jit(solution)/shard_map/forward_more/pallas_call | solution.py:138
  12.4 0.2 add_convert_fusion.refs_0_
  12.6 2.8 %collective-permute-start.3 = (bf16[12,224,128]{2,1,0:T(8,128)(2,1)S(1)}, bf16[12,224,128]{2,1,0:T(8,128)(2,1)S(1)}, u32[]{:S(2)}, u32[]{:S(2)}) collective-permute-start(bf16[12,224,128]{2,1,0:T(8,128)(2,1)S(1)} %add_convert_fusion.refs_0_), channel_id=1, source_target_pairs={{0,2},{1,3},{2,0},{3,1},{4,6},{5,7},{6,4},{7,5},{8,10},{9,11},{10,... | collective-permute-start | bytes 2064392 | tf_op jit(solution)/shard_map/ppermute | solution.py:27
  15.4 0.1 partner_features.1
  15.5 1.6 %collective-permute-start.6 = (bf16[224,1536]{1,0:T(8,128)(2,1)S(1)}, bf16[224,1536]{1,0:T(8,128)(2,1)S(1)}, u32[]{:S(2)}, u32[]{:S(2)}) collective-permute-start(bf16[224,1536]{1,0:T(8,128)(2,1)S(1)} %partner_features.1), channel_id=1, source_target_pairs={{0,8},{4,12},{8,0},{12,4},{16,24},{20,28},{24,16},{28,20},{1,9},{5... | collective-permute-start | bytes 2064392 | tf_op jit(solution)/shard_map/ppermute | solution.py:27
  17.1 3.1 %forward_more.3 = (bf16[6,224,128]{2,1,0:T(8,128)(2,1)S(1)}, bf16[6,224,128]{2,1,0:T(8,128)(2,1)S(1)}, f32[12,224,128]{2,1,0:T(8,128)S(1)}) custom-call(s32[288]{0:T(512)S(1)} %get-tuple-element.48.entry_ref, bf16[288,128,128]{2,1,0:T(8,128)(2,1)S(1)} %turn_weights.1.w_ref, bf16[224,3072]{1,0:T(8,128)(2,1)S(1)} %copy-done, ...), custom_call_target="tpu_custom_call" | custom-call | flops 1000 | bytes 1000 | tf_op jit(solution)/shard_map/forward_more/pallas_call | solution.py:138
  20.2 0.1 collective-permute-start.1
  20.3 0.5 collective-permute-start.2
  20.8 1.1 collective-permute-done.1.near_lo_ref
  21.9 0.5 collective-permute-done.2.near_hi_ref
  22.4 8.9 %collective-permute-done.3.across_ref = bf16[12,224,128]{2,1,0:T(8,128)(2,1)S(1)} collective-permute-done((bf16[12,224,128]{2,1,0:T(8,128)(2,1)S(1)}, bf16[12,224,128]{2,1,0:T(8,128)(2,1)S(1)}, u32[]{:S(2)}, u32[]{:S(2)}) %collective-permute-start.3) | collective-permute-done | bytes 688160 | tf_op jit(solution)/shard_map/ppermute | solution.py:27
  31.3 1.0 own_slope.1
  32.3 1.9 %collective-permute-start.8 = (bf16[6,224,128]{2,1,0:T(8,128)(2,1)S(1)}, bf16[6,224,128]{2,1,0:T(8,128)(2,1)S(1)}, u32[]{:S(2)}, u32[]{:S(2)}) collective-permute-start(bf16[6,224,128]{2,1,0:T(8,128)(2,1)S(1)} %get-tuple-element.56), channel_id=1, source_target_pairs={{0,8},{4,12},{8,0},{12,4},{16,24},{20,28},{24,16},{28,20},{1,9},{5... | collective-permute-start | bytes 1032200 | tf_op jit(solution)/shard_map/ppermute | solution.py:27
  34.1 1.5 %collective-permute-start.10 = (bf16[6,224,128]{2,1,0:T(8,128)(2,1)S(1)}, bf16[6,224,128]{2,1,0:T(8,128)(2,1)S(1)}, u32[]{:S(2)}, u32[]{:S(2)}) collective-permute-start(bf16[6,224,128]{2,1,0:T(8,128)(2,1)S(1)} %get-tuple-element.58), channel_id=1, source_target_pairs={{0,2},{1,3},{2,0},{3,1},{4,6},{5,7},{6,4},{7,5},{8,10},{9,11},{10,... | collective-permute-start | bytes 1032200 | tf_op jit(solution)/shard_map/ppermute | solution.py:27
  35.7 0.4 collective-permute-start.7
  36.1 0.3 collective-permute-start.5
  36.4 0.3 turn_features.2.xt_ref
  36.7 0.3 turn_features.3.xt2_ref
  37.0 6.3 %collective-permute-done.8.refs_6_ = bf16[6,224,128]{2,1,0:T(8,128)(2,1)S(1)} collective-permute-done((bf16[6,224,128]{2,1,0:T(8,128)(2,1)S(1)}, bf16[6,224,128]{2,1,0:T(8,128)(2,1)S(1)}, u32[]{:S(2)}, u32[]{:S(2)}) %collective-permute-start.8) | collective-permute-done | bytes 344096 | tf_op jit(solution)/shard_map/ppermute | solution.py:27
  43.3 1.8 %collective-permute-start.9 = (bf16[6,224,128]{2,1,0:T(8,128)(2,1)S(1)}, bf16[6,224,128]{2,1,0:T(8,128)(2,1)S(1)}, u32[]{:S(2)}, u32[]{:S(2)}) collective-permute-start(bf16[6,224,128]{2,1,0:T(8,128)(2,1)S(1)} %collective-permute-done.8.refs_6_), channel_id=1, source_target_pairs={{0,2},{1,3},{2,0},{3,1},{4,6},{5,7},{6,4},{7,5},{8,10},{9,11},{10,... | collective-permute-start | bytes 1032200 | tf_op jit(solution)/shard_map/ppermute | solution.py:27
  45.1 0.1 collective-permute-done.10.refs_3_
  45.1 1.5 %collective-permute-start.11 = (bf16[6,224,128]{2,1,0:T(8,128)(2,1)S(1)}, bf16[6,224,128]{2,1,0:T(8,128)(2,1)S(1)}, u32[]{:S(2)}, u32[]{:S(2)}) collective-permute-start(bf16[6,224,128]{2,1,0:T(8,128)(2,1)S(1)} %collective-permute-done.10.refs_3_), channel_id=1, source_target_pairs={{0,8},{4,12},{8,0},{12,4},{16,24},{20,28},{24,16},{28,20},{1,9},{5... | collective-permute-start | bytes 1032200 | tf_op jit(solution)/shard_map/ppermute | solution.py:27
  46.7 4.0 %collective-permute-done.7.refs_7_ = bf16[6,224,128]{2,1,0:T(8,128)(2,1)S(1)} collective-permute-done((bf16[6,224,128]{2,1,0:T(8,128)(2,1)S(1)}, bf16[6,224,128]{2,1,0:T(8,128)(2,1)S(1)}, u32[]{:S(2)}, u32[]{:S(2)}) %collective-permute-start.7) | collective-permute-done | bytes 344096 | tf_op jit(solution)/shard_map/ppermute | solution.py:27
  50.7 1.9 %collective-permute-done.5.refs_2_ = bf16[6,224,128]{2,1,0:T(8,128)(2,1)S(1)} collective-permute-done((bf16[6,224,128]{2,1,0:T(8,128)(2,1)S(1)}, bf16[6,224,128]{2,1,0:T(8,128)(2,1)S(1)}, u32[]{:S(2)}, u32[]{:S(2)}) %collective-permute-start.5) | collective-permute-done | bytes 344096 | tf_op jit(solution)/shard_map/ppermute | solution.py:27
  52.5 5.5 %collective-permute-done.9.refs_10_ = bf16[6,224,128]{2,1,0:T(8,128)(2,1)S(1)} collective-permute-done((bf16[6,224,128]{2,1,0:T(8,128)(2,1)S(1)}, bf16[6,224,128]{2,1,0:T(8,128)(2,1)S(1)}, u32[]{:S(2)}, u32[]{:S(2)}) %collective-permute-start.9) | collective-permute-done | bytes 344096 | tf_op jit(solution)/shard_map/ppermute | solution.py:27
  58.1 0.5 collective-permute-start.15
  58.6 0.5 collective-permute-start.17
  59.1 0.6 collective-permute-done.12.refs_4_
  59.7 0.5 collective-permute-done.15.refs_9_
  60.2 0.5 collective-permute-done.16.refs_12_
  60.7 0.5 collective-permute-done.17.refs_13_
  61.2 3.5 %first_grads.1 = (bf16[2,2,192,128]{3,2,1,0:T(8,128)(2,1)S(1)}, f32[2,192,128]{2,1,0:T(8,128)S(1)}, f32[2,192,128]{2,1,0:T(8,128)S(1)}, bf16[96,224,128]{2,1,0:T(8,128)(2,1)S(1)}) custom-call(s32[12,24]{1,0:T(8,128)S(1)} %bitcast.35, bf16[12,128,224]{2,1,0:T(8,128)(2,1)S(1)} %turn_features.2.xt_ref, bf16[12,128,224]{2,1,0:T(8,128)(2,1)S(1)} %turn_features.3.xt2_ref, ...), custom_call_target="tpu_custom_call" | custom-call | flops 1000 | bytes 1000 | tf_op jit(solution)/shard_map/first_grads/pallas_call | solution.py:292
  64.7 1.5 %collective-permute-start.18 = (bf16[2,2,192,128]{3,2,1,0:T(8,128)(2,1)S(1)}, bf16[2,2,192,128]{3,2,1,0:T(8,128)(2,1)S(1)}, u32[]{:S(2)}, u32[]{:S(2)}) collective-permute-start(bf16[2,2,192,128]{3,2,1,0:T(8,128)(2,1)S(1)} %get-tuple-element.70), channel_id=1, source_target_pairs={{0,4},{4,0},{8,12},{12,8},{16,20},{20,16},{24,28},{28,24},{1,5},{5... | collective-permute-start | bytes 589832 | tf_op jit(solution)/shard_map/ppermute | solution.py:27
  66.2 1.4 %more_grads.3 = (bf16[2,5,192,128]{3,2,1,0:T(8,128)(2,1)S(1)}, f32[5,192,128]{2,1,0:T(8,128)S(1)}, f32[5,192,128]{2,1,0:T(8,128)S(1)}) custom-call(s32[12,24]{1,0:T(8,128)S(1)} %bitcast.36, bf16[12,128,224]{2,1,0:T(8,128)(2,1)S(1)} %turn_features.2.xt_ref, bf16[12,128,224]{2,1,0:T(8,128)(2,1)S(1)} %turn_features.3.xt2_ref, ...), custom_call_target="tpu_custom_call" | custom-call | flops 1000 | bytes 1000 | tf_op jit(solution)/shard_map/more_grads/pallas_call | solution.py:307
  67.7 0.6 collective-permute-start.21
  68.3 4.2 %collective-permute-done.18 = bf16[2,2,192,128]{3,2,1,0:T(8,128)(2,1)S(1)} collective-permute-done((bf16[2,2,192,128]{3,2,1,0:T(8,128)(2,1)S(1)}, bf16[2,2,192,128]{3,2,1,0:T(8,128)(2,1)S(1)}, u32[]{:S(2)}, u32[]{:S(2)}) %collective-permute-start.18) | collective-permute-done | bytes 196640 | tf_op jit(solution)/shard_map/ppermute | solution.py:27
  72.5 2.7 %collective-permute-start.20 = (bf16[2,192,128]{2,1,0:T(8,128)(2,1)S(1)}, bf16[2,192,128]{2,1,0:T(8,128)(2,1)S(1)}, u32[]{:S(2)}, u32[]{:S(2)}) collective-permute-start(bf16[2,192,128]{2,1,0:T(8,128)(2,1)S(1)} %get-tuple-element.94.refs_0_), channel_id=1, source_target_pairs={{0,16},{4,20},{8,24},{12,28},{16,0},{20,4},{24,8},{28,12},{1,17},{... | collective-permute-start | bytes 294920 | tf_op jit(solution)/shard_map/ppermute | solution.py:27
  75.2 2.2 %more_grads.4 = (bf16[12,192,128]{2,1,0:T(8,128)(2,1)S(1)}, bf16[12,192,128]{2,1,0:T(8,128)(2,1)S(1)}, f32[12,192,128]{2,1,0:T(8,128)S(1)}, f32[12,192,128]{2,1,0:T(8,128)S(1)}) custom-call(s32[12,24]{1,0:T(8,128)S(1)} %bitcast.37, bf16[12,128,224]{2,1,0:T(8,128)(2,1)S(1)} %turn_features.2.xt_ref, bf16[12,128,224]{2,1,0:T(8,128)(2,1)S(1)} %turn_features.3.xt2_ref, ...), custom_call_target="tpu_custom_call" | custom-call | flops 1000 | bytes 1000 | tf_op jit(solution)/shard_map/more_grads/pallas_call | solution.py:307
  77.4 1.6 %collective-permute-start.25 = (bf16[12,192,128]{2,1,0:T(8,128)(2,1)S(1)}, bf16[12,192,128]{2,1,0:T(8,128)(2,1)S(1)}, u32[]{:S(2)}, u32[]{:S(2)}) collective-permute-start(bf16[12,192,128]{2,1,0:T(8,128)(2,1)S(1)} %get-tuple-element.87), channel_id=1, source_target_pairs={{0,4},{4,0},{8,12},{12,8},{16,20},{20,16},{24,28},{28,24},{1,5},{5... | collective-permute-start | bytes 1769480 | tf_op jit(solution)/shard_map/ppermute | solution.py:27
  79.0 0.2 collective-permute-start.19
  79.2 1.4 %more_grads.5 = (bf16[2,5,192,128]{3,2,1,0:T(8,128)(2,1)S(1)}, f32[5,192,128]{2,1,0:T(8,128)S(1)}, f32[5,192,128]{2,1,0:T(8,128)S(1)}) custom-call(s32[12,24]{1,0:T(8,128)S(1)} %bitcast.38, bf16[12,128,224]{2,1,0:T(8,128)(2,1)S(1)} %turn_features.2.xt_ref, bf16[12,128,224]{2,1,0:T(8,128)(2,1)S(1)} %turn_features.3.xt2_ref, ...), custom_call_target="tpu_custom_call" | custom-call | flops 1000 | bytes 1000 | tf_op jit(solution)/shard_map/more_grads/pallas_call | solution.py:307
  80.6 0.7 collective-permute-start.24
  81.3 1.7 %collective-permute-done.21 = bf16[2,5,192,128]{3,2,1,0:T(8,128)(2,1)S(1)} collective-permute-done((bf16[2,5,192,128]{3,2,1,0:T(8,128)(2,1)S(1)}, bf16[2,5,192,128]{3,2,1,0:T(8,128)(2,1)S(1)}, u32[]{:S(2)}, u32[]{:S(2)}) %collective-permute-start.21) | collective-permute-done | bytes 491552 | tf_op jit(solution)/shard_map/ppermute | solution.py:27
  83.1 2.7 %collective-permute-start.22 = (bf16[5,192,128]{2,1,0:T(8,128)(2,1)S(1)}, bf16[5,192,128]{2,1,0:T(8,128)(2,1)S(1)}, u32[]{:S(2)}, u32[]{:S(2)}) collective-permute-start(bf16[5,192,128]{2,1,0:T(8,128)(2,1)S(1)} %fusion.3.refs_6_), channel_id=1, source_target_pairs={{0,16},{4,20},{8,24},{12,28},{16,0},{20,4},{24,8},{28,12},{1,17},{... | collective-permute-start | bytes 737288 | tf_op jit(solution)/shard_map/ppermute | solution.py:27
  85.7 0.1 collective-permute-done.19.refs_3_
  85.8 0.1 fusion.2.refs_7_
  85.8 0.3 collective-permute-start.23
  86.1 1.4 %collective-permute-start.26 = (bf16[12,192,128]{2,1,0:T(8,128)(2,1)S(1)}, bf16[12,192,128]{2,1,0:T(8,128)(2,1)S(1)}, u32[]{:S(2)}, u32[]{:S(2)}) collective-permute-start(bf16[12,192,128]{2,1,0:T(8,128)(2,1)S(1)} %get-tuple-element.89), channel_id=1, source_target_pairs={{0,4},{4,0},{8,12},{12,8},{16,20},{20,16},{24,28},{28,24},{1,5},{5... | collective-permute-start | bytes 1769480 | tf_op jit(solution)/shard_map/ppermute | solution.py:27
  87.5 13.7 %collective-permute-done.22.refs_0_ = bf16[5,192,128]{2,1,0:T(8,128)(2,1)S(1)} collective-permute-done((bf16[5,192,128]{2,1,0:T(8,128)(2,1)S(1)}, bf16[5,192,128]{2,1,0:T(8,128)(2,1)S(1)}, u32[]{:S(2)}, u32[]{:S(2)}) %collective-permute-start.22) | collective-permute-done | bytes 245792 | tf_op jit(solution)/shard_map/ppermute | solution.py:27
  101.3 0.1 add_convert_fusion.1.refs_10_
  101.4 0.5 collective-permute-start.27
  102.0 4.2 %collective-permute-done.24 = bf16[2,5,192,128]{3,2,1,0:T(8,128)(2,1)S(1)} collective-permute-done((bf16[2,5,192,128]{3,2,1,0:T(8,128)(2,1)S(1)}, bf16[2,5,192,128]{3,2,1,0:T(8,128)(2,1)S(1)}, u32[]{:S(2)}, u32[]{:S(2)}) %collective-permute-start.24) | collective-permute-done | bytes 491552 | tf_op jit(solution)/shard_map/ppermute | solution.py:27
  106.2 0.1 fusion.1.refs_8_
  106.3 2.7 %collective-permute-start.28 = (bf16[5,192,128]{2,1,0:T(8,128)(2,1)S(1)}, bf16[5,192,128]{2,1,0:T(8,128)(2,1)S(1)}, u32[]{:S(2)}, u32[]{:S(2)}) collective-permute-start(bf16[5,192,128]{2,1,0:T(8,128)(2,1)S(1)} %fusion.1.refs_8_), channel_id=1, source_target_pairs={{0,16},{4,20},{8,24},{12,28},{16,0},{20,4},{24,8},{28,12},{1,17},{... | collective-permute-start | bytes 737288 | tf_op jit(solution)/shard_map/ppermute | solution.py:27
  108.9 0.1 fusion.refs_9_
  109.0 0.4 collective-permute-start.29
  109.3 14.3 %input_grads.1 = bf16[224,3072]{1,0:T(8,128)(2,1)} custom-call(s32[12,24]{1,0:T(8,128)S(1)} %bitcast.39, bf16[12,24,128,128]{3,2,1,0:T(8,128)(2,1)S(1)} %bitcast.33, bf16[12,224,128]{2,1,0:T(8,128)(2,1)S(1)} %get-tuple-element.55.refs_1_.refs_0_, bf16[12,224,128]{2,1,0:T(8,128)(2,1)S(1)} %collective-permute-done.4.refs_1_, ...), custom_call_target="tpu_custom_call" | custom-call | flops 1000 | bytes 1000 | tf_op jit(solution)/shard_map/input_grads/pallas_call | solution.py:336
  123.7 1.0 main_sum.1.base_ref
  124.7 2.0 %collective-permute-done.29.other_ref = bf16[5,192,128]{2,1,0:T(8,128)(2,1)S(1)} collective-permute-done((bf16[5,192,128]{2,1,0:T(8,128)(2,1)S(1)}, bf16[5,192,128]{2,1,0:T(8,128)(2,1)S(1)}, u32[]{:S(2)}, u32[]{:S(2)}) %collective-permute-start.29) | collective-permute-done | bytes 245792 | tf_op jit(solution)/shard_map/ppermute | solution.py:27
  126.7 0.5 collective-permute-done.27.near_ref
  127.2 2.3 %last_sum.1 = f32[192,24,128]{2,1,0:T(8,128)} custom-call(f32[192,24,128]{2,1,0:T(8,128)S(1)} %main_sum.1.base_ref, bf16[12,192,128]{2,1,0:T(8,128)(2,1)S(1)} %collective-permute-done.27.near_ref, f32[5,192,128]{2,1,0:T(8,128)S(1)} %convert_element_type.91.mine_ref, bf16[5,192,128]{2,1,0:T(8,128)(2,1)S(1)} %collective-permute-done.29.other_ref), custom_call_target="tpu_custom_call" | custom-call | flops 1000 | bytes 1000 | tf_op jit(solution)/shard_map/last_sum/pallas_call | solution.py:407
  (25 shorter events, 0.2 us)
Async XLA Ops:
  0.6 6.5 %copy-start = (bf16[224,3072]{1,0:T(8,128)(2,1)S(1)}, bf16[224,3072]{1,0:T(8,128)(2,1)}, u32[]{:S(2)}) copy-start(bf16[224,3072]{1,0:T(8,128)(2,1)} %refs_0_) | copy-start | bytes 4128772
  0.6 6.5 %copy-start.2 = (s32[24,12]{0,1:T(8,128)S(1)}, s32[24,12]{0,1:T(8,128)}, u32[]{:S(2)}) copy-start(s32[24,12]{0,1:T(8,128)} %param.6) | copy-start | bytes 3460
  10.0 2.4 %collective-permute-start = (bf16[12,224,128]{2,1,0:T(8,128)(2,1)S(1)}, bf16[12,224,128]{2,1,0:T(8,128)(2,1)S(1)}, u32[]{:S(2)}, u32[]{:S(2)}) collective-permute-start(bf16[12,224,128]{2,1,0:T(8,128)(2,1)S(1)} %get-tuple-element.49), channel_id=1, source_target_pairs={{0,1},{1,0},{2,3},{3,2},{4,5},{5,4},{6,7},{7,6},{8,9},{9,8},{10,11... | collective-permute-start | bytes 2064392 | tf_op jit(solution)/shard_map/ppermute | solution.py:27
  12.6 18.7 %collective-permute-start.3 = (bf16[12,224,128]{2,1,0:T(8,128)(2,1)S(1)}, bf16[12,224,128]{2,1,0:T(8,128)(2,1)S(1)}, u32[]{:S(2)}, u32[]{:S(2)}) collective-permute-start(bf16[12,224,128]{2,1,0:T(8,128)(2,1)S(1)} %add_convert_fusion.refs_0_), channel_id=1, source_target_pairs={{0,2},{1,3},{2,0},{3,1},{4,6},{5,7},{6,4},{7,5},{8,10},{9,11},{10,... | collective-permute-start | bytes 2064392 | tf_op jit(solution)/shard_map/ppermute | solution.py:27
  15.4 15.8 %copy-start.1 = (bf16[224,1536]{1,0:T(8,128)(2,1)S(1)}, bf16[224,1536]{1,0:T(8,128)(2,1)}, u32[]{:S(2)}) copy-start(bf16[224,1536]{1,0:T(8,128)(2,1)} %cot_ref.1) | copy-start | bytes 2064388
  15.5 20.2 %collective-permute-start.6 = (bf16[224,1536]{1,0:T(8,128)(2,1)S(1)}, bf16[224,1536]{1,0:T(8,128)(2,1)S(1)}, u32[]{:S(2)}, u32[]{:S(2)}) collective-permute-start(bf16[224,1536]{1,0:T(8,128)(2,1)S(1)} %partner_features.1), channel_id=1, source_target_pairs={{0,8},{4,12},{8,0},{12,4},{16,24},{20,28},{24,16},{28,20},{1,9},{5... | collective-permute-start | bytes 2064392 | tf_op jit(solution)/shard_map/ppermute | solution.py:27
  20.2 1.7 %collective-permute-start.1 = (bf16[6,224,128]{2,1,0:T(8,128)(2,1)S(1)}, bf16[6,224,128]{2,1,0:T(8,128)(2,1)S(1)}, u32[]{:S(2)}, u32[]{:S(2)}) collective-permute-start(bf16[6,224,128]{2,1,0:T(8,128)(2,1)S(1)} %get-tuple-element.53.refs_1_), channel_id=1, source_target_pairs={{0,1},{1,0},{2,3},{3,2},{4,5},{5,4},{6,7},{7,6},{8,9},{9,8},{10,11... | collective-permute-start | bytes 1032200 | tf_op jit(solution)/shard_map/ppermute | solution.py:27
  20.3 2.1 %collective-permute-start.2 = (bf16[6,224,128]{2,1,0:T(8,128)(2,1)S(1)}, bf16[6,224,128]{2,1,0:T(8,128)(2,1)S(1)}, u32[]{:S(2)}, u32[]{:S(2)}) collective-permute-start(bf16[6,224,128]{2,1,0:T(8,128)(2,1)S(1)} %get-tuple-element.54), channel_id=1, source_target_pairs={{0,1},{1,0},{2,3},{3,2},{4,5},{5,4},{6,7},{7,6},{8,9},{9,8},{10,11... | collective-permute-start | bytes 1032200 | tf_op jit(solution)/shard_map/ppermute | solution.py:27
  32.3 11.0 %collective-permute-start.8 = (bf16[6,224,128]{2,1,0:T(8,128)(2,1)S(1)}, bf16[6,224,128]{2,1,0:T(8,128)(2,1)S(1)}, u32[]{:S(2)}, u32[]{:S(2)}) collective-permute-start(bf16[6,224,128]{2,1,0:T(8,128)(2,1)S(1)} %get-tuple-element.56), channel_id=1, source_target_pairs={{0,8},{4,12},{8,0},{12,4},{16,24},{20,28},{24,16},{28,20},{1,9},{5... | collective-permute-start | bytes 1032200 | tf_op jit(solution)/shard_map/ppermute | solution.py:27
  34.1 11.0 %collective-permute-start.10 = (bf16[6,224,128]{2,1,0:T(8,128)(2,1)S(1)}, bf16[6,224,128]{2,1,0:T(8,128)(2,1)S(1)}, u32[]{:S(2)}, u32[]{:S(2)}) collective-permute-start(bf16[6,224,128]{2,1,0:T(8,128)(2,1)S(1)} %get-tuple-element.58), channel_id=1, source_target_pairs={{0,2},{1,3},{2,0},{3,1},{4,6},{5,7},{6,4},{7,5},{8,10},{9,11},{10,... | collective-permute-start | bytes 1032200 | tf_op jit(solution)/shard_map/ppermute | solution.py:27
  35.7 15.0 %collective-permute-start.7 = (bf16[6,224,128]{2,1,0:T(8,128)(2,1)S(1)}, bf16[6,224,128]{2,1,0:T(8,128)(2,1)S(1)}, u32[]{:S(2)}, u32[]{:S(2)}) collective-permute-start(bf16[6,224,128]{2,1,0:T(8,128)(2,1)S(1)} %get-tuple-element.58), channel_id=1, source_target_pairs={{0,8},{4,12},{8,0},{12,4},{16,24},{20,28},{24,16},{28,20},{1,9},{5... | collective-permute-start | bytes 1032200 | tf_op jit(solution)/shard_map/ppermute | solution.py:27
  36.1 16.4 %collective-permute-start.5 = (bf16[6,224,128]{2,1,0:T(8,128)(2,1)S(1)}, bf16[6,224,128]{2,1,0:T(8,128)(2,1)S(1)}, u32[]{:S(2)}, u32[]{:S(2)}) collective-permute-start(bf16[6,224,128]{2,1,0:T(8,128)(2,1)S(1)} %get-tuple-element.56), channel_id=1, source_target_pairs={{0,2},{1,3},{2,0},{3,1},{4,6},{5,7},{6,4},{7,5},{8,10},{9,11},{10,... | collective-permute-start | bytes 1032200 | tf_op jit(solution)/shard_map/ppermute | solution.py:27
  43.3 14.8 %collective-permute-start.9 = (bf16[6,224,128]{2,1,0:T(8,128)(2,1)S(1)}, bf16[6,224,128]{2,1,0:T(8,128)(2,1)S(1)}, u32[]{:S(2)}, u32[]{:S(2)}) collective-permute-start(bf16[6,224,128]{2,1,0:T(8,128)(2,1)S(1)} %collective-permute-done.8.refs_6_), channel_id=1, source_target_pairs={{0,2},{1,3},{2,0},{3,1},{4,6},{5,7},{6,4},{7,5},{8,10},{9,11},{10,... | collective-permute-start | bytes 1032200 | tf_op jit(solution)/shard_map/ppermute | solution.py:27
  45.1 12.9 %collective-permute-start.11 = (bf16[6,224,128]{2,1,0:T(8,128)(2,1)S(1)}, bf16[6,224,128]{2,1,0:T(8,128)(2,1)S(1)}, u32[]{:S(2)}, u32[]{:S(2)}) collective-permute-start(bf16[6,224,128]{2,1,0:T(8,128)(2,1)S(1)} %collective-permute-done.10.refs_3_), channel_id=1, source_target_pairs={{0,8},{4,12},{8,0},{12,4},{16,24},{20,28},{24,16},{28,20},{1,9},{5... | collective-permute-start | bytes 1032200 | tf_op jit(solution)/shard_map/ppermute | solution.py:27
  46.7 11.9 %collective-permute-start.14 = (bf16[6,224,128]{2,1,0:T(8,128)(2,1)S(1)}, bf16[6,224,128]{2,1,0:T(8,128)(2,1)S(1)}, u32[]{:S(2)}, u32[]{:S(2)}) collective-permute-start(bf16[6,224,128]{2,1,0:T(8,128)(2,1)S(1)} %collective-permute-done.8.refs_6_), channel_id=1, source_target_pairs={{0,1},{1,0},{2,3},{3,2},{4,5},{5,4},{6,7},{7,6},{8,9},{9,8},{10,11... | collective-permute-start | bytes 1032200 | tf_op jit(solution)/shard_map/ppermute | solution.py:27
  50.7 8.4 %collective-permute-start.4 = (bf16[12,224,128]{2,1,0:T(8,128)(2,1)S(1)}, bf16[12,224,128]{2,1,0:T(8,128)(2,1)S(1)}, u32[]{:S(2)}, u32[]{:S(2)}) collective-permute-start(bf16[12,224,128]{2,1,0:T(8,128)(2,1)S(1)} %get-tuple-element.55.refs_1_.refs_0_), channel_id=1, source_target_pairs={{0,1},{1,0},{2,3},{3,2},{4,5},{5,4},{6,7},{7,6},{8,9},{9,8},{10,11... | collective-permute-start | bytes 2064392 | tf_op jit(solution)/shard_map/ppermute | solution.py:27
  52.5 6.1 %collective-permute-start.13 = (bf16[6,224,128]{2,1,0:T(8,128)(2,1)S(1)}, bf16[6,224,128]{2,1,0:T(8,128)(2,1)S(1)}, u32[]{:S(2)}, u32[]{:S(2)}) collective-permute-start(bf16[6,224,128]{2,1,0:T(8,128)(2,1)S(1)} %collective-permute-done.10.refs_3_), channel_id=1, source_target_pairs={{0,1},{1,0},{2,3},{3,2},{4,5},{5,4},{6,7},{7,6},{8,9},{9,8},{10,11... | collective-permute-start | bytes 1032200 | tf_op jit(solution)/shard_map/ppermute | solution.py:27
  58.1 1.7 %collective-permute-start.12 = (bf16[6,224,128]{2,1,0:T(8,128)(2,1)S(1)}, bf16[6,224,128]{2,1,0:T(8,128)(2,1)S(1)}, u32[]{:S(2)}, u32[]{:S(2)}) collective-permute-start(bf16[6,224,128]{2,1,0:T(8,128)(2,1)S(1)} %collective-permute-done.5.refs_2_), channel_id=1, source_target_pairs={{0,1},{1,0},{2,3},{3,2},{4,5},{5,4},{6,7},{7,6},{8,9},{9,8},{10,11... | collective-permute-start | bytes 1032200 | tf_op jit(solution)/shard_map/ppermute | solution.py:27
  58.1 2.1 %collective-permute-start.15 = (bf16[6,224,128]{2,1,0:T(8,128)(2,1)S(1)}, bf16[6,224,128]{2,1,0:T(8,128)(2,1)S(1)}, u32[]{:S(2)}, u32[]{:S(2)}) collective-permute-start(bf16[6,224,128]{2,1,0:T(8,128)(2,1)S(1)} %collective-permute-done.7.refs_7_), channel_id=1, source_target_pairs={{0,1},{1,0},{2,3},{3,2},{4,5},{5,4},{6,7},{7,6},{8,9},{9,8},{10,11... | collective-permute-start | bytes 1032200 | tf_op jit(solution)/shard_map/ppermute | solution.py:27
  58.6 2.1 %collective-permute-start.16 = (bf16[6,224,128]{2,1,0:T(8,128)(2,1)S(1)}, bf16[6,224,128]{2,1,0:T(8,128)(2,1)S(1)}, u32[]{:S(2)}, u32[]{:S(2)}) collective-permute-start(bf16[6,224,128]{2,1,0:T(8,128)(2,1)S(1)} %collective-permute-done.9.refs_10_), channel_id=1, source_target_pairs={{0,1},{1,0},{2,3},{3,2},{4,5},{5,4},{6,7},{7,6},{8,9},{9,8},{10,11... | collective-permute-start | bytes 1032200 | tf_op jit(solution)/shard_map/ppermute | solution.py:27
  58.6 2.6 %collective-permute-start.17 = (bf16[6,224,128]{2,1,0:T(8,128)(2,1)S(1)}, bf16[6,224,128]{2,1,0:T(8,128)(2,1)S(1)}, u32[]{:S(2)}, u32[]{:S(2)}) collective-permute-start(bf16[6,224,128]{2,1,0:T(8,128)(2,1)S(1)} %collective-permute-done.11.refs_11_), channel_id=1, source_target_pairs={{0,1},{1,0},{2,3},{3,2},{4,5},{5,4},{6,7},{7,6},{8,9},{9,8},{10,11... | collective-permute-start | bytes 1032200 | tf_op jit(solution)/shard_map/ppermute | solution.py:27
  64.7 7.8 %collective-permute-start.18 = (bf16[2,2,192,128]{3,2,1,0:T(8,128)(2,1)S(1)}, bf16[2,2,192,128]{3,2,1,0:T(8,128)(2,1)S(1)}, u32[]{:S(2)}, u32[]{:S(2)}) collective-permute-start(bf16[2,2,192,128]{3,2,1,0:T(8,128)(2,1)S(1)} %get-tuple-element.70), channel_id=1, source_target_pairs={{0,4},{4,0},{8,12},{12,8},{16,20},{20,16},{24,28},{28,24},{1,5},{5... | collective-permute-start | bytes 589832 | tf_op jit(solution)/shard_map/ppermute | solution.py:27
  67.7 15.4 %collective-permute-start.21 = (bf16[2,5,192,128]{3,2,1,0:T(8,128)(2,1)S(1)}, bf16[2,5,192,128]{3,2,1,0:T(8,128)(2,1)S(1)}, u32[]{:S(2)}, u32[]{:S(2)}) collective-permute-start(bf16[2,5,192,128]{3,2,1,0:T(8,128)(2,1)S(1)} %get-tuple-element.74), channel_id=1, source_target_pairs={{0,4},{4,0},{8,12},{12,8},{16,20},{20,16},{24,28},{28,24},{1,5},{5... | collective-permute-start | bytes 1474568 | tf_op jit(solution)/shard_map/ppermute | solution.py:27
  72.5 8.8 %collective-permute-start.20 = (bf16[2,192,128]{2,1,0:T(8,128)(2,1)S(1)}, bf16[2,192,128]{2,1,0:T(8,128)(2,1)S(1)}, u32[]{:S(2)}, u32[]{:S(2)}) collective-permute-start(bf16[2,192,128]{2,1,0:T(8,128)(2,1)S(1)} %get-tuple-element.94.refs_0_), channel_id=1, source_target_pairs={{0,16},{4,20},{8,24},{12,28},{16,0},{20,4},{24,8},{28,12},{1,17},{... | collective-permute-start | bytes 294920 | tf_op jit(solution)/shard_map/ppermute | solution.py:27
  77.4 23.9 %collective-permute-start.25 = (bf16[12,192,128]{2,1,0:T(8,128)(2,1)S(1)}, bf16[12,192,128]{2,1,0:T(8,128)(2,1)S(1)}, u32[]{:S(2)}, u32[]{:S(2)}) collective-permute-start(bf16[12,192,128]{2,1,0:T(8,128)(2,1)S(1)} %get-tuple-element.87), channel_id=1, source_target_pairs={{0,4},{4,0},{8,12},{12,8},{16,20},{20,16},{24,28},{28,24},{1,5},{5... | collective-permute-start | bytes 1769480 | tf_op jit(solution)/shard_map/ppermute | solution.py:27
  79.0 6.8 %collective-permute-start.19 = (bf16[2,192,128]{2,1,0:T(8,128)(2,1)S(1)}, bf16[2,192,128]{2,1,0:T(8,128)(2,1)S(1)}, u32[]{:S(2)}, u32[]{:S(2)}) collective-permute-start(bf16[2,192,128]{2,1,0:T(8,128)(2,1)S(1)} %get-tuple-element.95.refs_1_), channel_id=1, source_target_pairs={{0,24},{4,28},{8,16},{12,20},{16,8},{20,12},{24,0},{28,4},{1,25},{... | collective-permute-start | bytes 294920 | tf_op jit(solution)/shard_map/ppermute | solution.py:27
  80.6 25.6 %collective-permute-start.24 = (bf16[2,5,192,128]{3,2,1,0:T(8,128)(2,1)S(1)}, bf16[2,5,192,128]{3,2,1,0:T(8,128)(2,1)S(1)}, u32[]{:S(2)}, u32[]{:S(2)}) collective-permute-start(bf16[2,5,192,128]{3,2,1,0:T(8,128)(2,1)S(1)} %get-tuple-element.83), channel_id=1, source_target_pairs={{0,4},{4,0},{8,12},{12,8},{16,20},{20,16},{24,28},{28,24},{1,5},{5... | collective-permute-start | bytes 1474568 | tf_op jit(solution)/shard_map/ppermute | solution.py:27
  83.1 18.2 %collective-permute-start.22 = (bf16[5,192,128]{2,1,0:T(8,128)(2,1)S(1)}, bf16[5,192,128]{2,1,0:T(8,128)(2,1)S(1)}, u32[]{:S(2)}, u32[]{:S(2)}) collective-permute-start(bf16[5,192,128]{2,1,0:T(8,128)(2,1)S(1)} %fusion.3.refs_6_), channel_id=1, source_target_pairs={{0,16},{4,20},{8,24},{12,28},{16,0},{20,4},{24,8},{28,12},{1,17},{... | collective-permute-start | bytes 737288 | tf_op jit(solution)/shard_map/ppermute | solution.py:27
  85.8 23.1 %collective-permute-start.23 = (bf16[5,192,128]{2,1,0:T(8,128)(2,1)S(1)}, bf16[5,192,128]{2,1,0:T(8,128)(2,1)S(1)}, u32[]{:S(2)}, u32[]{:S(2)}) collective-permute-start(bf16[5,192,128]{2,1,0:T(8,128)(2,1)S(1)} %fusion.2.refs_7_), channel_id=1, source_target_pairs={{0,24},{4,28},{8,16},{12,20},{16,8},{20,12},{24,0},{28,4},{1,25},{... | collective-permute-start | bytes 737288 | tf_op jit(solution)/shard_map/ppermute | solution.py:27
  86.1 37.5 %collective-permute-start.26 = (bf16[12,192,128]{2,1,0:T(8,128)(2,1)S(1)}, bf16[12,192,128]{2,1,0:T(8,128)(2,1)S(1)}, u32[]{:S(2)}, u32[]{:S(2)}) collective-permute-start(bf16[12,192,128]{2,1,0:T(8,128)(2,1)S(1)} %get-tuple-element.89), channel_id=1, source_target_pairs={{0,4},{4,0},{8,12},{12,8},{16,20},{20,16},{24,28},{28,24},{1,5},{5... | collective-permute-start | bytes 1769480 | tf_op jit(solution)/shard_map/ppermute | solution.py:27
  101.4 25.8 %collective-permute-start.27 = (bf16[12,192,128]{2,1,0:T(8,128)(2,1)S(1)}, bf16[12,192,128]{2,1,0:T(8,128)(2,1)S(1)}, u32[]{:S(2)}, u32[]{:S(2)}) collective-permute-start(bf16[12,192,128]{2,1,0:T(8,128)(2,1)S(1)} %add_convert_fusion.1.refs_10_), channel_id=1, source_target_pairs={{0,8},{4,12},{8,0},{12,4},{16,24},{20,28},{24,16},{28,20},{1,9},{5... | collective-permute-start | bytes 1769480 | tf_op jit(solution)/shard_map/ppermute | solution.py:27
  106.3 17.4 %collective-permute-start.28 = (bf16[5,192,128]{2,1,0:T(8,128)(2,1)S(1)}, bf16[5,192,128]{2,1,0:T(8,128)(2,1)S(1)}, u32[]{:S(2)}, u32[]{:S(2)}) collective-permute-start(bf16[5,192,128]{2,1,0:T(8,128)(2,1)S(1)} %fusion.1.refs_8_), channel_id=1, source_target_pairs={{0,16},{4,20},{8,24},{12,28},{16,0},{20,4},{24,8},{28,12},{1,17},{... | collective-permute-start | bytes 737288 | tf_op jit(solution)/shard_map/ppermute | solution.py:27
  109.0 17.7 %collective-permute-start.29 = (bf16[5,192,128]{2,1,0:T(8,128)(2,1)S(1)}, bf16[5,192,128]{2,1,0:T(8,128)(2,1)S(1)}, u32[]{:S(2)}, u32[]{:S(2)}) collective-permute-start(bf16[5,192,128]{2,1,0:T(8,128)(2,1)S(1)} %fusion.refs_9_), channel_id=1, source_target_pairs={{0,24},{4,28},{8,16},{12,20},{16,8},{20,12},{24,0},{28,4},{1,25},{... | collective-permute-start | bytes 737288 | tf_op jit(solution)/shard_map/ppermute | solution.py:27

commit v3 on v2

--- a/solution.py
+++ b/solution.py
@@ -186,8 +186,26 @@
         n = ref.shape[0]
         copies.append(pltpu.make_async_copy(ref, held.at[pl.ds(at, n)], sems.at[i]))
         at += n
-    for i, c in enumerate(copies):
-        c.start(priority=i % 2)
+    for c in copies:
+        c.start()
+    for c in copies:
+        c.wait()
+
+
+COPIED = 2
+
+
+def place_pieces(pieces, held, sems):
+    copies = []
+    at = 0
+    for i, ref in enumerate(pieces):
+        here = pl.ds(at, ref.shape[0])
+        at += ref.shape[0]
+        if i < COPIED:
+            copies.append(pltpu.make_async_copy(ref, held.at[here], sems.at[i]))
+            copies[-1].start()
+        else:
+            held[here] = ref[...]
     for c in copies:
         c.wait()
 
@@ -268,7 +286,7 @@
 
 def first_grads(slots, flips, lo, hi, n_pieces, cols_ref, xt_ref, xt2_ref, *refs):
     pieces, outs, (held, sems) = refs[:n_pieces], refs[n_pieces:-2], refs[-2:]
-    load_pieces(pieces, held, sems)
+    place_pieces(pieces, held, sems)
     n = len(outs) - len(flips)
     block_grads(slots, flips, lo, hi, cols_ref, xt_ref, xt2_ref, held, outs[:n], outs[n:])
 
@@ -291,10 +309,12 @@
     shapes = grad_shapes(flips, lo, hi, True) + [jax.ShapeDtypeStruct((8 * slots, tokens, 128), bf16)]
     return pl.pallas_call(
         functools.partial(first_grads, slots, flips, lo, hi, n),
-        in_specs=[pl.BlockSpec(memory_space=pltpu.SMEM), whole(), whole()] + [anywhere()] * n,
+        in_specs=[pl.BlockSpec(memory_space=pltpu.SMEM), whole(), whole()]
+        + [anywhere()] * COPIED
+        + [whole()] * (n - COPIED),
         out_specs=[whole()] * len(shapes),
         out_shape=shapes,
-        scratch_shapes=[pltpu.SemaphoreType.DMA((n,))],
+        scratch_shapes=[pltpu.SemaphoreType.DMA((COPIED,))],
         compiler_params=pltpu.CompilerParams(vmem_limit_bytes=20 * 2**20),
         cost_estimate=SHORT,
         name="first_grads",
@@ -391,26 +411,33 @@
     )(*args)
 
 
-def last_sum(scale, base_ref, near_ref, mine_ref, other_ref, out_ref):
-    n, half = mine_ref.shape[0], near_ref.shape[0]
-    near = near_ref[...].astype(f32)
-    mine = jnp.concatenate([mine_ref[...].astype(f32), jnp.zeros_like(near[n:])], axis=0)
-    other = jnp.concatenate([near[:n] + other_ref[...].astype(f32), near[n:]], axis=0)
-    late = jnp.concatenate(by_rows(mine, other), axis=0) * scale
-    out_ref[...] = base_ref[...] + jnp.swapaxes(late, 0, 1)
+def last_sum(scale, base_ref, near_ref, mine_ref, other_ref, out_ref, parts, sems):
+    n = mine_ref.shape[0]
+    size = parts.shape[1]
+    copies = []
+    for i in range(parts.shape[0]):
+        here = slice(i * size, (i + 1) * size)
+        near = near_ref[:, here].astype(f32)
+        mine = jnp.concatenate([mine_ref[:, here].astype(f32), jnp.zeros_like(near[n:])], axis=0)
+        other = jnp.concatenate([near[:n] + other_ref[:, here].astype(f32), near[n:]], axis=0)
+        late = jnp.concatenate(by_rows(mine, other), axis=0) * scale
+        parts[i] = base_ref[here] + jnp.swapaxes(late, 0, 1)
+        copies.append(pltpu.make_async_copy(parts.at[i], out_ref.at[pl.ds(i * size, size)], sems.at[i]))
+        copies[-1].start()
+    for copy in copies:
+        copy.wait()
 
 
 def run_last_sum(scale, base, near, mine, other):
-    rows = base.shape[1]
-    tile = pl.BlockSpec((48, rows, 128), lambda i: (i, 0, 0))
-    late = [pl.BlockSpec((a.shape[0], 48, 128), lambda i: (0, i, 0)) for a in (near, mine, other)]
+    count = 6
+    size, rows = base.shape[0] // count, base.shape[1]
     return pl.pallas_call(
         functools.partial(last_sum, scale),
-        grid=(4,),
-        in_specs=[tile, *late],
-        out_specs=tile,
+        in_specs=[whole()] * 4,
+        out_specs=anywhere(),
         out_shape=jax.ShapeDtypeStruct(base.shape, f32),
-        compiler_params=pltpu.CompilerParams(vmem_limit_bytes=8 * 2**20),
+        scratch_shapes=[pltpu.VMEM((count, size, rows, 128), f32), pltpu.SemaphoreType.DMA((count,))],
+        compiler_params=pltpu.CompilerParams(vmem_limit_bytes=12 * 2**20),
         cost_estimate=SHORT,
         name="last_sum",
     )(base, near, mine, other)

time: 130 us -> 128 us (0.985)
  Pallas kernels: 42 us -> 39.9 us
    pallas_call x1, Pallas kernels: 3.47 us -> 2.14 us  [run_first_grads(): pl.pallas_call(functools.partial(first_grads, slots, flips, lo, hi, n), i...]
  transfers between devices with their start and end apart: 30 -> 30, of which waited for: 19 -> 18; matrix products, arithmetic and copies ran while one was open for 0% -> 0% of each run, Pallas kernels for 21% -> 21%
where the time goes in v3:
time: 128 us
  waiting for transfers between devices  56.8 us (44%)
  Pallas kernels  39.9 us (31%)
  starting transfers between devices  29.2 us (23%)
    ppermute x30, waiting for transfers between devices, swap(): return lax.ppermute(value, axis, [(i, i ^ bit) for i in range(count)])  56.8 us
    ppermute x30, starting transfers between devices, swap(): return lax.ppermute(value, axis, [(i, i ^ bit) for i in range(count)])  29.2 us
    pallas_call x1, Pallas kernels, run_input_grads(): pl.pallas_call(functools.partial(input_grads, slots, len(pieces)), grid_s...  14.3 us
    pallas_call x1, Pallas kernels, run_turn_weights(): pl.pallas_call(functools.partial(turn_weights, slots, rows), in_specs=[an...  6.52 us
    pallas_call x3, Pallas kernels, run_more_grads(): pl.pallas_call(functools.partial(more_grads, slots, flips, lo, hi, len(af...  5.08 us
    pallas_call x2, Pallas kernels, run_forward_more(): pl.pallas_call(functools.partial(forward_more, slots, width // 512, [w[:2...  4.97 us
    pallas_call x1, Pallas kernels, run_forward_first(): pl.pallas_call(functools.partial(forward_first, slots, rows // 4), in_spe...  2.76 us
  transfers between devices with their start and end apart: 30, of which 18 were waited for; matrix products, arithmetic and copies ran while one was open for 0% of the time, Pallas kernels for 21%

profile of v3, /device:TPU:0, one launch (start us, length us, event | category | flops | bytes accessed | tf_op | source)
XLA Modules:
  0.0 127.6 jit_solution(14371135040045985537)
XLA Ops:
  0.6 6.5 %turn_weights.1.w_ref = bf16[288,128,128]{2,1,0:T(8,128)(2,1)S(1)} custom-call(bf16[12,128,24,128]{3,2,1,0:T(8,128)(2,1)} %bitcast.40), custom_call_target="tpu_custom_call" | custom-call | flops 1000 | bytes 1000 | tf_op jit(solution)/shard_map/turn_weights/pallas_call | solution.py:86
  7.2 2.8 %forward_first.1 = (bf16[12,224,128]{2,1,0:T(8,128)(2,1)S(1)}, s32[288]{0:T(512)S(1)}) custom-call(s32[12,24]{1,0:T(8,128)S(1)} %bitcast.34, bf16[288,128,128]{2,1,0:T(8,128)(2,1)S(1)} %turn_weights.1.w_ref, bf16[224,3072]{1,0:T(8,128)(2,1)S(1)} %copy-done), custom_call_target="tpu_custom_call" | custom-call | flops 1000 | bytes 1000 | tf_op jit(solution)/shard_map/forward_first/pallas_call | solution.py:121
  10.0 0.5 collective-permute-start
  10.5 1.9 %forward_more.2 = f32[12,224,128]{2,1,0:T(8,128)S(1)} custom-call(s32[288]{0:T(512)S(1)} %get-tuple-element.48.entry_ref, bf16[288,128,128]{2,1,0:T(8,128)(2,1)S(1)} %turn_weights.1.w_ref, bf16[224,3072]{1,0:T(8,128)(2,1)S(1)} %copy-done), custom_call_target="tpu_custom_call" | custom-call | flops 1000 | bytes 1000 | tf_op jit(solution)/shard_map/forward_more/pallas_call | solution.py:138
  12.4 0.2 add_convert_fusion.refs_0_
  12.6 2.8 %collective-permute-start.3 = (bf16[12,224,128]{2,1,0:T(8,128)(2,1)S(1)}, bf16[12,224,128]{2,1,0:T(8,128)(2,1)S(1)}, u32[]{:S(2)}, u32[]{:S(2)}) collective-permute-start(bf16[12,224,128]{2,1,0:T(8,128)(2,1)S(1)} %add_convert_fusion.refs_0_), channel_id=1, source_target_pairs={{0,2},{1,3},{2,0},{3,1},{4,6},{5,7},{6,4},{7,5},{8,10},{9,11},{10,... | collective-permute-start | bytes 2064392 | tf_op jit(solution)/shard_map/ppermute | solution.py:27
  15.4 0.1 partner_features.1
  15.5 1.6 %collective-permute-start.6 = (bf16[224,1536]{1,0:T(8,128)(2,1)S(1)}, bf16[224,1536]{1,0:T(8,128)(2,1)S(1)}, u32[]{:S(2)}, u32[]{:S(2)}) collective-permute-start(bf16[224,1536]{1,0:T(8,128)(2,1)S(1)} %partner_features.1), channel_id=1, source_target_pairs={{0,8},{4,12},{8,0},{12,4},{16,24},{20,28},{24,16},{28,20},{1,9},{5... | collective-permute-start | bytes 2064392 | tf_op jit(solution)/shard_map/ppermute | solution.py:27
  17.1 3.1 %forward_more.3 = (bf16[6,224,128]{2,1,0:T(8,128)(2,1)S(1)}, bf16[6,224,128]{2,1,0:T(8,128)(2,1)S(1)}, f32[12,224,128]{2,1,0:T(8,128)S(1)}) custom-call(s32[288]{0:T(512)S(1)} %get-tuple-element.48.entry_ref, bf16[288,128,128]{2,1,0:T(8,128)(2,1)S(1)} %turn_weights.1.w_ref, bf16[224,3072]{1,0:T(8,128)(2,1)S(1)} %copy-done, ...), custom_call_target="tpu_custom_call" | custom-call | flops 1000 | bytes 1000 | tf_op jit(solution)/shard_map/forward_more/pallas_call | solution.py:138
  20.2 0.1 collective-permute-start.1
  20.3 0.5 collective-permute-start.2
  20.8 1.1 collective-permute-done.1.near_lo_ref
  21.9 0.5 collective-permute-done.2.near_hi_ref
  22.4 8.9 %collective-permute-done.3.across_ref = bf16[12,224,128]{2,1,0:T(8,128)(2,1)S(1)} collective-permute-done((bf16[12,224,128]{2,1,0:T(8,128)(2,1)S(1)}, bf16[12,224,128]{2,1,0:T(8,128)(2,1)S(1)}, u32[]{:S(2)}, u32[]{:S(2)}) %collective-permute-start.3) | collective-permute-done | bytes 688160 | tf_op jit(solution)/shard_map/ppermute | solution.py:27
  31.3 1.0 own_slope.1
  32.3 1.9 %collective-permute-start.8 = (bf16[6,224,128]{2,1,0:T(8,128)(2,1)S(1)}, bf16[6,224,128]{2,1,0:T(8,128)(2,1)S(1)}, u32[]{:S(2)}, u32[]{:S(2)}) collective-permute-start(bf16[6,224,128]{2,1,0:T(8,128)(2,1)S(1)} %get-tuple-element.56), channel_id=1, source_target_pairs={{0,8},{4,12},{8,0},{12,4},{16,24},{20,28},{24,16},{28,20},{1,9},{5... | collective-permute-start | bytes 1032200 | tf_op jit(solution)/shard_map/ppermute | solution.py:27
  34.1 1.5 %collective-permute-start.10 = (bf16[6,224,128]{2,1,0:T(8,128)(2,1)S(1)}, bf16[6,224,128]{2,1,0:T(8,128)(2,1)S(1)}, u32[]{:S(2)}, u32[]{:S(2)}) collective-permute-start(bf16[6,224,128]{2,1,0:T(8,128)(2,1)S(1)} %get-tuple-element.58), channel_id=1, source_target_pairs={{0,2},{1,3},{2,0},{3,1},{4,6},{5,7},{6,4},{7,5},{8,10},{9,11},{10,... | collective-permute-start | bytes 1032200 | tf_op jit(solution)/shard_map/ppermute | solution.py:27
  35.7 0.4 collective-permute-start.7
  36.1 0.3 collective-permute-start.5
  36.4 0.3 turn_features.2.xt_ref
  36.7 0.3 turn_features.3.xt2_ref
  37.0 6.3 %collective-permute-done.8.refs_6_ = bf16[6,224,128]{2,1,0:T(8,128)(2,1)S(1)} collective-permute-done((bf16[6,224,128]{2,1,0:T(8,128)(2,1)S(1)}, bf16[6,224,128]{2,1,0:T(8,128)(2,1)S(1)}, u32[]{:S(2)}, u32[]{:S(2)}) %collective-permute-start.8) | collective-permute-done | bytes 344096 | tf_op jit(solution)/shard_map/ppermute | solution.py:27
  43.3 1.8 %collective-permute-start.9 = (bf16[6,224,128]{2,1,0:T(8,128)(2,1)S(1)}, bf16[6,224,128]{2,1,0:T(8,128)(2,1)S(1)}, u32[]{:S(2)}, u32[]{:S(2)}) collective-permute-start(bf16[6,224,128]{2,1,0:T(8,128)(2,1)S(1)} %collective-permute-done.8.refs_6_), channel_id=1, source_target_pairs={{0,2},{1,3},{2,0},{3,1},{4,6},{5,7},{6,4},{7,5},{8,10},{9,11},{10,... | collective-permute-start | bytes 1032200 | tf_op jit(solution)/shard_map/ppermute | solution.py:27
  45.1 0.1 collective-permute-done.10.refs_3_
  45.1 1.5 %collective-permute-start.11 = (bf16[6,224,128]{2,1,0:T(8,128)(2,1)S(1)}, bf16[6,224,128]{2,1,0:T(8,128)(2,1)S(1)}, u32[]{:S(2)}, u32[]{:S(2)}) collective-permute-start(bf16[6,224,128]{2,1,0:T(8,128)(2,1)S(1)} %collective-permute-done.10.refs_3_), channel_id=1, source_target_pairs={{0,8},{4,12},{8,0},{12,4},{16,24},{20,28},{24,16},{28,20},{1,9},{5... | collective-permute-start | bytes 1032200 | tf_op jit(solution)/shard_map/ppermute | solution.py:27
  46.7 4.0 %collective-permute-done.7.refs_7_ = bf16[6,224,128]{2,1,0:T(8,128)(2,1)S(1)} collective-permute-done((bf16[6,224,128]{2,1,0:T(8,128)(2,1)S(1)}, bf16[6,224,128]{2,1,0:T(8,128)(2,1)S(1)}, u32[]{:S(2)}, u32[]{:S(2)}) %collective-permute-start.7) | collective-permute-done | bytes 344096 | tf_op jit(solution)/shard_map/ppermute | solution.py:27
  50.7 1.8 %collective-permute-done.5.refs_2_ = bf16[6,224,128]{2,1,0:T(8,128)(2,1)S(1)} collective-permute-done((bf16[6,224,128]{2,1,0:T(8,128)(2,1)S(1)}, bf16[6,224,128]{2,1,0:T(8,128)(2,1)S(1)}, u32[]{:S(2)}, u32[]{:S(2)}) %collective-permute-start.5) | collective-permute-done | bytes 344096 | tf_op jit(solution)/shard_map/ppermute | solution.py:27
  52.5 5.5 %collective-permute-done.9.refs_10_ = bf16[6,224,128]{2,1,0:T(8,128)(2,1)S(1)} collective-permute-done((bf16[6,224,128]{2,1,0:T(8,128)(2,1)S(1)}, bf16[6,224,128]{2,1,0:T(8,128)(2,1)S(1)}, u32[]{:S(2)}, u32[]{:S(2)}) %collective-permute-start.9) | collective-permute-done | bytes 344096 | tf_op jit(solution)/shard_map/ppermute | solution.py:27
  58.0 0.5 collective-permute-start.15
  58.6 0.5 collective-permute-start.17
  59.1 0.6 collective-permute-done.12.refs_4_
  59.7 0.5 collective-permute-done.15.refs_9_
  60.2 0.5 collective-permute-done.16.refs_12_
  60.7 0.5 collective-permute-done.17.refs_13_
  61.2 2.1 %first_grads.1 = (bf16[2,2,192,128]{3,2,1,0:T(8,128)(2,1)S(1)}, f32[2,192,128]{2,1,0:T(8,128)S(1)}, f32[2,192,128]{2,1,0:T(8,128)S(1)}, bf16[96,224,128]{2,1,0:T(8,128)(2,1)S(1)}) custom-call(s32[12,24]{1,0:T(8,128)S(1)} %bitcast.35, bf16[12,128,224]{2,1,0:T(8,128)(2,1)S(1)} %turn_features.2.xt_ref, bf16[12,128,224]{2,1,0:T(8,128)(2,1)S(1)} %turn_features.3.xt2_ref, ...), custom_call_target="tpu_custom_call" | custom-call | flops 1000 | bytes 1000 | tf_op jit(solution)/shard_map/first_grads/pallas_call | solution.py:310
  63.3 1.6 %collective-permute-start.18 = (bf16[2,2,192,128]{3,2,1,0:T(8,128)(2,1)S(1)}, bf16[2,2,192,128]{3,2,1,0:T(8,128)(2,1)S(1)}, u32[]{:S(2)}, u32[]{:S(2)}) collective-permute-start(bf16[2,2,192,128]{3,2,1,0:T(8,128)(2,1)S(1)} %get-tuple-element.70), channel_id=1, source_target_pairs={{0,4},{4,0},{8,12},{12,8},{16,20},{20,16},{24,28},{28,24},{1,5},{5... | collective-permute-start | bytes 589832 | tf_op jit(solution)/shard_map/ppermute | solution.py:27
  64.9 1.4 %more_grads.3 = (bf16[2,5,192,128]{3,2,1,0:T(8,128)(2,1)S(1)}, f32[5,192,128]{2,1,0:T(8,128)S(1)}, f32[5,192,128]{2,1,0:T(8,128)S(1)}) custom-call(s32[12,24]{1,0:T(8,128)S(1)} %bitcast.36, bf16[12,128,224]{2,1,0:T(8,128)(2,1)S(1)} %turn_features.2.xt_ref, bf16[12,128,224]{2,1,0:T(8,128)(2,1)S(1)} %turn_features.3.xt2_ref, ...), custom_call_target="tpu_custom_call" | custom-call | flops 1000 | bytes 1000 | tf_op jit(solution)/shard_map/more_grads/pallas_call | solution.py:327
  66.3 0.6 collective-permute-start.21
  66.9 4.2 %collective-permute-done.18 = bf16[2,2,192,128]{3,2,1,0:T(8,128)(2,1)S(1)} collective-permute-done((bf16[2,2,192,128]{3,2,1,0:T(8,128)(2,1)S(1)}, bf16[2,2,192,128]{3,2,1,0:T(8,128)(2,1)S(1)}, u32[]{:S(2)}, u32[]{:S(2)}) %collective-permute-start.18) | collective-permute-done | bytes 196640 | tf_op jit(solution)/shard_map/ppermute | solution.py:27
  71.2 2.7 %collective-permute-start.20 = (bf16[2,192,128]{2,1,0:T(8,128)(2,1)S(1)}, bf16[2,192,128]{2,1,0:T(8,128)(2,1)S(1)}, u32[]{:S(2)}, u32[]{:S(2)}) collective-permute-start(bf16[2,192,128]{2,1,0:T(8,128)(2,1)S(1)} %get-tuple-element.94.refs_0_), channel_id=1, source_target_pairs={{0,16},{4,20},{8,24},{12,28},{16,0},{20,4},{24,8},{28,12},{1,17},{... | collective-permute-start | bytes 294920 | tf_op jit(solution)/shard_map/ppermute | solution.py:27
  73.8 2.2 %more_grads.4 = (bf16[12,192,128]{2,1,0:T(8,128)(2,1)S(1)}, bf16[12,192,128]{2,1,0:T(8,128)(2,1)S(1)}, f32[12,192,128]{2,1,0:T(8,128)S(1)}, f32[12,192,128]{2,1,0:T(8,128)S(1)}) custom-call(s32[12,24]{1,0:T(8,128)S(1)} %bitcast.37, bf16[12,128,224]{2,1,0:T(8,128)(2,1)S(1)} %turn_features.2.xt_ref, bf16[12,128,224]{2,1,0:T(8,128)(2,1)S(1)} %turn_features.3.xt2_ref, ...), custom_call_target="tpu_custom_call" | custom-call | flops 1000 | bytes 1000 | tf_op jit(solution)/shard_map/more_grads/pallas_call | solution.py:327
  76.1 1.6 %collective-permute-start.25 = (bf16[12,192,128]{2,1,0:T(8,128)(2,1)S(1)}, bf16[12,192,128]{2,1,0:T(8,128)(2,1)S(1)}, u32[]{:S(2)}, u32[]{:S(2)}) collective-permute-start(bf16[12,192,128]{2,1,0:T(8,128)(2,1)S(1)} %get-tuple-element.87), channel_id=1, source_target_pairs={{0,4},{4,0},{8,12},{12,8},{16,20},{20,16},{24,28},{28,24},{1,5},{5... | collective-permute-start | bytes 1769480 | tf_op jit(solution)/shard_map/ppermute | solution.py:27
  77.6 0.2 collective-permute-start.19
  77.8 1.4 %more_grads.5 = (bf16[2,5,192,128]{3,2,1,0:T(8,128)(2,1)S(1)}, f32[5,192,128]{2,1,0:T(8,128)S(1)}, f32[5,192,128]{2,1,0:T(8,128)S(1)}) custom-call(s32[12,24]{1,0:T(8,128)S(1)} %bitcast.38, bf16[12,128,224]{2,1,0:T(8,128)(2,1)S(1)} %turn_features.2.xt_ref, bf16[12,128,224]{2,1,0:T(8,128)(2,1)S(1)} %turn_features.3.xt2_ref, ...), custom_call_target="tpu_custom_call" | custom-call | flops 1000 | bytes 1000 | tf_op jit(solution)/shard_map/more_grads/pallas_call | solution.py:327
  79.3 0.7 collective-permute-start.24
  80.0 1.7 %collective-permute-done.21 = bf16[2,5,192,128]{3,2,1,0:T(8,128)(2,1)S(1)} collective-permute-done((bf16[2,5,192,128]{3,2,1,0:T(8,128)(2,1)S(1)}, bf16[2,5,192,128]{3,2,1,0:T(8,128)(2,1)S(1)}, u32[]{:S(2)}, u32[]{:S(2)}) %collective-permute-start.21) | collective-permute-done | bytes 491552 | tf_op jit(solution)/shard_map/ppermute | solution.py:27
  81.7 0.1 fusion.3.refs_6_
  81.7 2.7 %collective-permute-start.22 = (bf16[5,192,128]{2,1,0:T(8,128)(2,1)S(1)}, bf16[5,192,128]{2,1,0:T(8,128)(2,1)S(1)}, u32[]{:S(2)}, u32[]{:S(2)}) collective-permute-start(bf16[5,192,128]{2,1,0:T(8,128)(2,1)S(1)} %fusion.3.refs_6_), channel_id=1, source_target_pairs={{0,16},{4,20},{8,24},{12,28},{16,0},{20,4},{24,8},{28,12},{1,17},{... | collective-permute-start | bytes 737288 | tf_op jit(solution)/shard_map/ppermute | solution.py:27
  84.4 0.1 fusion.2.refs_7_
  84.5 0.3 collective-permute-start.23
  84.8 1.4 %collective-permute-start.26 = (bf16[12,192,128]{2,1,0:T(8,128)(2,1)S(1)}, bf16[12,192,128]{2,1,0:T(8,128)(2,1)S(1)}, u32[]{:S(2)}, u32[]{:S(2)}) collective-permute-start(bf16[12,192,128]{2,1,0:T(8,128)(2,1)S(1)} %get-tuple-element.89), channel_id=1, source_target_pairs={{0,4},{4,0},{8,12},{12,8},{16,20},{20,16},{24,28},{28,24},{1,5},{5... | collective-permute-start | bytes 1769480 | tf_op jit(solution)/shard_map/ppermute | solution.py:27
  86.2 13.7 %collective-permute-done.22.refs_0_ = bf16[5,192,128]{2,1,0:T(8,128)(2,1)S(1)} collective-permute-done((bf16[5,192,128]{2,1,0:T(8,128)(2,1)S(1)}, bf16[5,192,128]{2,1,0:T(8,128)(2,1)S(1)}, u32[]{:S(2)}, u32[]{:S(2)}) %collective-permute-start.22) | collective-permute-done | bytes 245792 | tf_op jit(solution)/shard_map/ppermute | solution.py:27
  99.9 0.1 add_convert_fusion.1.refs_10_
  100.1 0.5 collective-permute-start.27
  100.6 4.2 %collective-permute-done.24 = bf16[2,5,192,128]{3,2,1,0:T(8,128)(2,1)S(1)} collective-permute-done((bf16[2,5,192,128]{3,2,1,0:T(8,128)(2,1)S(1)}, bf16[2,5,192,128]{3,2,1,0:T(8,128)(2,1)S(1)}, u32[]{:S(2)}, u32[]{:S(2)}) %collective-permute-start.24) | collective-permute-done | bytes 491552 | tf_op jit(solution)/shard_map/ppermute | solution.py:27
  104.8 0.1 fusion.1.refs_8_
  104.9 2.6 %collective-permute-start.28 = (bf16[5,192,128]{2,1,0:T(8,128)(2,1)S(1)}, bf16[5,192,128]{2,1,0:T(8,128)(2,1)S(1)}, u32[]{:S(2)}, u32[]{:S(2)}) collective-permute-start(bf16[5,192,128]{2,1,0:T(8,128)(2,1)S(1)} %fusion.1.refs_8_), channel_id=1, source_target_pairs={{0,16},{4,20},{8,24},{12,28},{16,0},{20,4},{24,8},{28,12},{1,17},{... | collective-permute-start | bytes 737288 | tf_op jit(solution)/shard_map/ppermute | solution.py:27
  107.6 0.1 fusion.refs_9_
  107.6 0.4 collective-permute-start.29
  108.0 14.3 %input_grads.1 = bf16[224,3072]{1,0:T(8,128)(2,1)} custom-call(s32[12,24]{1,0:T(8,128)S(1)} %bitcast.39, bf16[12,24,128,128]{3,2,1,0:T(8,128)(2,1)S(1)} %bitcast.33, bf16[12,224,128]{2,1,0:T(8,128)(2,1)S(1)} %get-tuple-element.55.refs_1_.refs_0_, bf16[12,224,128]{2,1,0:T(8,128)(2,1)S(1)} %collective-permute-done.4.refs_1_, ...), custom_call_target="tpu_custom_call" | custom-call | flops 1000 | bytes 1000 | tf_op jit(solution)/shard_map/input_grads/pallas_call | solution.py:356
  122.4 1.0 main_sum.1.base_ref
  123.3 2.1 %collective-permute-done.29.other_ref = bf16[5,192,128]{2,1,0:T(8,128)(2,1)S(1)} collective-permute-done((bf16[5,192,128]{2,1,0:T(8,128)(2,1)S(1)}, bf16[5,192,128]{2,1,0:T(8,128)(2,1)S(1)}, u32[]{:S(2)}, u32[]{:S(2)}) %collective-permute-start.29) | collective-permute-done | bytes 245792 | tf_op jit(solution)/shard_map/ppermute | solution.py:27
  125.4 0.4 collective-permute-done.27.near_ref
  125.9 1.6 %last_sum.1 = f32[192,24,128]{2,1,0:T(8,128)} custom-call(f32[192,24,128]{2,1,0:T(8,128)S(1)} %main_sum.1.base_ref, bf16[12,192,128]{2,1,0:T(8,128)(2,1)S(1)} %collective-permute-done.27.near_ref, f32[5,192,128]{2,1,0:T(8,128)S(1)} %convert_element_type.91.mine_ref, bf16[5,192,128]{2,1,0:T(8,128)(2,1)S(1)} %collective-permute-done.29.other_ref), custom_call_target="tpu_custom_call" | custom-call | flops 1000 | bytes 1000 | tf_op jit(solution)/shard_map/last_sum/pallas_call | solution.py:434
  (25 shorter events, 0.2 us)
Async XLA Ops:
  0.6 6.5 %copy-start = (bf16[224,3072]{1,0:T(8,128)(2,1)S(1)}, bf16[224,3072]{1,0:T(8,128)(2,1)}, u32[]{:S(2)}) copy-start(bf16[224,3072]{1,0:T(8,128)(2,1)} %refs_0_) | copy-start | bytes 4128772
  0.6 6.5 %copy-start.2 = (s32[24,12]{0,1:T(8,128)S(1)}, s32[24,12]{0,1:T(8,128)}, u32[]{:S(2)}) copy-start(s32[24,12]{0,1:T(8,128)} %param.6) | copy-start | bytes 3460
  10.0 2.4 %collective-permute-start = (bf16[12,224,128]{2,1,0:T(8,128)(2,1)S(1)}, bf16[12,224,128]{2,1,0:T(8,128)(2,1)S(1)}, u32[]{:S(2)}, u32[]{:S(2)}) collective-permute-start(bf16[12,224,128]{2,1,0:T(8,128)(2,1)S(1)} %get-tuple-element.49), channel_id=1, source_target_pairs={{0,1},{1,0},{2,3},{3,2},{4,5},{5,4},{6,7},{7,6},{8,9},{9,8},{10,11... | collective-permute-start | bytes 2064392 | tf_op jit(solution)/shard_map/ppermute | solution.py:27
  12.6 18.7 %collective-permute-start.3 = (bf16[12,224,128]{2,1,0:T(8,128)(2,1)S(1)}, bf16[12,224,128]{2,1,0:T(8,128)(2,1)S(1)}, u32[]{:S(2)}, u32[]{:S(2)}) collective-permute-start(bf16[12,224,128]{2,1,0:T(8,128)(2,1)S(1)} %add_convert_fusion.refs_0_), channel_id=1, source_target_pairs={{0,2},{1,3},{2,0},{3,1},{4,6},{5,7},{6,4},{7,5},{8,10},{9,11},{10,... | collective-permute-start | bytes 2064392 | tf_op jit(solution)/shard_map/ppermute | solution.py:27
  15.4 15.8 %copy-start.1 = (bf16[224,1536]{1,0:T(8,128)(2,1)S(1)}, bf16[224,1536]{1,0:T(8,128)(2,1)}, u32[]{:S(2)}) copy-start(bf16[224,1536]{1,0:T(8,128)(2,1)} %cot_ref.1) | copy-start | bytes 2064388
  15.5 20.2 %collective-permute-start.6 = (bf16[224,1536]{1,0:T(8,128)(2,1)S(1)}, bf16[224,1536]{1,0:T(8,128)(2,1)S(1)}, u32[]{:S(2)}, u32[]{:S(2)}) collective-permute-start(bf16[224,1536]{1,0:T(8,128)(2,1)S(1)} %partner_features.1), channel_id=1, source_target_pairs={{0,8},{4,12},{8,0},{12,4},{16,24},{20,28},{24,16},{28,20},{1,9},{5... | collective-permute-start | bytes 2064392 | tf_op jit(solution)/shard_map/ppermute | solution.py:27
  20.2 1.7 %collective-permute-start.1 = (bf16[6,224,128]{2,1,0:T(8,128)(2,1)S(1)}, bf16[6,224,128]{2,1,0:T(8,128)(2,1)S(1)}, u32[]{:S(2)}, u32[]{:S(2)}) collective-permute-start(bf16[6,224,128]{2,1,0:T(8,128)(2,1)S(1)} %get-tuple-element.53.refs_1_), channel_id=1, source_target_pairs={{0,1},{1,0},{2,3},{3,2},{4,5},{5,4},{6,7},{7,6},{8,9},{9,8},{10,11... | collective-permute-start | bytes 1032200 | tf_op jit(solution)/shard_map/ppermute | solution.py:27
  20.3 2.1 %collective-permute-start.2 = (bf16[6,224,128]{2,1,0:T(8,128)(2,1)S(1)}, bf16[6,224,128]{2,1,0:T(8,128)(2,1)S(1)}, u32[]{:S(2)}, u32[]{:S(2)}) collective-permute-start(bf16[6,224,128]{2,1,0:T(8,128)(2,1)S(1)} %get-tuple-element.54), channel_id=1, source_target_pairs={{0,1},{1,0},{2,3},{3,2},{4,5},{5,4},{6,7},{7,6},{8,9},{9,8},{10,11... | collective-permute-start | bytes 1032200 | tf_op jit(solution)/shard_map/ppermute | solution.py:27
  32.3 11.0 %collective-permute-start.8 = (bf16[6,224,128]{2,1,0:T(8,128)(2,1)S(1)}, bf16[6,224,128]{2,1,0:T(8,128)(2,1)S(1)}, u32[]{:S(2)}, u32[]{:S(2)}) collective-permute-start(bf16[6,224,128]{2,1,0:T(8,128)(2,1)S(1)} %get-tuple-element.56), channel_id=1, source_target_pairs={{0,8},{4,12},{8,0},{12,4},{16,24},{20,28},{24,16},{28,20},{1,9},{5... | collective-permute-start | bytes 1032200 | tf_op jit(solution)/shard_map/ppermute | solution.py:27
  34.1 11.0 %collective-permute-start.10 = (bf16[6,224,128]{2,1,0:T(8,128)(2,1)S(1)}, bf16[6,224,128]{2,1,0:T(8,128)(2,1)S(1)}, u32[]{:S(2)}, u32[]{:S(2)}) collective-permute-start(bf16[6,224,128]{2,1,0:T(8,128)(2,1)S(1)} %get-tuple-element.58), channel_id=1, source_target_pairs={{0,2},{1,3},{2,0},{3,1},{4,6},{5,7},{6,4},{7,5},{8,10},{9,11},{10,... | collective-permute-start | bytes 1032200 | tf_op jit(solution)/shard_map/ppermute | solution.py:27
  35.7 15.0 %collective-permute-start.7 = (bf16[6,224,128]{2,1,0:T(8,128)(2,1)S(1)}, bf16[6,224,128]{2,1,0:T(8,128)(2,1)S(1)}, u32[]{:S(2)}, u32[]{:S(2)}) collective-permute-start(bf16[6,224,128]{2,1,0:T(8,128)(2,1)S(1)} %get-tuple-element.58), channel_id=1, source_target_pairs={{0,8},{4,12},{8,0},{12,4},{16,24},{20,28},{24,16},{28,20},{1,9},{5... | collective-permute-start | bytes 1032200 | tf_op jit(solution)/shard_map/ppermute | solution.py:27
  36.1 16.4 %collective-permute-start.5 = (bf16[6,224,128]{2,1,0:T(8,128)(2,1)S(1)}, bf16[6,224,128]{2,1,0:T(8,128)(2,1)S(1)}, u32[]{:S(2)}, u32[]{:S(2)}) collective-permute-start(bf16[6,224,128]{2,1,0:T(8,128)(2,1)S(1)} %get-tuple-element.56), channel_id=1, source_target_pairs={{0,2},{1,3},{2,0},{3,1},{4,6},{5,7},{6,4},{7,5},{8,10},{9,11},{10,... | collective-permute-start | bytes 1032200 | tf_op jit(solution)/shard_map/ppermute | solution.py:27
  43.3 14.7 %collective-permute-start.9 = (bf16[6,224,128]{2,1,0:T(8,128)(2,1)S(1)}, bf16[6,224,128]{2,1,0:T(8,128)(2,1)S(1)}, u32[]{:S(2)}, u32[]{:S(2)}) collective-permute-start(bf16[6,224,128]{2,1,0:T(8,128)(2,1)S(1)} %collective-permute-done.8.refs_6_), channel_id=1, source_target_pairs={{0,2},{1,3},{2,0},{3,1},{4,6},{5,7},{6,4},{7,5},{8,10},{9,11},{10,... | collective-permute-start | bytes 1032200 | tf_op jit(solution)/shard_map/ppermute | solution.py:27
  45.1 12.9 %collective-permute-start.11 = (bf16[6,224,128]{2,1,0:T(8,128)(2,1)S(1)}, bf16[6,224,128]{2,1,0:T(8,128)(2,1)S(1)}, u32[]{:S(2)}, u32[]{:S(2)}) collective-permute-start(bf16[6,224,128]{2,1,0:T(8,128)(2,1)S(1)} %collective-permute-done.10.refs_3_), channel_id=1, source_target_pairs={{0,8},{4,12},{8,0},{12,4},{16,24},{20,28},{24,16},{28,20},{1,9},{5... | collective-permute-start | bytes 1032200 | tf_op jit(solution)/shard_map/ppermute | solution.py:27
  46.7 11.9 %collective-permute-start.14 = (bf16[6,224,128]{2,1,0:T(8,128)(2,1)S(1)}, bf16[6,224,128]{2,1,0:T(8,128)(2,1)S(1)}, u32[]{:S(2)}, u32[]{:S(2)}) collective-permute-start(bf16[6,224,128]{2,1,0:T(8,128)(2,1)S(1)} %collective-permute-done.8.refs_6_), channel_id=1, source_target_pairs={{0,1},{1,0},{2,3},{3,2},{4,5},{5,4},{6,7},{7,6},{8,9},{9,8},{10,11... | collective-permute-start | bytes 1032200 | tf_op jit(solution)/shard_map/ppermute | solution.py:27
  50.7 8.4 %collective-permute-start.4 = (bf16[12,224,128]{2,1,0:T(8,128)(2,1)S(1)}, bf16[12,224,128]{2,1,0:T(8,128)(2,1)S(1)}, u32[]{:S(2)}, u32[]{:S(2)}) collective-permute-start(bf16[12,224,128]{2,1,0:T(8,128)(2,1)S(1)} %get-tuple-element.55.refs_1_.refs_0_), channel_id=1, source_target_pairs={{0,1},{1,0},{2,3},{3,2},{4,5},{5,4},{6,7},{7,6},{8,9},{9,8},{10,11... | collective-permute-start | bytes 2064392 | tf_op jit(solution)/shard_map/ppermute | solution.py:27
  52.5 6.0 %collective-permute-start.13 = (bf16[6,224,128]{2,1,0:T(8,128)(2,1)S(1)}, bf16[6,224,128]{2,1,0:T(8,128)(2,1)S(1)}, u32[]{:S(2)}, u32[]{:S(2)}) collective-permute-start(bf16[6,224,128]{2,1,0:T(8,128)(2,1)S(1)} %collective-permute-done.10.refs_3_), channel_id=1, source_target_pairs={{0,1},{1,0},{2,3},{3,2},{4,5},{5,4},{6,7},{7,6},{8,9},{9,8},{10,11... | collective-permute-start | bytes 1032200 | tf_op jit(solution)/shard_map/ppermute | solution.py:27
  58.0 1.7 %collective-permute-start.12 = (bf16[6,224,128]{2,1,0:T(8,128)(2,1)S(1)}, bf16[6,224,128]{2,1,0:T(8,128)(2,1)S(1)}, u32[]{:S(2)}, u32[]{:S(2)}) collective-permute-start(bf16[6,224,128]{2,1,0:T(8,128)(2,1)S(1)} %collective-permute-done.5.refs_2_), channel_id=1, source_target_pairs={{0,1},{1,0},{2,3},{3,2},{4,5},{5,4},{6,7},{7,6},{8,9},{9,8},{10,11... | collective-permute-start | bytes 1032200 | tf_op jit(solution)/shard_map/ppermute | solution.py:27
  58.0 2.1 %collective-permute-start.15 = (bf16[6,224,128]{2,1,0:T(8,128)(2,1)S(1)}, bf16[6,224,128]{2,1,0:T(8,128)(2,1)S(1)}, u32[]{:S(2)}, u32[]{:S(2)}) collective-permute-start(bf16[6,224,128]{2,1,0:T(8,128)(2,1)S(1)} %collective-permute-done.7.refs_7_), channel_id=1, source_target_pairs={{0,1},{1,0},{2,3},{3,2},{4,5},{5,4},{6,7},{7,6},{8,9},{9,8},{10,11... | collective-permute-start | bytes 1032200 | tf_op jit(solution)/shard_map/ppermute | solution.py:27
  58.6 2.1 %collective-permute-start.16 = (bf16[6,224,128]{2,1,0:T(8,128)(2,1)S(1)}, bf16[6,224,128]{2,1,0:T(8,128)(2,1)S(1)}, u32[]{:S(2)}, u32[]{:S(2)}) collective-permute-start(bf16[6,224,128]{2,1,0:T(8,128)(2,1)S(1)} %collective-permute-done.9.refs_10_), channel_id=1, source_target_pairs={{0,1},{1,0},{2,3},{3,2},{4,5},{5,4},{6,7},{7,6},{8,9},{9,8},{10,11... | collective-permute-start | bytes 1032200 | tf_op jit(solution)/shard_map/ppermute | solution.py:27
  58.6 2.6 %collective-permute-start.17 = (bf16[6,224,128]{2,1,0:T(8,128)(2,1)S(1)}, bf16[6,224,128]{2,1,0:T(8,128)(2,1)S(1)}, u32[]{:S(2)}, u32[]{:S(2)}) collective-permute-start(bf16[6,224,128]{2,1,0:T(8,128)(2,1)S(1)} %collective-permute-done.11.refs_11_), channel_id=1, source_target_pairs={{0,1},{1,0},{2,3},{3,2},{4,5},{5,4},{6,7},{7,6},{8,9},{9,8},{10,11... | collective-permute-start | bytes 1032200 | tf_op jit(solution)/shard_map/ppermute | solution.py:27
  63.3 7.8 %collective-permute-start.18 = (bf16[2,2,192,128]{3,2,1,0:T(8,128)(2,1)S(1)}, bf16[2,2,192,128]{3,2,1,0:T(8,128)(2,1)S(1)}, u32[]{:S(2)}, u32[]{:S(2)}) collective-permute-start(bf16[2,2,192,128]{3,2,1,0:T(8,128)(2,1)S(1)} %get-tuple-element.70), channel_id=1, source_target_pairs={{0,4},{4,0},{8,12},{12,8},{16,20},{20,16},{24,28},{28,24},{1,5},{5... | collective-permute-start | bytes 589832 | tf_op jit(solution)/shard_map/ppermute | solution.py:27
  66.3 15.4 %collective-permute-start.21 = (bf16[2,5,192,128]{3,2,1,0:T(8,128)(2,1)S(1)}, bf16[2,5,192,128]{3,2,1,0:T(8,128)(2,1)S(1)}, u32[]{:S(2)}, u32[]{:S(2)}) collective-permute-start(bf16[2,5,192,128]{3,2,1,0:T(8,128)(2,1)S(1)} %get-tuple-element.74), channel_id=1, source_target_pairs={{0,4},{4,0},{8,12},{12,8},{16,20},{20,16},{24,28},{28,24},{1,5},{5... | collective-permute-start | bytes 1474568 | tf_op jit(solution)/shard_map/ppermute | solution.py:27
  71.2 8.8 %collective-permute-start.20 = (bf16[2,192,128]{2,1,0:T(8,128)(2,1)S(1)}, bf16[2,192,128]{2,1,0:T(8,128)(2,1)S(1)}, u32[]{:S(2)}, u32[]{:S(2)}) collective-permute-start(bf16[2,192,128]{2,1,0:T(8,128)(2,1)S(1)} %get-tuple-element.94.refs_0_), channel_id=1, source_target_pairs={{0,16},{4,20},{8,24},{12,28},{16,0},{20,4},{24,8},{28,12},{1,17},{... | collective-permute-start | bytes 294920 | tf_op jit(solution)/shard_map/ppermute | solution.py:27
  76.1 23.9 %collective-permute-start.25 = (bf16[12,192,128]{2,1,0:T(8,128)(2,1)S(1)}, bf16[12,192,128]{2,1,0:T(8,128)(2,1)S(1)}, u32[]{:S(2)}, u32[]{:S(2)}) collective-permute-start(bf16[12,192,128]{2,1,0:T(8,128)(2,1)S(1)} %get-tuple-element.87), channel_id=1, source_target_pairs={{0,4},{4,0},{8,12},{12,8},{16,20},{20,16},{24,28},{28,24},{1,5},{5... | collective-permute-start | bytes 1769480 | tf_op jit(solution)/shard_map/ppermute | solution.py:27
  77.6 6.8 %collective-permute-start.19 = (bf16[2,192,128]{2,1,0:T(8,128)(2,1)S(1)}, bf16[2,192,128]{2,1,0:T(8,128)(2,1)S(1)}, u32[]{:S(2)}, u32[]{:S(2)}) collective-permute-start(bf16[2,192,128]{2,1,0:T(8,128)(2,1)S(1)} %get-tuple-element.95.refs_1_), channel_id=1, source_target_pairs={{0,24},{4,28},{8,16},{12,20},{16,8},{20,12},{24,0},{28,4},{1,25},{... | collective-permute-start | bytes 294920 | tf_op jit(solution)/shard_map/ppermute | solution.py:27
  79.3 25.6 %collective-permute-start.24 = (bf16[2,5,192,128]{3,2,1,0:T(8,128)(2,1)S(1)}, bf16[2,5,192,128]{3,2,1,0:T(8,128)(2,1)S(1)}, u32[]{:S(2)}, u32[]{:S(2)}) collective-permute-start(bf16[2,5,192,128]{3,2,1,0:T(8,128)(2,1)S(1)} %get-tuple-element.83), channel_id=1, source_target_pairs={{0,4},{4,0},{8,12},{12,8},{16,20},{20,16},{24,28},{28,24},{1,5},{5... | collective-permute-start | bytes 1474568 | tf_op jit(solution)/shard_map/ppermute | solution.py:27
  81.7 18.2 %collective-permute-start.22 = (bf16[5,192,128]{2,1,0:T(8,128)(2,1)S(1)}, bf16[5,192,128]{2,1,0:T(8,128)(2,1)S(1)}, u32[]{:S(2)}, u32[]{:S(2)}) collective-permute-start(bf16[5,192,128]{2,1,0:T(8,128)(2,1)S(1)} %fusion.3.refs_6_), channel_id=1, source_target_pairs={{0,16},{4,20},{8,24},{12,28},{16,0},{20,4},{24,8},{28,12},{1,17},{... | collective-permute-start | bytes 737288 | tf_op jit(solution)/shard_map/ppermute | solution.py:27
  84.5 23.1 %collective-permute-start.23 = (bf16[5,192,128]{2,1,0:T(8,128)(2,1)S(1)}, bf16[5,192,128]{2,1,0:T(8,128)(2,1)S(1)}, u32[]{:S(2)}, u32[]{:S(2)}) collective-permute-start(bf16[5,192,128]{2,1,0:T(8,128)(2,1)S(1)} %fusion.2.refs_7_), channel_id=1, source_target_pairs={{0,24},{4,28},{8,16},{12,20},{16,8},{20,12},{24,0},{28,4},{1,25},{... | collective-permute-start | bytes 737288 | tf_op jit(solution)/shard_map/ppermute | solution.py:27
  84.8 37.5 %collective-permute-start.26 = (bf16[12,192,128]{2,1,0:T(8,128)(2,1)S(1)}, bf16[12,192,128]{2,1,0:T(8,128)(2,1)S(1)}, u32[]{:S(2)}, u32[]{:S(2)}) collective-permute-start(bf16[12,192,128]{2,1,0:T(8,128)(2,1)S(1)} %get-tuple-element.89), channel_id=1, source_target_pairs={{0,4},{4,0},{8,12},{12,8},{16,20},{20,16},{24,28},{28,24},{1,5},{5... | collective-permute-start | bytes 1769480 | tf_op jit(solution)/shard_map/ppermute | solution.py:27
  100.1 25.8 %collective-permute-start.27 = (bf16[12,192,128]{2,1,0:T(8,128)(2,1)S(1)}, bf16[12,192,128]{2,1,0:T(8,128)(2,1)S(1)}, u32[]{:S(2)}, u32[]{:S(2)}) collective-permute-start(bf16[12,192,128]{2,1,0:T(8,128)(2,1)S(1)} %add_convert_fusion.1.refs_10_), channel_id=1, source_target_pairs={{0,8},{4,12},{8,0},{12,4},{16,24},{20,28},{24,16},{28,20},{1,9},{5... | collective-permute-start | bytes 1769480 | tf_op jit(solution)/shard_map/ppermute | solution.py:27
  104.9 17.4 %collective-permute-start.28 = (bf16[5,192,128]{2,1,0:T(8,128)(2,1)S(1)}, bf16[5,192,128]{2,1,0:T(8,128)(2,1)S(1)}, u32[]{:S(2)}, u32[]{:S(2)}) collective-permute-start(bf16[5,192,128]{2,1,0:T(8,128)(2,1)S(1)} %fusion.1.refs_8_), channel_id=1, source_target_pairs={{0,16},{4,20},{8,24},{12,28},{16,0},{20,4},{24,8},{28,12},{1,17},{... | collective-permute-start | bytes 737288 | tf_op jit(solution)/shard_map/ppermute | solution.py:27
  107.6 17.8 %collective-permute-start.29 = (bf16[5,192,128]{2,1,0:T(8,128)(2,1)S(1)}, bf16[5,192,128]{2,1,0:T(8,128)(2,1)S(1)}, u32[]{:S(2)}, u32[]{:S(2)}) collective-permute-start(bf16[5,192,128]{2,1,0:T(8,128)(2,1)S(1)} %fusion.refs_9_), channel_id=1, source_target_pairs={{0,24},{4,28},{8,16},{12,20},{16,8},{20,12},{24,0},{28,4},{1,25},{... | collective-permute-start | bytes 737288 | tf_op jit(solution)/shard_map/ppermute | solution.py:27

commit v4 on v3

--- a/solution.py
+++ b/solution.py
@@ -503,7 +503,7 @@
     pieces = own + [z0a, z0b, z1a, z1b, z2a, z2b, z3a, z3b]
 
     half = rows // 2
-    cuts = [0, half * 5 // 12, half * 10 // 12, half]
+    cuts = [0, half * 4 // 12, half * 9 // 12, half]
     far = (2, 3)
 
     def add(keep, recv):

time: 128 us -> 129 us (level)
  starting transfers between devices: 29.2 us -> 30.7 us
    ppermute x30, starting transfers between devices: 29.2 us -> 30.7 us  [swap(): return lax.ppermute(value, axis, [(i, i ^ bit) for i in range(count)])]
  transfers between devices with their start and end apart: 30 -> 30, of which waited for: 18 -> 17; matrix products, arithmetic and copies ran while one was open for 0% -> 0% of each run, Pallas kernels for 21% -> 21%
where the time goes in v4:
time: 129 us
  waiting for transfers between devices  57 us (44%)
  Pallas kernels  39.9 us (31%)
  starting transfers between devices  30.7 us (24%)
    ppermute x30, waiting for transfers between devices, swap(): return lax.ppermute(value, axis, [(i, i ^ bit) for i in range(count)])  57 us
    ppermute x30, starting transfers between devices, swap(): return lax.ppermute(value, axis, [(i, i ^ bit) for i in range(count)])  30.7 us
    pallas_call x1, Pallas kernels, run_input_grads(): pl.pallas_call(functools.partial(input_grads, slots, len(pieces)), grid_s...  14.3 us
    pallas_call x1, Pallas kernels, run_turn_weights(): pl.pallas_call(functools.partial(turn_weights, slots, rows), in_specs=[an...  6.52 us
    pallas_call x2, Pallas kernels, run_forward_more(): pl.pallas_call(functools.partial(forward_more, slots, width // 512, [w[:2...  4.97 us
    pallas_call x3, Pallas kernels, run_more_grads(): pl.pallas_call(functools.partial(more_grads, slots, flips, lo, hi, len(af...  4.95 us
    pallas_call x1, Pallas kernels, run_forward_first(): pl.pallas_call(functools.partial(forward_first, slots, rows // 4), in_spe...  2.76 us
  transfers between devices with their start and end apart: 30, of which 17 were waited for; matrix products, arithmetic and copies ran while one was open for 0% of the time, Pallas kernels for 21%

profile of v4, /device:TPU:0, one launch (start us, length us, event | category | flops | bytes accessed | tf_op | source)
XLA Modules:
  0.0 129.3 jit_solution(4902264362778531943)
XLA Ops:
  0.6 6.5 %turn_weights.1.w_ref = bf16[288,128,128]{2,1,0:T(8,128)(2,1)S(1)} custom-call(bf16[12,128,24,128]{3,2,1,0:T(8,128)(2,1)} %bitcast.40), custom_call_target="tpu_custom_call" | custom-call | flops 1000 | bytes 1000 | tf_op jit(solution)/shard_map/turn_weights/pallas_call | solution.py:86
  7.2 2.8 %forward_first.1 = (bf16[12,224,128]{2,1,0:T(8,128)(2,1)S(1)}, s32[288]{0:T(512)S(1)}) custom-call(s32[12,24]{1,0:T(8,128)S(1)} %bitcast.34, bf16[288,128,128]{2,1,0:T(8,128)(2,1)S(1)} %turn_weights.1.w_ref, bf16[224,3072]{1,0:T(8,128)(2,1)S(1)} %copy-done), custom_call_target="tpu_custom_call" | custom-call | flops 1000 | bytes 1000 | tf_op jit(solution)/shard_map/forward_first/pallas_call | solution.py:121
  10.0 0.5 collective-permute-start
  10.5 1.9 %forward_more.2 = f32[12,224,128]{2,1,0:T(8,128)S(1)} custom-call(s32[288]{0:T(512)S(1)} %get-tuple-element.48.entry_ref, bf16[288,128,128]{2,1,0:T(8,128)(2,1)S(1)} %turn_weights.1.w_ref, bf16[224,3072]{1,0:T(8,128)(2,1)S(1)} %copy-done), custom_call_target="tpu_custom_call" | custom-call | flops 1000 | bytes 1000 | tf_op jit(solution)/shard_map/forward_more/pallas_call | solution.py:138
  12.4 0.2 add_convert_fusion.refs_0_
  12.6 2.8 %collective-permute-start.3 = (bf16[12,224,128]{2,1,0:T(8,128)(2,1)S(1)}, bf16[12,224,128]{2,1,0:T(8,128)(2,1)S(1)}, u32[]{:S(2)}, u32[]{:S(2)}) collective-permute-start(bf16[12,224,128]{2,1,0:T(8,128)(2,1)S(1)} %add_convert_fusion.refs_0_), channel_id=1, source_target_pairs={{0,2},{1,3},{2,0},{3,1},{4,6},{5,7},{6,4},{7,5},{8,10},{9,11},{10,... | collective-permute-start | bytes 2064392 | tf_op jit(solution)/shard_map/ppermute | solution.py:27
  15.4 0.1 partner_features.1
  15.4 0.0 copy-start.1
  15.4 1.6 %collective-permute-start.6 = (bf16[224,1536]{1,0:T(8,128)(2,1)S(1)}, bf16[224,1536]{1,0:T(8,128)(2,1)S(1)}, u32[]{:S(2)}, u32[]{:S(2)}) collective-permute-start(bf16[224,1536]{1,0:T(8,128)(2,1)S(1)} %partner_features.1), channel_id=1, source_target_pairs={{0,8},{4,12},{8,0},{12,4},{16,24},{20,28},{24,16},{28,20},{1,9},{5... | collective-permute-start | bytes 2064392 | tf_op jit(solution)/shard_map/ppermute | solution.py:27
  17.1 3.1 %forward_more.3 = (bf16[6,224,128]{2,1,0:T(8,128)(2,1)S(1)}, bf16[6,224,128]{2,1,0:T(8,128)(2,1)S(1)}, f32[12,224,128]{2,1,0:T(8,128)S(1)}) custom-call(s32[288]{0:T(512)S(1)} %get-tuple-element.48.entry_ref, bf16[288,128,128]{2,1,0:T(8,128)(2,1)S(1)} %turn_weights.1.w_ref, bf16[224,3072]{1,0:T(8,128)(2,1)S(1)} %copy-done, ...), custom_call_target="tpu_custom_call" | custom-call | flops 1000 | bytes 1000 | tf_op jit(solution)/shard_map/forward_more/pallas_call | solution.py:138
  20.2 0.1 collective-permute-start.1
  20.3 0.5 collective-permute-start.2
  20.8 1.1 collective-permute-done.1.near_lo_ref
  21.9 0.5 collective-permute-done.2.near_hi_ref
  22.4 8.9 %collective-permute-done.3.across_ref = bf16[12,224,128]{2,1,0:T(8,128)(2,1)S(1)} collective-permute-done((bf16[12,224,128]{2,1,0:T(8,128)(2,1)S(1)}, bf16[12,224,128]{2,1,0:T(8,128)(2,1)S(1)}, u32[]{:S(2)}, u32[]{:S(2)}) %collective-permute-start.3) | collective-permute-done | bytes 688160 | tf_op jit(solution)/shard_map/ppermute | solution.py:27
  31.3 1.0 own_slope.1
  32.3 1.9 %collective-permute-start.8 = (bf16[6,224,128]{2,1,0:T(8,128)(2,1)S(1)}, bf16[6,224,128]{2,1,0:T(8,128)(2,1)S(1)}, u32[]{:S(2)}, u32[]{:S(2)}) collective-permute-start(bf16[6,224,128]{2,1,0:T(8,128)(2,1)S(1)} %get-tuple-element.56), channel_id=1, source_target_pairs={{0,8},{4,12},{8,0},{12,4},{16,24},{20,28},{24,16},{28,20},{1,9},{5... | collective-permute-start | bytes 1032200 | tf_op jit(solution)/shard_map/ppermute | solution.py:27
  34.1 1.5 %collective-permute-start.10 = (bf16[6,224,128]{2,1,0:T(8,128)(2,1)S(1)}, bf16[6,224,128]{2,1,0:T(8,128)(2,1)S(1)}, u32[]{:S(2)}, u32[]{:S(2)}) collective-permute-start(bf16[6,224,128]{2,1,0:T(8,128)(2,1)S(1)} %get-tuple-element.58), channel_id=1, source_target_pairs={{0,2},{1,3},{2,0},{3,1},{4,6},{5,7},{6,4},{7,5},{8,10},{9,11},{10,... | collective-permute-start | bytes 1032200 | tf_op jit(solution)/shard_map/ppermute | solution.py:27
  35.7 0.4 collective-permute-start.7
  36.1 0.3 collective-permute-start.5
  36.4 0.3 turn_features.2.xt_ref
  36.7 0.3 turn_features.3.xt2_ref
  37.0 6.3 %collective-permute-done.8.refs_6_ = bf16[6,224,128]{2,1,0:T(8,128)(2,1)S(1)} collective-permute-done((bf16[6,224,128]{2,1,0:T(8,128)(2,1)S(1)}, bf16[6,224,128]{2,1,0:T(8,128)(2,1)S(1)}, u32[]{:S(2)}, u32[]{:S(2)}) %collective-permute-start.8) | collective-permute-done | bytes 344096 | tf_op jit(solution)/shard_map/ppermute | solution.py:27
  43.3 1.8 %collective-permute-start.9 = (bf16[6,224,128]{2,1,0:T(8,128)(2,1)S(1)}, bf16[6,224,128]{2,1,0:T(8,128)(2,1)S(1)}, u32[]{:S(2)}, u32[]{:S(2)}) collective-permute-start(bf16[6,224,128]{2,1,0:T(8,128)(2,1)S(1)} %collective-permute-done.8.refs_6_), channel_id=1, source_target_pairs={{0,2},{1,3},{2,0},{3,1},{4,6},{5,7},{6,4},{7,5},{8,10},{9,11},{10,... | collective-permute-start | bytes 1032200 | tf_op jit(solution)/shard_map/ppermute | solution.py:27
  45.1 0.1 collective-permute-done.10.refs_3_
  45.1 1.5 %collective-permute-start.11 = (bf16[6,224,128]{2,1,0:T(8,128)(2,1)S(1)}, bf16[6,224,128]{2,1,0:T(8,128)(2,1)S(1)}, u32[]{:S(2)}, u32[]{:S(2)}) collective-permute-start(bf16[6,224,128]{2,1,0:T(8,128)(2,1)S(1)} %collective-permute-done.10.refs_3_), channel_id=1, source_target_pairs={{0,8},{4,12},{8,0},{12,4},{16,24},{20,28},{24,16},{28,20},{1,9},{5... | collective-permute-start | bytes 1032200 | tf_op jit(solution)/shard_map/ppermute | solution.py:27
  46.7 4.0 %collective-permute-done.7.refs_7_ = bf16[6,224,128]{2,1,0:T(8,128)(2,1)S(1)} collective-permute-done((bf16[6,224,128]{2,1,0:T(8,128)(2,1)S(1)}, bf16[6,224,128]{2,1,0:T(8,128)(2,1)S(1)}, u32[]{:S(2)}, u32[]{:S(2)}) %collective-permute-start.7) | collective-permute-done | bytes 344096 | tf_op jit(solution)/shard_map/ppermute | solution.py:27
  50.7 1.8 %collective-permute-done.5.refs_2_ = bf16[6,224,128]{2,1,0:T(8,128)(2,1)S(1)} collective-permute-done((bf16[6,224,128]{2,1,0:T(8,128)(2,1)S(1)}, bf16[6,224,128]{2,1,0:T(8,128)(2,1)S(1)}, u32[]{:S(2)}, u32[]{:S(2)}) %collective-permute-start.5) | collective-permute-done | bytes 344096 | tf_op jit(solution)/shard_map/ppermute | solution.py:27
  52.5 5.5 %collective-permute-done.9.refs_10_ = bf16[6,224,128]{2,1,0:T(8,128)(2,1)S(1)} collective-permute-done((bf16[6,224,128]{2,1,0:T(8,128)(2,1)S(1)}, bf16[6,224,128]{2,1,0:T(8,128)(2,1)S(1)}, u32[]{:S(2)}, u32[]{:S(2)}) %collective-permute-start.9) | collective-permute-done | bytes 344096 | tf_op jit(solution)/shard_map/ppermute | solution.py:27
  58.0 0.5 collective-permute-start.15
  58.6 0.0 collective-permute-start.16
  58.6 0.5 collective-permute-start.17
  59.1 0.6 collective-permute-done.12.refs_4_
  59.7 0.5 collective-permute-done.15.refs_9_
  60.2 0.5 collective-permute-done.16.refs_12_
  60.7 0.5 collective-permute-done.17.refs_13_
  61.2 2.3 %first_grads.1 = (bf16[2,3,192,128]{3,2,1,0:T(8,128)(2,1)S(1)}, f32[3,192,128]{2,1,0:T(8,128)S(1)}, f32[3,192,128]{2,1,0:T(8,128)S(1)}, bf16[96,224,128]{2,1,0:T(8,128)(2,1)S(1)}) custom-call(s32[12,24]{1,0:T(8,128)S(1)} %bitcast.35, bf16[12,128,224]{2,1,0:T(8,128)(2,1)S(1)} %turn_features.2.xt_ref, bf16[12,128,224]{2,1,0:T(8,128)(2,1)S(1)} %turn_features.3.xt2_ref, ...), custom_call_target="tpu_custom_call" | custom-call | flops 1000 | bytes 1000 | tf_op jit(solution)/shard_map/first_grads/pallas_call | solution.py:310
  63.4 1.6 %collective-permute-start.18 = (bf16[2,3,192,128]{3,2,1,0:T(8,128)(2,1)S(1)}, bf16[2,3,192,128]{3,2,1,0:T(8,128)(2,1)S(1)}, u32[]{:S(2)}, u32[]{:S(2)}) collective-permute-start(bf16[2,3,192,128]{3,2,1,0:T(8,128)(2,1)S(1)} %get-tuple-element.70), channel_id=1, source_target_pairs={{0,4},{4,0},{8,12},{12,8},{16,20},{20,16},{24,28},{28,24},{1,5},{5... | collective-permute-start | bytes 884744 | tf_op jit(solution)/shard_map/ppermute | solution.py:27
  65.0 1.4 %more_grads.3 = (bf16[2,5,192,128]{3,2,1,0:T(8,128)(2,1)S(1)}, f32[5,192,128]{2,1,0:T(8,128)S(1)}, f32[5,192,128]{2,1,0:T(8,128)S(1)}) custom-call(s32[12,24]{1,0:T(8,128)S(1)} %bitcast.36, bf16[12,128,224]{2,1,0:T(8,128)(2,1)S(1)} %turn_features.2.xt_ref, bf16[12,128,224]{2,1,0:T(8,128)(2,1)S(1)} %turn_features.3.xt2_ref, ...), custom_call_target="tpu_custom_call" | custom-call | flops 1000 | bytes 1000 | tf_op jit(solution)/shard_map/more_grads/pallas_call | solution.py:327
  66.4 0.6 collective-permute-start.21
  67.0 6.3 %collective-permute-done.18 = bf16[2,3,192,128]{3,2,1,0:T(8,128)(2,1)S(1)} collective-permute-done((bf16[2,3,192,128]{3,2,1,0:T(8,128)(2,1)S(1)}, bf16[2,3,192,128]{3,2,1,0:T(8,128)(2,1)S(1)}, u32[]{:S(2)}, u32[]{:S(2)}) %collective-permute-start.18) | collective-permute-done | bytes 294944 | tf_op jit(solution)/shard_map/ppermute | solution.py:27
  73.3 0.1 fusion.4
  73.4 2.6 %collective-permute-start.20 = (bf16[3,192,128]{2,1,0:T(8,128)(2,1)S(1)}, bf16[3,192,128]{2,1,0:T(8,128)(2,1)S(1)}, u32[]{:S(2)}, u32[]{:S(2)}) collective-permute-start(bf16[3,192,128]{2,1,0:T(8,128)(2,1)S(1)} %get-tuple-element.94.refs_0_), channel_id=1, source_target_pairs={{0,16},{4,20},{8,24},{12,28},{16,0},{20,4},{24,8},{28,12},{1,17},{... | collective-permute-start | bytes 442376 | tf_op jit(solution)/shard_map/ppermute | solution.py:27
  76.1 2.2 %more_grads.4 = (bf16[12,192,128]{2,1,0:T(8,128)(2,1)S(1)}, bf16[12,192,128]{2,1,0:T(8,128)(2,1)S(1)}, f32[12,192,128]{2,1,0:T(8,128)S(1)}, f32[12,192,128]{2,1,0:T(8,128)S(1)}) custom-call(s32[12,24]{1,0:T(8,128)S(1)} %bitcast.37, bf16[12,128,224]{2,1,0:T(8,128)(2,1)S(1)} %turn_features.2.xt_ref, bf16[12,128,224]{2,1,0:T(8,128)(2,1)S(1)} %turn_features.3.xt2_ref, ...), custom_call_target="tpu_custom_call" | custom-call | flops 1000 | bytes 1000 | tf_op jit(solution)/shard_map/more_grads/pallas_call | solution.py:327
  78.3 1.6 %collective-permute-start.25 = (bf16[12,192,128]{2,1,0:T(8,128)(2,1)S(1)}, bf16[12,192,128]{2,1,0:T(8,128)(2,1)S(1)}, u32[]{:S(2)}, u32[]{:S(2)}) collective-permute-start(bf16[12,192,128]{2,1,0:T(8,128)(2,1)S(1)} %get-tuple-element.87), channel_id=1, source_target_pairs={{0,4},{4,0},{8,12},{12,8},{16,20},{20,16},{24,28},{28,24},{1,5},{5... | collective-permute-start | bytes 1769480 | tf_op jit(solution)/shard_map/ppermute | solution.py:27
  79.8 0.2 collective-permute-start.19
  80.1 1.3 %more_grads.5 = (bf16[2,4,192,128]{3,2,1,0:T(8,128)(2,1)S(1)}, f32[4,192,128]{2,1,0:T(8,128)S(1)}, f32[4,192,128]{2,1,0:T(8,128)S(1)}) custom-call(s32[12,24]{1,0:T(8,128)S(1)} %bitcast.38, bf16[12,128,224]{2,1,0:T(8,128)(2,1)S(1)} %turn_features.2.xt_ref, bf16[12,128,224]{2,1,0:T(8,128)(2,1)S(1)} %turn_features.3.xt2_ref, ...), custom_call_target="tpu_custom_call" | custom-call | flops 1000 | bytes 1000 | tf_op jit(solution)/shard_map/more_grads/pallas_call | solution.py:327
  81.4 0.7 collective-permute-start.24
  82.1 2.2 %collective-permute-done.20.refs_1_ = bf16[3,192,128]{2,1,0:T(8,128)(2,1)S(1)} collective-permute-done((bf16[3,192,128]{2,1,0:T(8,128)(2,1)S(1)}, bf16[3,192,128]{2,1,0:T(8,128)(2,1)S(1)}, u32[]{:S(2)}, u32[]{:S(2)}) %collective-permute-start.20) | collective-permute-done | bytes 147488 | tf_op jit(solution)/shard_map/ppermute | solution.py:27
  84.3 0.1 fusion.1.refs_6_
  84.4 2.2 %collective-permute-start.22 = (bf16[5,192,128]{2,1,0:T(8,128)(2,1)S(1)}, bf16[5,192,128]{2,1,0:T(8,128)(2,1)S(1)}, u32[]{:S(2)}, u32[]{:S(2)}) collective-permute-start(bf16[5,192,128]{2,1,0:T(8,128)(2,1)S(1)} %fusion.1.refs_6_), channel_id=1, source_target_pairs={{0,16},{4,20},{8,24},{12,28},{16,0},{20,4},{24,8},{28,12},{1,17},{... | collective-permute-start | bytes 737288 | tf_op jit(solution)/shard_map/ppermute | solution.py:27
  86.6 1.1 collective-permute-done.19.refs_3_
  87.7 0.1 fusion.refs_7_
  87.8 1.1 collective-permute-start.23
  88.9 1.5 %collective-permute-start.26 = (bf16[12,192,128]{2,1,0:T(8,128)(2,1)S(1)}, bf16[12,192,128]{2,1,0:T(8,128)(2,1)S(1)}, u32[]{:S(2)}, u32[]{:S(2)}) collective-permute-start(bf16[12,192,128]{2,1,0:T(8,128)(2,1)S(1)} %get-tuple-element.89), channel_id=1, source_target_pairs={{0,4},{4,0},{8,12},{12,8},{16,20},{20,16},{24,28},{28,24},{1,5},{5... | collective-permute-start | bytes 1769480 | tf_op jit(solution)/shard_map/ppermute | solution.py:27
  90.4 14.5 %collective-permute-done.22.refs_0_ = bf16[5,192,128]{2,1,0:T(8,128)(2,1)S(1)} collective-permute-done((bf16[5,192,128]{2,1,0:T(8,128)(2,1)S(1)}, bf16[5,192,128]{2,1,0:T(8,128)(2,1)S(1)}, u32[]{:S(2)}, u32[]{:S(2)}) %collective-permute-start.22) | collective-permute-done | bytes 245792 | tf_op jit(solution)/shard_map/ppermute | solution.py:27
  104.9 0.1 add_convert_fusion.1.refs_10_
  105.0 0.1 collective-permute-start.27
  105.2 3.3 %collective-permute-start.28 = (bf16[4,192,128]{2,1,0:T(8,128)(2,1)S(1)}, bf16[4,192,128]{2,1,0:T(8,128)(2,1)S(1)}, u32[]{:S(2)}, u32[]{:S(2)}) collective-permute-start(bf16[4,192,128]{2,1,0:T(8,128)(2,1)S(1)} %fusion.3.refs_8_), channel_id=1, source_target_pairs={{0,16},{4,20},{8,24},{12,28},{16,0},{20,4},{24,8},{28,12},{1,17},{... | collective-permute-start | bytes 589832 | tf_op jit(solution)/shard_map/ppermute | solution.py:27
  108.5 1.2 collective-permute-start.29
  109.7 14.3 %input_grads.1 = bf16[224,3072]{1,0:T(8,128)(2,1)} custom-call(s32[12,24]{1,0:T(8,128)S(1)} %bitcast.39, bf16[12,24,128,128]{3,2,1,0:T(8,128)(2,1)S(1)} %bitcast.33, bf16[12,224,128]{2,1,0:T(8,128)(2,1)S(1)} %get-tuple-element.55.refs_1_.refs_0_, bf16[12,224,128]{2,1,0:T(8,128)(2,1)S(1)} %collective-permute-done.4.refs_1_, ...), custom_call_target="tpu_custom_call" | custom-call | flops 1000 | bytes 1000 | tf_op jit(solution)/shard_map/input_grads/pallas_call | solution.py:356
  124.1 1.0 main_sum.1.base_ref
  125.0 2.5 %collective-permute-done.29.other_ref = bf16[4,192,128]{2,1,0:T(8,128)(2,1)S(1)} collective-permute-done((bf16[4,192,128]{2,1,0:T(8,128)(2,1)S(1)}, bf16[4,192,128]{2,1,0:T(8,128)(2,1)S(1)}, u32[]{:S(2)}, u32[]{:S(2)}) %collective-permute-start.29) | collective-permute-done | bytes 196640 | tf_op jit(solution)/shard_map/ppermute | solution.py:27
  127.5 1.6 %last_sum.1 = f32[192,24,128]{2,1,0:T(8,128)} custom-call(f32[192,24,128]{2,1,0:T(8,128)S(1)} %main_sum.1.base_ref, bf16[12,192,128]{2,1,0:T(8,128)(2,1)S(1)} %collective-permute-done.27.near_ref, f32[4,192,128]{2,1,0:T(8,128)S(1)} %convert_element_type.91.mine_ref, bf16[4,192,128]{2,1,0:T(8,128)(2,1)S(1)} %collective-permute-done.29.other_ref), custom_call_target="tpu_custom_call" | custom-call | flops 1000 | bytes 1000 | tf_op jit(solution)/shard_map/last_sum/pallas_call | solution.py:434
  (25 shorter events, 0.2 us)
Async XLA Ops:
  0.6 6.5 %copy-start = (bf16[224,3072]{1,0:T(8,128)(2,1)S(1)}, bf16[224,3072]{1,0:T(8,128)(2,1)}, u32[]{:S(2)}) copy-start(bf16[224,3072]{1,0:T(8,128)(2,1)} %refs_0_) | copy-start | bytes 4128772
  0.6 6.5 %copy-start.2 = (s32[24,12]{0,1:T(8,128)S(1)}, s32[24,12]{0,1:T(8,128)}, u32[]{:S(2)}) copy-start(s32[24,12]{0,1:T(8,128)} %param.6) | copy-start | bytes 3460
  10.0 2.4 %collective-permute-start = (bf16[12,224,128]{2,1,0:T(8,128)(2,1)S(1)}, bf16[12,224,128]{2,1,0:T(8,128)(2,1)S(1)}, u32[]{:S(2)}, u32[]{:S(2)}) collective-permute-start(bf16[12,224,128]{2,1,0:T(8,128)(2,1)S(1)} %get-tuple-element.49), channel_id=1, source_target_pairs={{0,1},{1,0},{2,3},{3,2},{4,5},{5,4},{6,7},{7,6},{8,9},{9,8},{10,11... | collective-permute-start | bytes 2064392 | tf_op jit(solution)/shard_map/ppermute | solution.py:27
  12.6 18.7 %collective-permute-start.3 = (bf16[12,224,128]{2,1,0:T(8,128)(2,1)S(1)}, bf16[12,224,128]{2,1,0:T(8,128)(2,1)S(1)}, u32[]{:S(2)}, u32[]{:S(2)}) collective-permute-start(bf16[12,224,128]{2,1,0:T(8,128)(2,1)S(1)} %add_convert_fusion.refs_0_), channel_id=1, source_target_pairs={{0,2},{1,3},{2,0},{3,1},{4,6},{5,7},{6,4},{7,5},{8,10},{9,11},{10,... | collective-permute-start | bytes 2064392 | tf_op jit(solution)/shard_map/ppermute | solution.py:27
  15.4 15.8 %copy-start.1 = (bf16[224,1536]{1,0:T(8,128)(2,1)S(1)}, bf16[224,1536]{1,0:T(8,128)(2,1)}, u32[]{:S(2)}) copy-start(bf16[224,1536]{1,0:T(8,128)(2,1)} %cot_ref.1) | copy-start | bytes 2064388
  15.4 20.2 %collective-permute-start.6 = (bf16[224,1536]{1,0:T(8,128)(2,1)S(1)}, bf16[224,1536]{1,0:T(8,128)(2,1)S(1)}, u32[]{:S(2)}, u32[]{:S(2)}) collective-permute-start(bf16[224,1536]{1,0:T(8,128)(2,1)S(1)} %partner_features.1), channel_id=1, source_target_pairs={{0,8},{4,12},{8,0},{12,4},{16,24},{20,28},{24,16},{28,20},{1,9},{5... | collective-permute-start | bytes 2064392 | tf_op jit(solution)/shard_map/ppermute | solution.py:27
  20.2 1.7 %collective-permute-start.1 = (bf16[6,224,128]{2,1,0:T(8,128)(2,1)S(1)}, bf16[6,224,128]{2,1,0:T(8,128)(2,1)S(1)}, u32[]{:S(2)}, u32[]{:S(2)}) collective-permute-start(bf16[6,224,128]{2,1,0:T(8,128)(2,1)S(1)} %get-tuple-element.53.refs_1_), channel_id=1, source_target_pairs={{0,1},{1,0},{2,3},{3,2},{4,5},{5,4},{6,7},{7,6},{8,9},{9,8},{10,11... | collective-permute-start | bytes 1032200 | tf_op jit(solution)/shard_map/ppermute | solution.py:27
  20.3 2.1 %collective-permute-start.2 = (bf16[6,224,128]{2,1,0:T(8,128)(2,1)S(1)}, bf16[6,224,128]{2,1,0:T(8,128)(2,1)S(1)}, u32[]{:S(2)}, u32[]{:S(2)}) collective-permute-start(bf16[6,224,128]{2,1,0:T(8,128)(2,1)S(1)} %get-tuple-element.54), channel_id=1, source_target_pairs={{0,1},{1,0},{2,3},{3,2},{4,5},{5,4},{6,7},{7,6},{8,9},{9,8},{10,11... | collective-permute-start | bytes 1032200 | tf_op jit(solution)/shard_map/ppermute | solution.py:27
  32.3 11.0 %collective-permute-start.8 = (bf16[6,224,128]{2,1,0:T(8,128)(2,1)S(1)}, bf16[6,224,128]{2,1,0:T(8,128)(2,1)S(1)}, u32[]{:S(2)}, u32[]{:S(2)}) collective-permute-start(bf16[6,224,128]{2,1,0:T(8,128)(2,1)S(1)} %get-tuple-element.56), channel_id=1, source_target_pairs={{0,8},{4,12},{8,0},{12,4},{16,24},{20,28},{24,16},{28,20},{1,9},{5... | collective-permute-start | bytes 1032200 | tf_op jit(solution)/shard_map/ppermute | solution.py:27
  34.1 11.0 %collective-permute-start.10 = (bf16[6,224,128]{2,1,0:T(8,128)(2,1)S(1)}, bf16[6,224,128]{2,1,0:T(8,128)(2,1)S(1)}, u32[]{:S(2)}, u32[]{:S(2)}) collective-permute-start(bf16[6,224,128]{2,1,0:T(8,128)(2,1)S(1)} %get-tuple-element.58), channel_id=1, source_target_pairs={{0,2},{1,3},{2,0},{3,1},{4,6},{5,7},{6,4},{7,5},{8,10},{9,11},{10,... | collective-permute-start | bytes 1032200 | tf_op jit(solution)/shard_map/ppermute | solution.py:27
  35.7 15.0 %collective-permute-start.7 = (bf16[6,224,128]{2,1,0:T(8,128)(2,1)S(1)}, bf16[6,224,128]{2,1,0:T(8,128)(2,1)S(1)}, u32[]{:S(2)}, u32[]{:S(2)}) collective-permute-start(bf16[6,224,128]{2,1,0:T(8,128)(2,1)S(1)} %get-tuple-element.58), channel_id=1, source_target_pairs={{0,8},{4,12},{8,0},{12,4},{16,24},{20,28},{24,16},{28,20},{1,9},{5... | collective-permute-start | bytes 1032200 | tf_op jit(solution)/shard_map/ppermute | solution.py:27
  36.1 16.4 %collective-permute-start.5 = (bf16[6,224,128]{2,1,0:T(8,128)(2,1)S(1)}, bf16[6,224,128]{2,1,0:T(8,128)(2,1)S(1)}, u32[]{:S(2)}, u32[]{:S(2)}) collective-permute-start(bf16[6,224,128]{2,1,0:T(8,128)(2,1)S(1)} %get-tuple-element.56), channel_id=1, source_target_pairs={{0,2},{1,3},{2,0},{3,1},{4,6},{5,7},{6,4},{7,5},{8,10},{9,11},{10,... | collective-permute-start | bytes 1032200 | tf_op jit(solution)/shard_map/ppermute | solution.py:27
  43.3 14.7 %collective-permute-start.9 = (bf16[6,224,128]{2,1,0:T(8,128)(2,1)S(1)}, bf16[6,224,128]{2,1,0:T(8,128)(2,1)S(1)}, u32[]{:S(2)}, u32[]{:S(2)}) collective-permute-start(bf16[6,224,128]{2,1,0:T(8,128)(2,1)S(1)} %collective-permute-done.8.refs_6_), channel_id=1, source_target_pairs={{0,2},{1,3},{2,0},{3,1},{4,6},{5,7},{6,4},{7,5},{8,10},{9,11},{10,... | collective-permute-start | bytes 1032200 | tf_op jit(solution)/shard_map/ppermute | solution.py:27
  45.1 12.9 %collective-permute-start.11 = (bf16[6,224,128]{2,1,0:T(8,128)(2,1)S(1)}, bf16[6,224,128]{2,1,0:T(8,128)(2,1)S(1)}, u32[]{:S(2)}, u32[]{:S(2)}) collective-permute-start(bf16[6,224,128]{2,1,0:T(8,128)(2,1)S(1)} %collective-permute-done.10.refs_3_), channel_id=1, source_target_pairs={{0,8},{4,12},{8,0},{12,4},{16,24},{20,28},{24,16},{28,20},{1,9},{5... | collective-permute-start | bytes 1032200 | tf_op jit(solution)/shard_map/ppermute | solution.py:27
  46.7 11.9 %collective-permute-start.14 = (bf16[6,224,128]{2,1,0:T(8,128)(2,1)S(1)}, bf16[6,224,128]{2,1,0:T(8,128)(2,1)S(1)}, u32[]{:S(2)}, u32[]{:S(2)}) collective-permute-start(bf16[6,224,128]{2,1,0:T(8,128)(2,1)S(1)} %collective-permute-done.8.refs_6_), channel_id=1, source_target_pairs={{0,1},{1,0},{2,3},{3,2},{4,5},{5,4},{6,7},{7,6},{8,9},{9,8},{10,11... | collective-permute-start | bytes 1032200 | tf_op jit(solution)/shard_map/ppermute | solution.py:27
  50.7 8.4 %collective-permute-start.4 = (bf16[12,224,128]{2,1,0:T(8,128)(2,1)S(1)}, bf16[12,224,128]{2,1,0:T(8,128)(2,1)S(1)}, u32[]{:S(2)}, u32[]{:S(2)}) collective-permute-start(bf16[12,224,128]{2,1,0:T(8,128)(2,1)S(1)} %get-tuple-element.55.refs_1_.refs_0_), channel_id=1, source_target_pairs={{0,1},{1,0},{2,3},{3,2},{4,5},{5,4},{6,7},{7,6},{8,9},{9,8},{10,11... | collective-permute-start | bytes 2064392 | tf_op jit(solution)/shard_map/ppermute | solution.py:27
  52.5 6.0 %collective-permute-start.13 = (bf16[6,224,128]{2,1,0:T(8,128)(2,1)S(1)}, bf16[6,224,128]{2,1,0:T(8,128)(2,1)S(1)}, u32[]{:S(2)}, u32[]{:S(2)}) collective-permute-start(bf16[6,224,128]{2,1,0:T(8,128)(2,1)S(1)} %collective-permute-done.10.refs_3_), channel_id=1, source_target_pairs={{0,1},{1,0},{2,3},{3,2},{4,5},{5,4},{6,7},{7,6},{8,9},{9,8},{10,11... | collective-permute-start | bytes 1032200 | tf_op jit(solution)/shard_map/ppermute | solution.py:27
  58.0 1.7 %collective-permute-start.12 = (bf16[6,224,128]{2,1,0:T(8,128)(2,1)S(1)}, bf16[6,224,128]{2,1,0:T(8,128)(2,1)S(1)}, u32[]{:S(2)}, u32[]{:S(2)}) collective-permute-start(bf16[6,224,128]{2,1,0:T(8,128)(2,1)S(1)} %collective-permute-done.5.refs_2_), channel_id=1, source_target_pairs={{0,1},{1,0},{2,3},{3,2},{4,5},{5,4},{6,7},{7,6},{8,9},{9,8},{10,11... | collective-permute-start | bytes 1032200 | tf_op jit(solution)/shard_map/ppermute | solution.py:27
  58.0 2.1 %collective-permute-start.15 = (bf16[6,224,128]{2,1,0:T(8,128)(2,1)S(1)}, bf16[6,224,128]{2,1,0:T(8,128)(2,1)S(1)}, u32[]{:S(2)}, u32[]{:S(2)}) collective-permute-start(bf16[6,224,128]{2,1,0:T(8,128)(2,1)S(1)} %collective-permute-done.7.refs_7_), channel_id=1, source_target_pairs={{0,1},{1,0},{2,3},{3,2},{4,5},{5,4},{6,7},{7,6},{8,9},{9,8},{10,11... | collective-permute-start | bytes 1032200 | tf_op jit(solution)/shard_map/ppermute | solution.py:27
  58.6 2.1 %collective-permute-start.16 = (bf16[6,224,128]{2,1,0:T(8,128)(2,1)S(1)}, bf16[6,224,128]{2,1,0:T(8,128)(2,1)S(1)}, u32[]{:S(2)}, u32[]{:S(2)}) collective-permute-start(bf16[6,224,128]{2,1,0:T(8,128)(2,1)S(1)} %collective-permute-done.9.refs_10_), channel_id=1, source_target_pairs={{0,1},{1,0},{2,3},{3,2},{4,5},{5,4},{6,7},{7,6},{8,9},{9,8},{10,11... | collective-permute-start | bytes 1032200 | tf_op jit(solution)/shard_map/ppermute | solution.py:27
  58.6 2.6 %collective-permute-start.17 = (bf16[6,224,128]{2,1,0:T(8,128)(2,1)S(1)}, bf16[6,224,128]{2,1,0:T(8,128)(2,1)S(1)}, u32[]{:S(2)}, u32[]{:S(2)}) collective-permute-start(bf16[6,224,128]{2,1,0:T(8,128)(2,1)S(1)} %collective-permute-done.11.refs_11_), channel_id=1, source_target_pairs={{0,1},{1,0},{2,3},{3,2},{4,5},{5,4},{6,7},{7,6},{8,9},{9,8},{10,11... | collective-permute-start | bytes 1032200 | tf_op jit(solution)/shard_map/ppermute | solution.py:27
  63.4 9.9 %collective-permute-start.18 = (bf16[2,3,192,128]{3,2,1,0:T(8,128)(2,1)S(1)}, bf16[2,3,192,128]{3,2,1,0:T(8,128)(2,1)S(1)}, u32[]{:S(2)}, u32[]{:S(2)}) collective-permute-start(bf16[2,3,192,128]{3,2,1,0:T(8,128)(2,1)S(1)} %get-tuple-element.70), channel_id=1, source_target_pairs={{0,4},{4,0},{8,12},{12,8},{16,20},{20,16},{24,28},{28,24},{1,5},{5... | collective-permute-start | bytes 884744 | tf_op jit(solution)/shard_map/ppermute | solution.py:27
  66.4 17.9 %collective-permute-start.21 = (bf16[2,5,192,128]{3,2,1,0:T(8,128)(2,1)S(1)}, bf16[2,5,192,128]{3,2,1,0:T(8,128)(2,1)S(1)}, u32[]{:S(2)}, u32[]{:S(2)}) collective-permute-start(bf16[2,5,192,128]{3,2,1,0:T(8,128)(2,1)S(1)} %get-tuple-element.74), channel_id=1, source_target_pairs={{0,4},{4,0},{8,12},{12,8},{16,20},{20,16},{24,28},{28,24},{1,5},{5... | collective-permute-start | bytes 1474568 | tf_op jit(solution)/shard_map/ppermute | solution.py:27
  73.4 10.9 %collective-permute-start.20 = (bf16[3,192,128]{2,1,0:T(8,128)(2,1)S(1)}, bf16[3,192,128]{2,1,0:T(8,128)(2,1)S(1)}, u32[]{:S(2)}, u32[]{:S(2)}) collective-permute-start(bf16[3,192,128]{2,1,0:T(8,128)(2,1)S(1)} %get-tuple-element.94.refs_0_), channel_id=1, source_target_pairs={{0,16},{4,20},{8,24},{12,28},{16,0},{20,4},{24,8},{28,12},{1,17},{... | collective-permute-start | bytes 442376 | tf_op jit(solution)/shard_map/ppermute | solution.py:27
  78.3 26.6 %collective-permute-start.25 = (bf16[12,192,128]{2,1,0:T(8,128)(2,1)S(1)}, bf16[12,192,128]{2,1,0:T(8,128)(2,1)S(1)}, u32[]{:S(2)}, u32[]{:S(2)}) collective-permute-start(bf16[12,192,128]{2,1,0:T(8,128)(2,1)S(1)} %get-tuple-element.87), channel_id=1, source_target_pairs={{0,4},{4,0},{8,12},{12,8},{16,20},{20,16},{24,28},{28,24},{1,5},{5... | collective-permute-start | bytes 1769480 | tf_op jit(solution)/shard_map/ppermute | solution.py:27
  79.8 7.9 %collective-permute-start.19 = (bf16[3,192,128]{2,1,0:T(8,128)(2,1)S(1)}, bf16[3,192,128]{2,1,0:T(8,128)(2,1)S(1)}, u32[]{:S(2)}, u32[]{:S(2)}) collective-permute-start(bf16[3,192,128]{2,1,0:T(8,128)(2,1)S(1)} %get-tuple-element.95.refs_1_), channel_id=1, source_target_pairs={{0,24},{4,28},{8,16},{12,20},{16,8},{20,12},{24,0},{28,4},{1,25},{... | collective-permute-start | bytes 442376 | tf_op jit(solution)/shard_map/ppermute | solution.py:27
  81.4 23.7 %collective-permute-start.24 = (bf16[2,4,192,128]{3,2,1,0:T(8,128)(2,1)S(1)}, bf16[2,4,192,128]{3,2,1,0:T(8,128)(2,1)S(1)}, u32[]{:S(2)}, u32[]{:S(2)}) collective-permute-start(bf16[2,4,192,128]{3,2,1,0:T(8,128)(2,1)S(1)} %get-tuple-element.83), channel_id=1, source_target_pairs={{0,4},{4,0},{8,12},{12,8},{16,20},{20,16},{24,28},{28,24},{1,5},{5... | collective-permute-start | bytes 1179656 | tf_op jit(solution)/shard_map/ppermute | solution.py:27
  84.4 20.5 %collective-permute-start.22 = (bf16[5,192,128]{2,1,0:T(8,128)(2,1)S(1)}, bf16[5,192,128]{2,1,0:T(8,128)(2,1)S(1)}, u32[]{:S(2)}, u32[]{:S(2)}) collective-permute-start(bf16[5,192,128]{2,1,0:T(8,128)(2,1)S(1)} %fusion.1.refs_6_), channel_id=1, source_target_pairs={{0,16},{4,20},{8,24},{12,28},{16,0},{20,4},{24,8},{28,12},{1,17},{... | collective-permute-start | bytes 737288 | tf_op jit(solution)/shard_map/ppermute | solution.py:27
  87.8 20.7 %collective-permute-start.23 = (bf16[5,192,128]{2,1,0:T(8,128)(2,1)S(1)}, bf16[5,192,128]{2,1,0:T(8,128)(2,1)S(1)}, u32[]{:S(2)}, u32[]{:S(2)}) collective-permute-start(bf16[5,192,128]{2,1,0:T(8,128)(2,1)S(1)} %fusion.refs_7_), channel_id=1, source_target_pairs={{0,24},{4,28},{8,16},{12,20},{16,8},{20,12},{24,0},{28,4},{1,25},{... | collective-permute-start | bytes 737288 | tf_op jit(solution)/shard_map/ppermute | solution.py:27
  88.9 35.2 %collective-permute-start.26 = (bf16[12,192,128]{2,1,0:T(8,128)(2,1)S(1)}, bf16[12,192,128]{2,1,0:T(8,128)(2,1)S(1)}, u32[]{:S(2)}, u32[]{:S(2)}) collective-permute-start(bf16[12,192,128]{2,1,0:T(8,128)(2,1)S(1)} %get-tuple-element.89), channel_id=1, source_target_pairs={{0,4},{4,0},{8,12},{12,8},{16,20},{20,16},{24,28},{28,24},{1,5},{5... | collective-permute-start | bytes 1769480 | tf_op jit(solution)/shard_map/ppermute | solution.py:27
  105.0 22.5 %collective-permute-start.27 = (bf16[12,192,128]{2,1,0:T(8,128)(2,1)S(1)}, bf16[12,192,128]{2,1,0:T(8,128)(2,1)S(1)}, u32[]{:S(2)}, u32[]{:S(2)}) collective-permute-start(bf16[12,192,128]{2,1,0:T(8,128)(2,1)S(1)} %add_convert_fusion.1.refs_10_), channel_id=1, source_target_pairs={{0,8},{4,12},{8,0},{12,4},{16,24},{20,28},{24,16},{28,20},{1,9},{5... | collective-permute-start | bytes 1769480 | tf_op jit(solution)/shard_map/ppermute | solution.py:27
  105.2 18.8 %collective-permute-start.28 = (bf16[4,192,128]{2,1,0:T(8,128)(2,1)S(1)}, bf16[4,192,128]{2,1,0:T(8,128)(2,1)S(1)}, u32[]{:S(2)}, u32[]{:S(2)}) collective-permute-start(bf16[4,192,128]{2,1,0:T(8,128)(2,1)S(1)} %fusion.3.refs_8_), channel_id=1, source_target_pairs={{0,16},{4,20},{8,24},{12,28},{16,0},{20,4},{24,8},{28,12},{1,17},{... | collective-permute-start | bytes 589832 | tf_op jit(solution)/shard_map/ppermute | solution.py:27
  108.5 19.0 %collective-permute-start.29 = (bf16[4,192,128]{2,1,0:T(8,128)(2,1)S(1)}, bf16[4,192,128]{2,1,0:T(8,128)(2,1)S(1)}, u32[]{:S(2)}, u32[]{:S(2)}) collective-permute-start(bf16[4,192,128]{2,1,0:T(8,128)(2,1)S(1)} %fusion.2.refs_9_), channel_id=1, source_target_pairs={{0,24},{4,28},{8,16},{12,20},{16,8},{20,12},{24,0},{28,4},{1,25},{... | collective-permute-start | bytes 589832 | tf_op jit(solution)/shard_map/ppermute | solution.py:27

commit v5 on v3

--- a/solution.py
+++ b/solution.py
@@ -54,11 +54,14 @@
 def turn_weights(slots, rows, w_ref, wt_ref, raw, wide, sems):
     few = 8 * rows
 
+    cuts = [0, 2, slots // 2, slots]
+
     def fetch(n):
-        return pltpu.make_async_copy(w_ref.at[pl.ds(2 * n, 2)], raw.at[pl.ds(2 * n, 2)], sems.at[n])
-
-    for n in range(slots // 2):
-        fetch(n).start(priority=n % 2)
+        here = pl.ds(cuts[n], cuts[n + 1] - cuts[n])
+        return pltpu.make_async_copy(w_ref.at[here], raw.at[here], sems.at[n])
+
+    for n in range(3):
+        fetch(n).start()
     to = lax.broadcasted_iota(jnp.int32, (few, few), 0)
     source = lax.broadcasted_iota(jnp.int32, (few, few), 1)
     turn = jnp.where(source == (to % 8) * rows + to // 8, 1.0, 0.0).astype(bf16)
@@ -66,7 +69,12 @@
     @pl.loop(0, slots // 2)
     def _(n):
         k, j = 2 * n, 2 * n + 1
-        fetch(n).wait()
+        for m in range(3):
+
+            @pl.when(k == cuts[m])
+            def _(m=m):
+                fetch(m).wait()
+
         wide[...] = raw[k].astype(f32).reshape(128 * rows, 128)
         value = raw[j].astype(f32).reshape(128 * rows, 128).astype(bf16)
         for i in range(8):
@@ -90,7 +98,7 @@
         scratch_shapes=[
             pltpu.VMEM((slots, 128, rows, 128), bf16),
             pltpu.VMEM((128 * rows, 128), f32),
-            pltpu.SemaphoreType.DMA((slots // 2,)),
+            pltpu.SemaphoreType.DMA((3,)),
         ],
         out_shape=jax.ShapeDtypeStruct((rows * slots, 128, 128), bf16),
         compiler_params=pltpu.CompilerParams(vmem_limit_bytes=FAR_LIMIT * 2**20),

time: 128 us -> 128 us (level)
  transfers between devices with their start and end apart: 30 -> 30, of which waited for: 18 -> 17; matrix products, arithmetic and copies ran while one was open for 0% -> 0% of each run, Pallas kernels for 21% -> 21%
where the time goes in v5:
time: 128 us
  waiting for transfers between devices  57.4 us (45%)
  Pallas kernels  39.4 us (31%)
  starting transfers between devices  29.2 us (23%)
    ppermute x30, waiting for transfers between devices, swap(): return lax.ppermute(value, axis, [(i, i ^ bit) for i in range(count)])  57.4 us
    ppermute x30, starting transfers between devices, swap(): return lax.ppermute(value, axis, [(i, i ^ bit) for i in range(count)])  29.2 us
    pallas_call x1, Pallas kernels, run_input_grads(): pl.pallas_call(functools.partial(input_grads, slots, len(pieces)), grid_s...  14.3 us
    pallas_call x1, Pallas kernels, run_turn_weights(): pl.pallas_call(functools.partial(turn_weights, slots, rows), in_specs=[an...  6.02 us
    pallas_call x3, Pallas kernels, run_more_grads(): pl.pallas_call(functools.partial(more_grads, slots, flips, lo, hi, len(af...  5.06 us
    pallas_call x2, Pallas kernels, run_forward_more(): pl.pallas_call(functools.partial(forward_more, slots, width // 512, [w[:2...  4.97 us
    pallas_call x1, Pallas kernels, run_forward_first(): pl.pallas_call(functools.partial(forward_first, slots, rows // 4), in_spe...  2.76 us
  transfers between devices with their start and end apart: 30, of which 17 were waited for; matrix products, arithmetic and copies ran while one was open for 0% of the time, Pallas kernels for 21%

profile of v5, /device:TPU:0, one launch (start us, length us, event | category | flops | bytes accessed | tf_op | source)
XLA Modules:
  0.0 127.7 jit_solution(12332622806064286082)
XLA Ops:
  0.6 6.0 %turn_weights.1.w_ref = bf16[288,128,128]{2,1,0:T(8,128)(2,1)S(1)} custom-call(bf16[12,128,24,128]{3,2,1,0:T(8,128)(2,1)} %bitcast.40), custom_call_target="tpu_custom_call" | custom-call | flops 1000 | bytes 1000 | tf_op jit(solution)/shard_map/turn_weights/pallas_call | solution.py:94
  6.7 2.8 %forward_first.1 = (bf16[12,224,128]{2,1,0:T(8,128)(2,1)S(1)}, s32[288]{0:T(512)S(1)}) custom-call(s32[12,24]{1,0:T(8,128)S(1)} %bitcast.34, bf16[288,128,128]{2,1,0:T(8,128)(2,1)S(1)} %turn_weights.1.w_ref, bf16[224,3072]{1,0:T(8,128)(2,1)S(1)} %copy-done), custom_call_target="tpu_custom_call" | custom-call | flops 1000 | bytes 1000 | tf_op jit(solution)/shard_map/forward_first/pallas_call | solution.py:129
  9.5 0.5 collective-permute-start
  10.0 1.9 %forward_more.2 = f32[12,224,128]{2,1,0:T(8,128)S(1)} custom-call(s32[288]{0:T(512)S(1)} %get-tuple-element.48.entry_ref, bf16[288,128,128]{2,1,0:T(8,128)(2,1)S(1)} %turn_weights.1.w_ref, bf16[224,3072]{1,0:T(8,128)(2,1)S(1)} %copy-done), custom_call_target="tpu_custom_call" | custom-call | flops 1000 | bytes 1000 | tf_op jit(solution)/shard_map/forward_more/pallas_call | solution.py:146
  11.9 0.2 add_convert_fusion.refs_0_
  12.1 2.8 %collective-permute-start.3 = (bf16[12,224,128]{2,1,0:T(8,128)(2,1)S(1)}, bf16[12,224,128]{2,1,0:T(8,128)(2,1)S(1)}, u32[]{:S(2)}, u32[]{:S(2)}) collective-permute-start(bf16[12,224,128]{2,1,0:T(8,128)(2,1)S(1)} %add_convert_fusion.refs_0_), channel_id=1, source_target_pairs={{0,2},{1,3},{2,0},{3,1},{4,6},{5,7},{6,4},{7,5},{8,10},{9,11},{10,... | collective-permute-start | bytes 2064392 | tf_op jit(solution)/shard_map/ppermute | solution.py:27
  14.9 0.1 partner_features.1
  15.0 1.7 %collective-permute-start.6 = (bf16[224,1536]{1,0:T(8,128)(2,1)S(1)}, bf16[224,1536]{1,0:T(8,128)(2,1)S(1)}, u32[]{:S(2)}, u32[]{:S(2)}) collective-permute-start(bf16[224,1536]{1,0:T(8,128)(2,1)S(1)} %partner_features.1), channel_id=1, source_target_pairs={{0,8},{4,12},{8,0},{12,4},{16,24},{20,28},{24,16},{28,20},{1,9},{5... | collective-permute-start | bytes 2064392 | tf_op jit(solution)/shard_map/ppermute | solution.py:27
  16.6 3.1 %forward_more.3 = (bf16[6,224,128]{2,1,0:T(8,128)(2,1)S(1)}, bf16[6,224,128]{2,1,0:T(8,128)(2,1)S(1)}, f32[12,224,128]{2,1,0:T(8,128)S(1)}) custom-call(s32[288]{0:T(512)S(1)} %get-tuple-element.48.entry_ref, bf16[288,128,128]{2,1,0:T(8,128)(2,1)S(1)} %turn_weights.1.w_ref, bf16[224,3072]{1,0:T(8,128)(2,1)S(1)} %copy-done, ...), custom_call_target="tpu_custom_call" | custom-call | flops 1000 | bytes 1000 | tf_op jit(solution)/shard_map/forward_more/pallas_call | solution.py:146
  19.7 0.1 collective-permute-start.1
  19.8 0.5 collective-permute-start.2
  20.3 1.1 collective-permute-done.1.near_lo_ref
  21.4 0.5 collective-permute-done.2.near_hi_ref
  21.9 8.9 %collective-permute-done.3.across_ref = bf16[12,224,128]{2,1,0:T(8,128)(2,1)S(1)} collective-permute-done((bf16[12,224,128]{2,1,0:T(8,128)(2,1)S(1)}, bf16[12,224,128]{2,1,0:T(8,128)(2,1)S(1)}, u32[]{:S(2)}, u32[]{:S(2)}) %collective-permute-start.3) | collective-permute-done | bytes 688160 | tf_op jit(solution)/shard_map/ppermute | solution.py:27
  30.8 1.0 own_slope.1
  31.8 1.9 %collective-permute-start.8 = (bf16[6,224,128]{2,1,0:T(8,128)(2,1)S(1)}, bf16[6,224,128]{2,1,0:T(8,128)(2,1)S(1)}, u32[]{:S(2)}, u32[]{:S(2)}) collective-permute-start(bf16[6,224,128]{2,1,0:T(8,128)(2,1)S(1)} %get-tuple-element.56), channel_id=1, source_target_pairs={{0,8},{4,12},{8,0},{12,4},{16,24},{20,28},{24,16},{28,20},{1,9},{5... | collective-permute-start | bytes 1032200 | tf_op jit(solution)/shard_map/ppermute | solution.py:27
  33.6 1.5 %collective-permute-start.10 = (bf16[6,224,128]{2,1,0:T(8,128)(2,1)S(1)}, bf16[6,224,128]{2,1,0:T(8,128)(2,1)S(1)}, u32[]{:S(2)}, u32[]{:S(2)}) collective-permute-start(bf16[6,224,128]{2,1,0:T(8,128)(2,1)S(1)} %get-tuple-element.58), channel_id=1, source_target_pairs={{0,2},{1,3},{2,0},{3,1},{4,6},{5,7},{6,4},{7,5},{8,10},{9,11},{10,... | collective-permute-start | bytes 1032200 | tf_op jit(solution)/shard_map/ppermute | solution.py:27
  35.2 0.4 collective-permute-start.7
  35.6 0.3 collective-permute-start.5
  35.9 0.3 turn_features.2.xt_ref
  36.2 0.3 turn_features.3.xt2_ref
  36.5 6.3 %collective-permute-done.8.refs_6_ = bf16[6,224,128]{2,1,0:T(8,128)(2,1)S(1)} collective-permute-done((bf16[6,224,128]{2,1,0:T(8,128)(2,1)S(1)}, bf16[6,224,128]{2,1,0:T(8,128)(2,1)S(1)}, u32[]{:S(2)}, u32[]{:S(2)}) %collective-permute-start.8) | collective-permute-done | bytes 344096 | tf_op jit(solution)/shard_map/ppermute | solution.py:27
  42.8 1.8 %collective-permute-start.9 = (bf16[6,224,128]{2,1,0:T(8,128)(2,1)S(1)}, bf16[6,224,128]{2,1,0:T(8,128)(2,1)S(1)}, u32[]{:S(2)}, u32[]{:S(2)}) collective-permute-start(bf16[6,224,128]{2,1,0:T(8,128)(2,1)S(1)} %collective-permute-done.8.refs_6_), channel_id=1, source_target_pairs={{0,2},{1,3},{2,0},{3,1},{4,6},{5,7},{6,4},{7,5},{8,10},{9,11},{10,... | collective-permute-start | bytes 1032200 | tf_op jit(solution)/shard_map/ppermute | solution.py:27
  44.6 0.1 collective-permute-done.10.refs_3_
  44.6 1.5 %collective-permute-start.11 = (bf16[6,224,128]{2,1,0:T(8,128)(2,1)S(1)}, bf16[6,224,128]{2,1,0:T(8,128)(2,1)S(1)}, u32[]{:S(2)}, u32[]{:S(2)}) collective-permute-start(bf16[6,224,128]{2,1,0:T(8,128)(2,1)S(1)} %collective-permute-done.10.refs_3_), channel_id=1, source_target_pairs={{0,8},{4,12},{8,0},{12,4},{16,24},{20,28},{24,16},{28,20},{1,9},{5... | collective-permute-start | bytes 1032200 | tf_op jit(solution)/shard_map/ppermute | solution.py:27
  46.2 4.0 %collective-permute-done.7.refs_7_ = bf16[6,224,128]{2,1,0:T(8,128)(2,1)S(1)} collective-permute-done((bf16[6,224,128]{2,1,0:T(8,128)(2,1)S(1)}, bf16[6,224,128]{2,1,0:T(8,128)(2,1)S(1)}, u32[]{:S(2)}, u32[]{:S(2)}) %collective-permute-start.7) | collective-permute-done | bytes 344096 | tf_op jit(solution)/shard_map/ppermute | solution.py:27
  50.2 1.9 %collective-permute-done.5.refs_2_ = bf16[6,224,128]{2,1,0:T(8,128)(2,1)S(1)} collective-permute-done((bf16[6,224,128]{2,1,0:T(8,128)(2,1)S(1)}, bf16[6,224,128]{2,1,0:T(8,128)(2,1)S(1)}, u32[]{:S(2)}, u32[]{:S(2)}) %collective-permute-start.5) | collective-permute-done | bytes 344096 | tf_op jit(solution)/shard_map/ppermute | solution.py:27
  52.0 5.5 %collective-permute-done.9.refs_10_ = bf16[6,224,128]{2,1,0:T(8,128)(2,1)S(1)} collective-permute-done((bf16[6,224,128]{2,1,0:T(8,128)(2,1)S(1)}, bf16[6,224,128]{2,1,0:T(8,128)(2,1)S(1)}, u32[]{:S(2)}, u32[]{:S(2)}) %collective-permute-start.9) | collective-permute-done | bytes 344096 | tf_op jit(solution)/shard_map/ppermute | solution.py:27
  57.6 0.5 collective-permute-start.15
  58.1 0.5 collective-permute-start.17
  58.6 0.6 collective-permute-done.12.refs_4_
  59.2 0.5 collective-permute-done.15.refs_9_
  59.7 0.5 collective-permute-done.16.refs_12_
  60.2 0.5 collective-permute-done.17.refs_13_
  60.7 2.1 %first_grads.1 = (bf16[2,2,192,128]{3,2,1,0:T(8,128)(2,1)S(1)}, f32[2,192,128]{2,1,0:T(8,128)S(1)}, f32[2,192,128]{2,1,0:T(8,128)S(1)}, bf16[96,224,128]{2,1,0:T(8,128)(2,1)S(1)}) custom-call(s32[12,24]{1,0:T(8,128)S(1)} %bitcast.35, bf16[12,128,224]{2,1,0:T(8,128)(2,1)S(1)} %turn_features.2.xt_ref, bf16[12,128,224]{2,1,0:T(8,128)(2,1)S(1)} %turn_features.3.xt2_ref, ...), custom_call_target="tpu_custom_call" | custom-call | flops 1000 | bytes 1000 | tf_op jit(solution)/shard_map/first_grads/pallas_call | solution.py:318
  62.8 1.5 %collective-permute-start.18 = (bf16[2,2,192,128]{3,2,1,0:T(8,128)(2,1)S(1)}, bf16[2,2,192,128]{3,2,1,0:T(8,128)(2,1)S(1)}, u32[]{:S(2)}, u32[]{:S(2)}) collective-permute-start(bf16[2,2,192,128]{3,2,1,0:T(8,128)(2,1)S(1)} %get-tuple-element.70), channel_id=1, source_target_pairs={{0,4},{4,0},{8,12},{12,8},{16,20},{20,16},{24,28},{28,24},{1,5},{5... | collective-permute-start | bytes 589832 | tf_op jit(solution)/shard_map/ppermute | solution.py:27
  64.4 1.4 %more_grads.3 = (bf16[2,5,192,128]{3,2,1,0:T(8,128)(2,1)S(1)}, f32[5,192,128]{2,1,0:T(8,128)S(1)}, f32[5,192,128]{2,1,0:T(8,128)S(1)}) custom-call(s32[12,24]{1,0:T(8,128)S(1)} %bitcast.36, bf16[12,128,224]{2,1,0:T(8,128)(2,1)S(1)} %turn_features.2.xt_ref, bf16[12,128,224]{2,1,0:T(8,128)(2,1)S(1)} %turn_features.3.xt2_ref, ...), custom_call_target="tpu_custom_call" | custom-call | flops 1000 | bytes 1000 | tf_op jit(solution)/shard_map/more_grads/pallas_call | solution.py:335
  65.8 0.6 collective-permute-start.21
  66.4 4.2 %collective-permute-done.18 = bf16[2,2,192,128]{3,2,1,0:T(8,128)(2,1)S(1)} collective-permute-done((bf16[2,2,192,128]{3,2,1,0:T(8,128)(2,1)S(1)}, bf16[2,2,192,128]{3,2,1,0:T(8,128)(2,1)S(1)}, u32[]{:S(2)}, u32[]{:S(2)}) %collective-permute-start.18) | collective-permute-done | bytes 196640 | tf_op jit(solution)/shard_map/ppermute | solution.py:27
  70.7 2.6 %collective-permute-start.20 = (bf16[2,192,128]{2,1,0:T(8,128)(2,1)S(1)}, bf16[2,192,128]{2,1,0:T(8,128)(2,1)S(1)}, u32[]{:S(2)}, u32[]{:S(2)}) collective-permute-start(bf16[2,192,128]{2,1,0:T(8,128)(2,1)S(1)} %get-tuple-element.94.refs_0_), channel_id=1, source_target_pairs={{0,16},{4,20},{8,24},{12,28},{16,0},{20,4},{24,8},{28,12},{1,17},{... | collective-permute-start | bytes 294920 | tf_op jit(solution)/shard_map/ppermute | solution.py:27
  73.3 2.2 %more_grads.4 = (bf16[12,192,128]{2,1,0:T(8,128)(2,1)S(1)}, bf16[12,192,128]{2,1,0:T(8,128)(2,1)S(1)}, f32[12,192,128]{2,1,0:T(8,128)S(1)}, f32[12,192,128]{2,1,0:T(8,128)S(1)}) custom-call(s32[12,24]{1,0:T(8,128)S(1)} %bitcast.37, bf16[12,128,224]{2,1,0:T(8,128)(2,1)S(1)} %turn_features.2.xt_ref, bf16[12,128,224]{2,1,0:T(8,128)(2,1)S(1)} %turn_features.3.xt2_ref, ...), custom_call_target="tpu_custom_call" | custom-call | flops 1000 | bytes 1000 | tf_op jit(solution)/shard_map/more_grads/pallas_call | solution.py:335
  75.6 1.6 %collective-permute-start.25 = (bf16[12,192,128]{2,1,0:T(8,128)(2,1)S(1)}, bf16[12,192,128]{2,1,0:T(8,128)(2,1)S(1)}, u32[]{:S(2)}, u32[]{:S(2)}) collective-permute-start(bf16[12,192,128]{2,1,0:T(8,128)(2,1)S(1)} %get-tuple-element.87), channel_id=1, source_target_pairs={{0,4},{4,0},{8,12},{12,8},{16,20},{20,16},{24,28},{28,24},{1,5},{5... | collective-permute-start | bytes 1769480 | tf_op jit(solution)/shard_map/ppermute | solution.py:27
  77.1 0.2 collective-permute-start.19
  77.3 1.4 %more_grads.5 = (bf16[2,5,192,128]{3,2,1,0:T(8,128)(2,1)S(1)}, f32[5,192,128]{2,1,0:T(8,128)S(1)}, f32[5,192,128]{2,1,0:T(8,128)S(1)}) custom-call(s32[12,24]{1,0:T(8,128)S(1)} %bitcast.38, bf16[12,128,224]{2,1,0:T(8,128)(2,1)S(1)} %turn_features.2.xt_ref, bf16[12,128,224]{2,1,0:T(8,128)(2,1)S(1)} %turn_features.3.xt2_ref, ...), custom_call_target="tpu_custom_call" | custom-call | flops 1000 | bytes 1000 | tf_op jit(solution)/shard_map/more_grads/pallas_call | solution.py:335
  78.8 0.7 collective-permute-start.24
  79.5 1.7 %collective-permute-done.21 = bf16[2,5,192,128]{3,2,1,0:T(8,128)(2,1)S(1)} collective-permute-done((bf16[2,5,192,128]{3,2,1,0:T(8,128)(2,1)S(1)}, bf16[2,5,192,128]{3,2,1,0:T(8,128)(2,1)S(1)}, u32[]{:S(2)}, u32[]{:S(2)}) %collective-permute-start.21) | collective-permute-done | bytes 491552 | tf_op jit(solution)/shard_map/ppermute | solution.py:27
  81.2 0.1 fusion.3.refs_6_
  81.2 2.6 %collective-permute-start.22 = (bf16[5,192,128]{2,1,0:T(8,128)(2,1)S(1)}, bf16[5,192,128]{2,1,0:T(8,128)(2,1)S(1)}, u32[]{:S(2)}, u32[]{:S(2)}) collective-permute-start(bf16[5,192,128]{2,1,0:T(8,128)(2,1)S(1)} %fusion.3.refs_6_), channel_id=1, source_target_pairs={{0,16},{4,20},{8,24},{12,28},{16,0},{20,4},{24,8},{28,12},{1,17},{... | collective-permute-start | bytes 737288 | tf_op jit(solution)/shard_map/ppermute | solution.py:27
  83.9 0.0 collective-permute-done.19.refs_3_
  83.9 0.1 fusion.2.refs_7_
  84.0 0.3 collective-permute-start.23
  84.3 1.4 %collective-permute-start.26 = (bf16[12,192,128]{2,1,0:T(8,128)(2,1)S(1)}, bf16[12,192,128]{2,1,0:T(8,128)(2,1)S(1)}, u32[]{:S(2)}, u32[]{:S(2)}) collective-permute-start(bf16[12,192,128]{2,1,0:T(8,128)(2,1)S(1)} %get-tuple-element.89), channel_id=1, source_target_pairs={{0,4},{4,0},{8,12},{12,8},{16,20},{20,16},{24,28},{28,24},{1,5},{5... | collective-permute-start | bytes 1769480 | tf_op jit(solution)/shard_map/ppermute | solution.py:27
  85.7 13.7 %collective-permute-done.22.refs_0_ = bf16[5,192,128]{2,1,0:T(8,128)(2,1)S(1)} collective-permute-done((bf16[5,192,128]{2,1,0:T(8,128)(2,1)S(1)}, bf16[5,192,128]{2,1,0:T(8,128)(2,1)S(1)}, u32[]{:S(2)}, u32[]{:S(2)}) %collective-permute-start.22) | collective-permute-done | bytes 245792 | tf_op jit(solution)/shard_map/ppermute | solution.py:27
  99.4 0.1 add_convert_fusion.1.refs_10_
  99.6 0.6 collective-permute-start.27
  100.2 4.2 %collective-permute-done.24 = bf16[2,5,192,128]{3,2,1,0:T(8,128)(2,1)S(1)} collective-permute-done((bf16[2,5,192,128]{3,2,1,0:T(8,128)(2,1)S(1)}, bf16[2,5,192,128]{3,2,1,0:T(8,128)(2,1)S(1)}, u32[]{:S(2)}, u32[]{:S(2)}) %collective-permute-start.24) | collective-permute-done | bytes 491552 | tf_op jit(solution)/shard_map/ppermute | solution.py:27
  104.4 0.1 fusion.1.refs_8_
  104.4 2.6 %collective-permute-start.28 = (bf16[5,192,128]{2,1,0:T(8,128)(2,1)S(1)}, bf16[5,192,128]{2,1,0:T(8,128)(2,1)S(1)}, u32[]{:S(2)}, u32[]{:S(2)}) collective-permute-start(bf16[5,192,128]{2,1,0:T(8,128)(2,1)S(1)} %fusion.1.refs_8_), channel_id=1, source_target_pairs={{0,16},{4,20},{8,24},{12,28},{16,0},{20,4},{24,8},{28,12},{1,17},{... | collective-permute-start | bytes 737288 | tf_op jit(solution)/shard_map/ppermute | solution.py:27
  107.1 0.1 fusion.refs_9_
  107.2 0.4 collective-permute-start.29
  107.5 14.3 %input_grads.1 = bf16[224,3072]{1,0:T(8,128)(2,1)} custom-call(s32[12,24]{1,0:T(8,128)S(1)} %bitcast.39, bf16[12,24,128,128]{3,2,1,0:T(8,128)(2,1)S(1)} %bitcast.33, bf16[12,224,128]{2,1,0:T(8,128)(2,1)S(1)} %get-tuple-element.55.refs_1_.refs_0_, bf16[12,224,128]{2,1,0:T(8,128)(2,1)S(1)} %collective-permute-done.4.refs_1_, ...), custom_call_target="tpu_custom_call" | custom-call | flops 1000 | bytes 1000 | tf_op jit(solution)/shard_map/input_grads/pallas_call | solution.py:364
  121.8 3.1 %collective-permute-done.28 = bf16[5,192,128]{2,1,0:T(8,128)(2,1)S(1)} collective-permute-done((bf16[5,192,128]{2,1,0:T(8,128)(2,1)S(1)}, bf16[5,192,128]{2,1,0:T(8,128)(2,1)S(1)}, u32[]{:S(2)}, u32[]{:S(2)}) %collective-permute-start.28) | collective-permute-done | bytes 245792 | tf_op jit(solution)/shard_map/ppermute | solution.py:27
  124.9 1.0 main_sum.1.base_ref
  125.9 1.6 %last_sum.1 = f32[192,24,128]{2,1,0:T(8,128)} custom-call(f32[192,24,128]{2,1,0:T(8,128)S(1)} %main_sum.1.base_ref, bf16[12,192,128]{2,1,0:T(8,128)(2,1)S(1)} %collective-permute-done.27.near_ref, f32[5,192,128]{2,1,0:T(8,128)S(1)} %convert_element_type.91.mine_ref, bf16[5,192,128]{2,1,0:T(8,128)(2,1)S(1)} %collective-permute-done.29.other_ref), custom_call_target="tpu_custom_call" | custom-call | flops 1000 | bytes 1000 | tf_op jit(solution)/shard_map/last_sum/pallas_call | solution.py:442
  (25 shorter events, 0.1 us)
Async XLA Ops:
  0.6 6.1 %copy-start = (bf16[224,3072]{1,0:T(8,128)(2,1)S(1)}, bf16[224,3072]{1,0:T(8,128)(2,1)}, u32[]{:S(2)}) copy-start(bf16[224,3072]{1,0:T(8,128)(2,1)} %refs_0_) | copy-start | bytes 4128772
  0.6 6.1 %copy-start.2 = (s32[24,12]{0,1:T(8,128)S(1)}, s32[24,12]{0,1:T(8,128)}, u32[]{:S(2)}) copy-start(s32[24,12]{0,1:T(8,128)} %param.6) | copy-start | bytes 3460
  9.5 2.4 %collective-permute-start = (bf16[12,224,128]{2,1,0:T(8,128)(2,1)S(1)}, bf16[12,224,128]{2,1,0:T(8,128)(2,1)S(1)}, u32[]{:S(2)}, u32[]{:S(2)}) collective-permute-start(bf16[12,224,128]{2,1,0:T(8,128)(2,1)S(1)} %get-tuple-element.49), channel_id=1, source_target_pairs={{0,1},{1,0},{2,3},{3,2},{4,5},{5,4},{6,7},{7,6},{8,9},{9,8},{10,11... | collective-permute-start | bytes 2064392 | tf_op jit(solution)/shard_map/ppermute | solution.py:27
  12.1 18.7 %collective-permute-start.3 = (bf16[12,224,128]{2,1,0:T(8,128)(2,1)S(1)}, bf16[12,224,128]{2,1,0:T(8,128)(2,1)S(1)}, u32[]{:S(2)}, u32[]{:S(2)}) collective-permute-start(bf16[12,224,128]{2,1,0:T(8,128)(2,1)S(1)} %add_convert_fusion.refs_0_), channel_id=1, source_target_pairs={{0,2},{1,3},{2,0},{3,1},{4,6},{5,7},{6,4},{7,5},{8,10},{9,11},{10,... | collective-permute-start | bytes 2064392 | tf_op jit(solution)/shard_map/ppermute | solution.py:27
  14.9 15.8 %copy-start.1 = (bf16[224,1536]{1,0:T(8,128)(2,1)S(1)}, bf16[224,1536]{1,0:T(8,128)(2,1)}, u32[]{:S(2)}) copy-start(bf16[224,1536]{1,0:T(8,128)(2,1)} %cot_ref.1) | copy-start | bytes 2064388
  15.0 20.2 %collective-permute-start.6 = (bf16[224,1536]{1,0:T(8,128)(2,1)S(1)}, bf16[224,1536]{1,0:T(8,128)(2,1)S(1)}, u32[]{:S(2)}, u32[]{:S(2)}) collective-permute-start(bf16[224,1536]{1,0:T(8,128)(2,1)S(1)} %partner_features.1), channel_id=1, source_target_pairs={{0,8},{4,12},{8,0},{12,4},{16,24},{20,28},{24,16},{28,20},{1,9},{5... | collective-permute-start | bytes 2064392 | tf_op jit(solution)/shard_map/ppermute | solution.py:27
  19.7 1.7 %collective-permute-start.1 = (bf16[6,224,128]{2,1,0:T(8,128)(2,1)S(1)}, bf16[6,224,128]{2,1,0:T(8,128)(2,1)S(1)}, u32[]{:S(2)}, u32[]{:S(2)}) collective-permute-start(bf16[6,224,128]{2,1,0:T(8,128)(2,1)S(1)} %get-tuple-element.53.refs_1_), channel_id=1, source_target_pairs={{0,1},{1,0},{2,3},{3,2},{4,5},{5,4},{6,7},{7,6},{8,9},{9,8},{10,11... | collective-permute-start | bytes 1032200 | tf_op jit(solution)/shard_map/ppermute | solution.py:27
  19.8 2.1 %collective-permute-start.2 = (bf16[6,224,128]{2,1,0:T(8,128)(2,1)S(1)}, bf16[6,224,128]{2,1,0:T(8,128)(2,1)S(1)}, u32[]{:S(2)}, u32[]{:S(2)}) collective-permute-start(bf16[6,224,128]{2,1,0:T(8,128)(2,1)S(1)} %get-tuple-element.54), channel_id=1, source_target_pairs={{0,1},{1,0},{2,3},{3,2},{4,5},{5,4},{6,7},{7,6},{8,9},{9,8},{10,11... | collective-permute-start | bytes 1032200 | tf_op jit(solution)/shard_map/ppermute | solution.py:27
  31.8 11.0 %collective-permute-start.8 = (bf16[6,224,128]{2,1,0:T(8,128)(2,1)S(1)}, bf16[6,224,128]{2,1,0:T(8,128)(2,1)S(1)}, u32[]{:S(2)}, u32[]{:S(2)}) collective-permute-start(bf16[6,224,128]{2,1,0:T(8,128)(2,1)S(1)} %get-tuple-element.56), channel_id=1, source_target_pairs={{0,8},{4,12},{8,0},{12,4},{16,24},{20,28},{24,16},{28,20},{1,9},{5... | collective-permute-start | bytes 1032200 | tf_op jit(solution)/shard_map/ppermute | solution.py:27
  33.6 11.0 %collective-permute-start.10 = (bf16[6,224,128]{2,1,0:T(8,128)(2,1)S(1)}, bf16[6,224,128]{2,1,0:T(8,128)(2,1)S(1)}, u32[]{:S(2)}, u32[]{:S(2)}) collective-permute-start(bf16[6,224,128]{2,1,0:T(8,128)(2,1)S(1)} %get-tuple-element.58), channel_id=1, source_target_pairs={{0,2},{1,3},{2,0},{3,1},{4,6},{5,7},{6,4},{7,5},{8,10},{9,11},{10,... | collective-permute-start | bytes 1032200 | tf_op jit(solution)/shard_map/ppermute | solution.py:27
  35.2 15.0 %collective-permute-start.7 = (bf16[6,224,128]{2,1,0:T(8,128)(2,1)S(1)}, bf16[6,224,128]{2,1,0:T(8,128)(2,1)S(1)}, u32[]{:S(2)}, u32[]{:S(2)}) collective-permute-start(bf16[6,224,128]{2,1,0:T(8,128)(2,1)S(1)} %get-tuple-element.58), channel_id=1, source_target_pairs={{0,8},{4,12},{8,0},{12,4},{16,24},{20,28},{24,16},{28,20},{1,9},{5... | collective-permute-start | bytes 1032200 | tf_op jit(solution)/shard_map/ppermute | solution.py:27
  35.6 16.4 %collective-permute-start.5 = (bf16[6,224,128]{2,1,0:T(8,128)(2,1)S(1)}, bf16[6,224,128]{2,1,0:T(8,128)(2,1)S(1)}, u32[]{:S(2)}, u32[]{:S(2)}) collective-permute-start(bf16[6,224,128]{2,1,0:T(8,128)(2,1)S(1)} %get-tuple-element.56), channel_id=1, source_target_pairs={{0,2},{1,3},{2,0},{3,1},{4,6},{5,7},{6,4},{7,5},{8,10},{9,11},{10,... | collective-permute-start | bytes 1032200 | tf_op jit(solution)/shard_map/ppermute | solution.py:27
  42.8 14.8 %collective-permute-start.9 = (bf16[6,224,128]{2,1,0:T(8,128)(2,1)S(1)}, bf16[6,224,128]{2,1,0:T(8,128)(2,1)S(1)}, u32[]{:S(2)}, u32[]{:S(2)}) collective-permute-start(bf16[6,224,128]{2,1,0:T(8,128)(2,1)S(1)} %collective-permute-done.8.refs_6_), channel_id=1, source_target_pairs={{0,2},{1,3},{2,0},{3,1},{4,6},{5,7},{6,4},{7,5},{8,10},{9,11},{10,... | collective-permute-start | bytes 1032200 | tf_op jit(solution)/shard_map/ppermute | solution.py:27
  44.6 12.9 %collective-permute-start.11 = (bf16[6,224,128]{2,1,0:T(8,128)(2,1)S(1)}, bf16[6,224,128]{2,1,0:T(8,128)(2,1)S(1)}, u32[]{:S(2)}, u32[]{:S(2)}) collective-permute-start(bf16[6,224,128]{2,1,0:T(8,128)(2,1)S(1)} %collective-permute-done.10.refs_3_), channel_id=1, source_target_pairs={{0,8},{4,12},{8,0},{12,4},{16,24},{20,28},{24,16},{28,20},{1,9},{5... | collective-permute-start | bytes 1032200 | tf_op jit(solution)/shard_map/ppermute | solution.py:27
  46.2 11.9 %collective-permute-start.14 = (bf16[6,224,128]{2,1,0:T(8,128)(2,1)S(1)}, bf16[6,224,128]{2,1,0:T(8,128)(2,1)S(1)}, u32[]{:S(2)}, u32[]{:S(2)}) collective-permute-start(bf16[6,224,128]{2,1,0:T(8,128)(2,1)S(1)} %collective-permute-done.8.refs_6_), channel_id=1, source_target_pairs={{0,1},{1,0},{2,3},{3,2},{4,5},{5,4},{6,7},{7,6},{8,9},{9,8},{10,11... | collective-permute-start | bytes 1032200 | tf_op jit(solution)/shard_map/ppermute | solution.py:27
  50.2 8.4 %collective-permute-start.4 = (bf16[12,224,128]{2,1,0:T(8,128)(2,1)S(1)}, bf16[12,224,128]{2,1,0:T(8,128)(2,1)S(1)}, u32[]{:S(2)}, u32[]{:S(2)}) collective-permute-start(bf16[12,224,128]{2,1,0:T(8,128)(2,1)S(1)} %get-tuple-element.55.refs_1_.refs_0_), channel_id=1, source_target_pairs={{0,1},{1,0},{2,3},{3,2},{4,5},{5,4},{6,7},{7,6},{8,9},{9,8},{10,11... | collective-permute-start | bytes 2064392 | tf_op jit(solution)/shard_map/ppermute | solution.py:27
  52.0 6.1 %collective-permute-start.13 = (bf16[6,224,128]{2,1,0:T(8,128)(2,1)S(1)}, bf16[6,224,128]{2,1,0:T(8,128)(2,1)S(1)}, u32[]{:S(2)}, u32[]{:S(2)}) collective-permute-start(bf16[6,224,128]{2,1,0:T(8,128)(2,1)S(1)} %collective-permute-done.10.refs_3_), channel_id=1, source_target_pairs={{0,1},{1,0},{2,3},{3,2},{4,5},{5,4},{6,7},{7,6},{8,9},{9,8},{10,11... | collective-permute-start | bytes 1032200 | tf_op jit(solution)/shard_map/ppermute | solution.py:27
  57.6 1.7 %collective-permute-start.12 = (bf16[6,224,128]{2,1,0:T(8,128)(2,1)S(1)}, bf16[6,224,128]{2,1,0:T(8,128)(2,1)S(1)}, u32[]{:S(2)}, u32[]{:S(2)}) collective-permute-start(bf16[6,224,128]{2,1,0:T(8,128)(2,1)S(1)} %collective-permute-done.5.refs_2_), channel_id=1, source_target_pairs={{0,1},{1,0},{2,3},{3,2},{4,5},{5,4},{6,7},{7,6},{8,9},{9,8},{10,11... | collective-permute-start | bytes 1032200 | tf_op jit(solution)/shard_map/ppermute | solution.py:27
  57.6 2.1 %collective-permute-start.15 = (bf16[6,224,128]{2,1,0:T(8,128)(2,1)S(1)}, bf16[6,224,128]{2,1,0:T(8,128)(2,1)S(1)}, u32[]{:S(2)}, u32[]{:S(2)}) collective-permute-start(bf16[6,224,128]{2,1,0:T(8,128)(2,1)S(1)} %collective-permute-done.7.refs_7_), channel_id=1, source_target_pairs={{0,1},{1,0},{2,3},{3,2},{4,5},{5,4},{6,7},{7,6},{8,9},{9,8},{10,11... | collective-permute-start | bytes 1032200 | tf_op jit(solution)/shard_map/ppermute | solution.py:27
  58.1 2.1 %collective-permute-start.16 = (bf16[6,224,128]{2,1,0:T(8,128)(2,1)S(1)}, bf16[6,224,128]{2,1,0:T(8,128)(2,1)S(1)}, u32[]{:S(2)}, u32[]{:S(2)}) collective-permute-start(bf16[6,224,128]{2,1,0:T(8,128)(2,1)S(1)} %collective-permute-done.9.refs_10_), channel_id=1, source_target_pairs={{0,1},{1,0},{2,3},{3,2},{4,5},{5,4},{6,7},{7,6},{8,9},{9,8},{10,11... | collective-permute-start | bytes 1032200 | tf_op jit(solution)/shard_map/ppermute | solution.py:27
  58.1 2.6 %collective-permute-start.17 = (bf16[6,224,128]{2,1,0:T(8,128)(2,1)S(1)}, bf16[6,224,128]{2,1,0:T(8,128)(2,1)S(1)}, u32[]{:S(2)}, u32[]{:S(2)}) collective-permute-start(bf16[6,224,128]{2,1,0:T(8,128)(2,1)S(1)} %collective-permute-done.11.refs_11_), channel_id=1, source_target_pairs={{0,1},{1,0},{2,3},{3,2},{4,5},{5,4},{6,7},{7,6},{8,9},{9,8},{10,11... | collective-permute-start | bytes 1032200 | tf_op jit(solution)/shard_map/ppermute | solution.py:27
  62.8 7.8 %collective-permute-start.18 = (bf16[2,2,192,128]{3,2,1,0:T(8,128)(2,1)S(1)}, bf16[2,2,192,128]{3,2,1,0:T(8,128)(2,1)S(1)}, u32[]{:S(2)}, u32[]{:S(2)}) collective-permute-start(bf16[2,2,192,128]{3,2,1,0:T(8,128)(2,1)S(1)} %get-tuple-element.70), channel_id=1, source_target_pairs={{0,4},{4,0},{8,12},{12,8},{16,20},{20,16},{24,28},{28,24},{1,5},{5... | collective-permute-start | bytes 589832 | tf_op jit(solution)/shard_map/ppermute | solution.py:27
  65.8 15.4 %collective-permute-start.21 = (bf16[2,5,192,128]{3,2,1,0:T(8,128)(2,1)S(1)}, bf16[2,5,192,128]{3,2,1,0:T(8,128)(2,1)S(1)}, u32[]{:S(2)}, u32[]{:S(2)}) collective-permute-start(bf16[2,5,192,128]{3,2,1,0:T(8,128)(2,1)S(1)} %get-tuple-element.74), channel_id=1, source_target_pairs={{0,4},{4,0},{8,12},{12,8},{16,20},{20,16},{24,28},{28,24},{1,5},{5... | collective-permute-start | bytes 1474568 | tf_op jit(solution)/shard_map/ppermute | solution.py:27
  70.7 8.8 %collective-permute-start.20 = (bf16[2,192,128]{2,1,0:T(8,128)(2,1)S(1)}, bf16[2,192,128]{2,1,0:T(8,128)(2,1)S(1)}, u32[]{:S(2)}, u32[]{:S(2)}) collective-permute-start(bf16[2,192,128]{2,1,0:T(8,128)(2,1)S(1)} %get-tuple-element.94.refs_0_), channel_id=1, source_target_pairs={{0,16},{4,20},{8,24},{12,28},{16,0},{20,4},{24,8},{28,12},{1,17},{... | collective-permute-start | bytes 294920 | tf_op jit(solution)/shard_map/ppermute | solution.py:27
  75.6 23.9 %collective-permute-start.25 = (bf16[12,192,128]{2,1,0:T(8,128)(2,1)S(1)}, bf16[12,192,128]{2,1,0:T(8,128)(2,1)S(1)}, u32[]{:S(2)}, u32[]{:S(2)}) collective-permute-start(bf16[12,192,128]{2,1,0:T(8,128)(2,1)S(1)} %get-tuple-element.87), channel_id=1, source_target_pairs={{0,4},{4,0},{8,12},{12,8},{16,20},{20,16},{24,28},{28,24},{1,5},{5... | collective-permute-start | bytes 1769480 | tf_op jit(solution)/shard_map/ppermute | solution.py:27
  77.1 6.8 %collective-permute-start.19 = (bf16[2,192,128]{2,1,0:T(8,128)(2,1)S(1)}, bf16[2,192,128]{2,1,0:T(8,128)(2,1)S(1)}, u32[]{:S(2)}, u32[]{:S(2)}) collective-permute-start(bf16[2,192,128]{2,1,0:T(8,128)(2,1)S(1)} %get-tuple-element.95.refs_1_), channel_id=1, source_target_pairs={{0,24},{4,28},{8,16},{12,20},{16,8},{20,12},{24,0},{28,4},{1,25},{... | collective-permute-start | bytes 294920 | tf_op jit(solution)/shard_map/ppermute | solution.py:27
  78.8 25.6 %collective-permute-start.24 = (bf16[2,5,192,128]{3,2,1,0:T(8,128)(2,1)S(1)}, bf16[2,5,192,128]{3,2,1,0:T(8,128)(2,1)S(1)}, u32[]{:S(2)}, u32[]{:S(2)}) collective-permute-start(bf16[2,5,192,128]{3,2,1,0:T(8,128)(2,1)S(1)} %get-tuple-element.83), channel_id=1, source_target_pairs={{0,4},{4,0},{8,12},{12,8},{16,20},{20,16},{24,28},{28,24},{1,5},{5... | collective-permute-start | bytes 1474568 | tf_op jit(solution)/shard_map/ppermute | solution.py:27
  81.2 18.2 %collective-permute-start.22 = (bf16[5,192,128]{2,1,0:T(8,128)(2,1)S(1)}, bf16[5,192,128]{2,1,0:T(8,128)(2,1)S(1)}, u32[]{:S(2)}, u32[]{:S(2)}) collective-permute-start(bf16[5,192,128]{2,1,0:T(8,128)(2,1)S(1)} %fusion.3.refs_6_), channel_id=1, source_target_pairs={{0,16},{4,20},{8,24},{12,28},{16,0},{20,4},{24,8},{28,12},{1,17},{... | collective-permute-start | bytes 737288 | tf_op jit(solution)/shard_map/ppermute | solution.py:27
  84.0 23.1 %collective-permute-start.23 = (bf16[5,192,128]{2,1,0:T(8,128)(2,1)S(1)}, bf16[5,192,128]{2,1,0:T(8,128)(2,1)S(1)}, u32[]{:S(2)}, u32[]{:S(2)}) collective-permute-start(bf16[5,192,128]{2,1,0:T(8,128)(2,1)S(1)} %fusion.2.refs_7_), channel_id=1, source_target_pairs={{0,24},{4,28},{8,16},{12,20},{16,8},{20,12},{24,0},{28,4},{1,25},{... | collective-permute-start | bytes 737288 | tf_op jit(solution)/shard_map/ppermute | solution.py:27
  84.3 40.6 %collective-permute-start.26 = (bf16[12,192,128]{2,1,0:T(8,128)(2,1)S(1)}, bf16[12,192,128]{2,1,0:T(8,128)(2,1)S(1)}, u32[]{:S(2)}, u32[]{:S(2)}) collective-permute-start(bf16[12,192,128]{2,1,0:T(8,128)(2,1)S(1)} %get-tuple-element.89), channel_id=1, source_target_pairs={{0,4},{4,0},{8,12},{12,8},{16,20},{20,16},{24,28},{28,24},{1,5},{5... | collective-permute-start | bytes 1769480 | tf_op jit(solution)/shard_map/ppermute | solution.py:27
  99.6 26.3 %collective-permute-start.27 = (bf16[12,192,128]{2,1,0:T(8,128)(2,1)S(1)}, bf16[12,192,128]{2,1,0:T(8,128)(2,1)S(1)}, u32[]{:S(2)}, u32[]{:S(2)}) collective-permute-start(bf16[12,192,128]{2,1,0:T(8,128)(2,1)S(1)} %add_convert_fusion.1.refs_10_), channel_id=1, source_target_pairs={{0,8},{4,12},{8,0},{12,4},{16,24},{20,28},{24,16},{28,20},{1,9},{5... | collective-permute-start | bytes 1769480 | tf_op jit(solution)/shard_map/ppermute | solution.py:27
  104.4 20.4 %collective-permute-start.28 = (bf16[5,192,128]{2,1,0:T(8,128)(2,1)S(1)}, bf16[5,192,128]{2,1,0:T(8,128)(2,1)S(1)}, u32[]{:S(2)}, u32[]{:S(2)}) collective-permute-start(bf16[5,192,128]{2,1,0:T(8,128)(2,1)S(1)} %fusion.1.refs_8_), channel_id=1, source_target_pairs={{0,16},{4,20},{8,24},{12,28},{16,0},{20,4},{24,8},{28,12},{1,17},{... | collective-permute-start | bytes 737288 | tf_op jit(solution)/shard_map/ppermute | solution.py:27
  107.2 18.8 %collective-permute-start.29 = (bf16[5,192,128]{2,1,0:T(8,128)(2,1)S(1)}, bf16[5,192,128]{2,1,0:T(8,128)(2,1)S(1)}, u32[]{:S(2)}, u32[]{:S(2)}) collective-permute-start(bf16[5,192,128]{2,1,0:T(8,128)(2,1)S(1)} %fusion.refs_9_), channel_id=1, source_target_pairs={{0,24},{4,28},{8,16},{12,20},{16,8},{20,12},{24,0},{28,4},{1,25},{... | collective-permute-start | bytes 737288 | tf_op jit(solution)/shard_map/ppermute | solution.py:27
